TPU v7x, 32 devices: a whole 2x2x4 slice. The times are simulated.
32 devices in a mesh: seg: 8 (over y, x, core), gx: 4 (over z).
Axes of the slice: x: 2, y: 2, z: 4, core: 2. Of those that a mesh axis runs over, the one named last changes fastest.
Arguments:
- adjoint_in: float32 [8, 5, 64, 32, 512], P('seg', None, 'gx'), may hold values from -6 to 6
- sensor: float32 [8, 64, 32, 512], P('seg', 'gx'), may hold values from 0.06 to 0.15
- filter_matrix: float32 [512, 512], replicated
- coupling: float32 [5, 5], replicated
Outputs:
- adjoint_out: float32 [8, 5, 64, 32, 512], P('seg', None, 'gx')
All inputs are finite; a program needn't handle non-finite values.
Results may differ from a plain program's by a relative error of at most 0.00017.
Values sent between devices are 32-bit elements; how exact they have to be, the bound alone decides.
No kernel may reach another device: no remote copies, remote signals or barrier semaphores. Data moves between devices by JAX's collectives and lax.ppermute only.
A program may use at most 64 MiB of HBM per device.

v0:
```python
import functools

import jax
import jax.numpy as jnp
from jax import lax
from jax.experimental import pallas as pl
from jax.experimental.pallas import tpu as pltpu
from jax.sharding import PartitionSpec as P

STEPS = 3
LANES = 128
PAD = 8
ROWS = 16
GROUPS = (1, 1, 1, 2, 2)
VMEM_LIMIT = 56 * 1024 * 1024


class Stage:
    def __init__(self, start, stop, half):
        self.start, self.stop, self.half = start, stop, half
        self.first, self.last = start == -STEPS, stop == half
        self.todo = {}
        for level in range(1, STEPS + 2):
            lag = level - 1
            low = start + lag if self.first else start - lag
            self.todo[level] = (low, stop if self.last else stop - lag)
        self.base = {}
        self.slots = {}
        for level in range(1, STEPS + 1):
            low, high = self.todo[level]
            self.base[level] = low if self.first else low - 2
            self.slots[level] = high - self.base[level]
        self.sensor_low = self.todo[STEPS + 1][0] if not self.first else self.todo[2][0]
        self.sensor_high = self.todo[2][1]


def stage_kernel(stage, fields, planes, groups, *refs):
    refs = list(refs)

    def take(count):
        got = refs[:count]
        del refs[:count]
        return got

    (coupling, weights_in, own_in, sensor_in) = take(4)
    chunks_in = take(len(groups))
    halos_in = take(2 * STEPS) if stage.first else []
    sensor_halo_in = take(2) if stage.first else []
    carries_in = [] if stage.first else take(STEPS)
    if not stage.first:
        take(1)
    (out,) = take(1)
    carries_out = [] if stage.last else take(STEPS)
    (weights, own, sensor, raw) = take(4)
    filtered = dict(zip(range(1, STEPS + 1), take(STEPS)))
    highs = take(2)
    lows = take(2)
    (sems,) = take(1)

    sides = 2 * fields
    nth = raw.shape[-2]
    blocks = raw.shape[-1] // LANES
    used = [0]

    def copy(source, target):
        made = pltpu.make_async_copy(source, target, sems.at[used[0]])
        used[0] += 1
        made.start()
        return made

    waits = {level: [] for level in range(1, STEPS + 2)}
    waits[1].append(copy(weights_in, weights))
    low = stage.todo[1][0]
    if stage.first:
        for h in range(STEPS):
            for s in range(2):
                waits[1].append(copy(halos_in[2 * h + s], raw.at[-1 - h - low, s]))
    depth = max(low, 0)
    for ref, count in zip(chunks_in, groups):
        waits[1].append(copy(ref, raw.at[pl.ds(depth - low, count)]))
        depth += count
    if not stage.first:
        for level in range(1, STEPS + 1):
            waits[level + 1].append(
                copy(carries_in[level - 1], filtered[level].at[pl.ds(0, 2 * sides)])
            )
    for q in range(stage.sensor_high - 1, stage.sensor_low - 1, -1):
        for s in range(2):
            target = sensor.at[q - stage.sensor_low, s]
            if q < 0:
                source = sensor_halo_in[s].at[-1 - q]
            else:
                source = sensor_in.at[0, planes - 1 - q if s else q]
            waits[2].append(copy(source, target))
    out_low, out_high = stage.todo[STEPS + 1]
    for q in range(out_low, out_high):
        for s in range(2):
            plane = planes - 1 - q if s else q
            waits[STEPS + 1].append(copy(own_in.at[0, :, plane], own.at[q - out_low, s]))

    blank = jnp.zeros((PAD, LANES), jnp.float32)
    for level in range(1, STEPS + 1):
        skip = 0 if stage.first else 2 * sides
        ref = filtered[level]

        def clear(i, ref=ref):
            for b in range(blocks):
                ref[i, b, 0:PAD] = blank
                ref[i, b, PAD + nth : 2 * PAD + nth] = blank

        pl.loop(skip, ref.shape[0])(clear)

    lane = lax.broadcasted_iota(jnp.int32, (ROWS, LANES), 1)
    at_start = lane == 0
    at_end = lane == LANES - 1

    def put(value, place, row, b):
        high = value.astype(jnp.bfloat16)
        highs[place][row : row + ROWS, b * LANES : (b + 1) * LANES] = high
        low_part = value - high.astype(jnp.float32)
        lows[place][row : row + ROWS, b * LANES : (b + 1) * LANES] = low_part.astype(jnp.bfloat16)

    def split_raw(q, place):
        slot = q - stage.todo[1][0]
        for s in range(2):
            for f in range(fields):
                for t in range(0, nth, ROWS):
                    for b in range(blocks):
                        value = raw[slot, s, f, t : t + ROWS, b * LANES : (b + 1) * LANES]
                        put(value, place, (s * fields + f) * nth + t, b)

    def advance(level, q, place):
        ref = filtered[level - 1]
        slot = q - stage.base[level - 1]
        inner = not isinstance(q, int) or q < stage.half - 1
        for s in range(2):
            here = slot * sides + s * fields
            before = here - sides
            after = here + sides if inner else slot * sides + (1 - s) * fields
            for t in range(0, nth, ROWS):
                laps = []
                for f in range(fields):
                    middle = [ref[here + f, b, PAD + t : PAD + t + ROWS] for b in range(blocks)]
                    up = [pltpu.roll(v, 1, 1) for v in middle]
                    down = [pltpu.roll(v, LANES - 1, 1) for v in middle]
                    row = []
                    for b in range(blocks):
                        lap = ref[before + f, b, PAD + t : PAD + t + ROWS]
                        lap = lap + ref[after + f, b, PAD + t : PAD + t + ROWS]
                        lap = lap + ref[here + f, b, PAD + t - 1 : PAD + t - 1 + ROWS]
                        lap = lap + ref[here + f, b, PAD + t + 1 : PAD + t + 1 + ROWS]
                        lap = lap + jnp.where(at_start, up[b - 1] if b else 0.0, up[b])
                        lap = lap + jnp.where(
                            at_end, down[b + 1] if b + 1 < blocks else 0.0, down[b]
                        )
                        row.append(lap - 6.0 * middle[b])
                    laps.append(row)
                for b in range(blocks):
                    sens = sensor[q - stage.sensor_low, s, t : t + ROWS, b * LANES : (b + 1) * LANES]
                    for f in range(fields):
                        mixed = coupling[0, f] * laps[0][b]
                        for g in range(1, fields):
                            mixed = mixed + coupling[g, f] * laps[g][b]
                        value = ref[here + f, b, PAD + t : PAD + t + ROWS] + sens * mixed
                        if level == STEPS + 1:
                            at = (q - out_low, s, f, slice(t, t + ROWS), slice(b * LANES, (b + 1) * LANES))
                            own[at] = value - own[at]
                        else:
                            put(value, place, (s * fields + f) * nth + t, b)

    def project(level, q, place):
        ref = filtered[level]
        slot = q - stage.base[level]
        high = highs[place][...]
        left = jnp.concatenate([high, lows[place][...], high], axis=1)
        width = 2 * LANES
        for n in range(0, blocks * LANES, width):
            result = jnp.dot(left, weights[:, n : n + width], preferred_element_type=jnp.float32)
            for i in range(sides):
                for b in range(width // LANES):
                    ref[slot * sides + i, n // LANES + b, PAD : PAD + nth] = result[
                        i * nth : (i + 1) * nth, b * LANES : (b + 1) * LANES
                    ]

    def work(level, q, place):
        if level == 1:
            split_raw(q, place)
        else:
            advance(level, q, place)

    def send_out(q):
        sent = []
        for s in range(2):
            plane = planes - 1 - q if s else q
            sent.append(copy(own.at[q - out_low, s], out.at[0, :, plane]))
        return sent

    def ready(level):
        for made in waits[level]:
            made.wait()

    finish = []
    if stage.last:
        held = None
        for level in range(1, STEPS + 2):
            ready(level)
            for q in range(*stage.todo[level]):
                place = 0 if held is None else 1 - held[2]
                if held is not None:
                    project(*held)
                work(level, q, place)
                held = (level, q, place) if level <= STEPS else None
                if level == STEPS + 1:
                    finish += send_out(q)
    else:
        for level in range(1, STEPS + 2):
            ready(level)

            def step(q, level=level):
                work(level, q, 0)
                if level <= STEPS:
                    project(level, q, 0)

            pl.loop(*stage.todo[level])(step)
            if level <= STEPS:
                ref = filtered[level]
                finish.append(
                    copy(ref.at[pl.ds(ref.shape[0] - 2 * sides, 2 * sides)], carries_out[level - 1])
                )
        for q in range(out_low, out_high):
            finish += send_out(q)
    for made in finish:
        made.wait()


def run_stage(stage, groups, coupling, weights, own, sensor, chunks, halos, sensor_halos, carries, out):
    fields, planes, nth, nr = own.shape[1:]
    sides = 2 * fields
    blocks = nr // LANES
    held = nth + 2 * PAD
    anywhere = pl.BlockSpec(memory_space=pl.ANY)
    operands = [coupling, weights, own, sensor, *chunks]
    if stage.first:
        operands += [*halos, *sensor_halos]
    else:
        operands += [*carries, out]
    in_specs = [pl.BlockSpec(memory_space=pltpu.SMEM)] + [anywhere] * (len(operands) - 1)
    out_shape = [jax.ShapeDtypeStruct(own.shape, jnp.float32)]
    if not stage.last:
        out_shape += [jax.ShapeDtypeStruct((2 * sides, blocks, held, LANES), jnp.float32)] * STEPS
    low, high = stage.todo[1]
    outs = stage.todo[STEPS + 1][1] - stage.todo[STEPS + 1][0]
    depths = stage.sensor_high - stage.sensor_low
    copies = 1 + len(chunks) + 2 * STEPS + 2 + STEPS * 2 + 2 * depths + 4 * outs
    scratch = [
        pltpu.VMEM(weights.shape, jnp.bfloat16),
        pltpu.VMEM((outs, 2, fields, nth, nr), jnp.float32),
        pltpu.VMEM((depths, 2, nth, nr), jnp.float32),
        pltpu.VMEM((high - low, 2, fields, nth, nr), jnp.float32),
        *[
            pltpu.VMEM((stage.slots[level] * sides, blocks, held, LANES), jnp.float32)
            for level in range(1, STEPS + 1)
        ],
        *[pltpu.VMEM((sides * nth, nr), jnp.bfloat16)] * 4,
        pltpu.SemaphoreType.DMA((copies,)),
    ]
    dots = sum(stage.todo[level][1] - stage.todo[level][0] for level in range(1, STEPS + 1))
    flops = dots * 2 * sides * nth * nr * nr * 3
    return pl.pallas_call(
        functools.partial(stage_kernel, stage, fields, planes, groups),
        out_shape=out_shape,
        in_specs=in_specs,
        out_specs=[anywhere] * len(out_shape),
        scratch_shapes=scratch,
        input_output_aliases={} if stage.first else {len(operands) - 1: 0},
        cost_estimate=pl.CostEstimate(
            flops=flops * 2, bytes_accessed=8 * (high - low) * sides * nth * nr, transcendentals=0
        ),
        compiler_params=pltpu.CompilerParams(vmem_limit_bytes=VMEM_LIMIT),
        name=f"stage_{'first' if stage.first else 'last' if stage.last else 'middle'}",
    )(*operands)


def shards(adjoint_in, sensor, filter_matrix, coupling):
    fields, planes, nth, nr = adjoint_in.shape[1:]
    half = planes // 2
    segs = lax.axis_size("seg")
    slabs = lax.axis_size("gx")
    back = [((i + 1) % segs, i) for i in range(segs)]
    up = [(i, i + 1) for i in range(slabs - 1)]
    down = [(i + 1, i) for i in range(slabs - 1)]

    groups = []
    for count in GROUPS:
        if sum(groups) + count < half:
            groups.append(count)
    groups.append(half - sum(groups))

    own = adjoint_in[0]
    chunks = []
    depth = 0
    for count in groups:
        parts = []
        for q in range(depth, depth + count):
            parts += [own[:, q], own[:, planes - 1 - q]]
        packed = jnp.stack(parts).reshape(count, 2, fields, nth, nr)
        chunks.append(lax.ppermute(packed, "seg", back))
        depth += count

    sensor_halos = [
        lax.ppermute(jnp.flip(sensor[0, planes - (STEPS - 1) :], 0), "gx", up),
        lax.ppermute(sensor[0, : STEPS - 1], "gx", down),
    ]
    halos = []
    for h in range(STEPS):
        halos.append(lax.ppermute(chunks[h][0, 1], "gx", up))
        halos.append(lax.ppermute(chunks[h][0, 0], "gx", down))

    high = lax.reduce_precision(filter_matrix, 8, 7)
    low = filter_matrix - high
    weights = jnp.concatenate([high, high, low], axis=0).astype(jnp.bfloat16)

    cuts = [0, len(groups) - 2, len(groups) - 1, len(groups)]
    carries, out = None, None
    depth = 0
    for low_cut, high_cut in zip(cuts[:-1], cuts[1:]):
        mine = groups[low_cut:high_cut]
        stage = Stage(depth if low_cut else -STEPS, depth + sum(mine), half)
        depth += sum(mine)
        out, *carries = run_stage(
            stage, mine, coupling, weights, adjoint_in, sensor,
            chunks[low_cut:high_cut], halos, sensor_halos, carries, out,
        )
    return out


def solution(mesh):
    in_specs = (P("seg", None, "gx", None, None), P("seg", "gx", None, None), P(), P())
    out_specs = P("seg", None, "gx", None, None)
    return jax.shard_map(shards, mesh=mesh, in_specs=in_specs, out_specs=out_specs, check_vma=False)
```

profile of v0, /device:TPU:0, one launch (start us, length us, event | category | flops | bytes accessed | tf_op | source)
XLA Modules:
  0.0 110.9 jit_solution(544761909860025419)
XLA Ops:
  1.0 4.9 %collective-permute-start.12 = (f32[2,32,512]{2,1,0:T(8,128)S(1)}, f32[2,32,512]{2,1,0:T(8,128)S(1)}, u32[]{:S(2)}, u32[]{:S(2)}) collective-permute-start(f32[2,32,512]{2,1,0:T(8,128)S(1)} %rev.4), channel_id=1, source_target_pairs={{0,1},{1,2},{2,3},{4,5},{5,6},{6,7},{8,9},{9,10},{10,11},{12,13},{... | collective-permute-start | bytes 393224 | tf_op jit(solution)/shard_map/ppermute | solution.py:311
  6.0 3.1 %copy.9 = f32[1,5,16,32,512]{4,3,1,2,0:T(8,128)S(1)} copy(f32[1,5,16,32,512]{4,3,2,1,0:T(8,128)} %refs_2_.5) | data formatting | bytes 10485760 | tf_op args[0]
  9.0 1.1 slice_bitcast_fusion.9
  10.1 1.7 %collective-permute-start.2 = (f32[1,2,5,32,512]{4,3,2,1,0:T(8,128)S(1)}, f32[1,2,5,32,512]{4,3,2,1,0:T(8,128)S(1)}, u32[]{:S(2)}, u32[]{:S(2)}) collective-permute-start(f32[1,2,5,32,512]{4,3,2,1,0:T(8,128)S(1)} %maximum_bitcast_fusion.1), channel_id=1, source_target_pairs={{4,0},{8,4},{12,8},{16,12},{20,16},{24,20},{28,24},{0,28},{5,1},{9... | collective-permute-start | bytes 1966088 | tf_op jit(solution)/shard_map/ppermute | solution.py:307
  11.9 1.0 collective-permute-start.3
  14.5 5.5 %collective-permute-done.2.refs_4_ = f32[1,2,5,32,512]{4,3,2,1,0:T(8,128)S(1)} collective-permute-done((f32[1,2,5,32,512]{4,3,2,1,0:T(8,128)S(1)}, f32[1,2,5,32,512]{4,3,2,1,0:T(8,128)S(1)}, u32[]{:S(2)}, u32[]{:S(2)}) %collective-permute-start.2) | collective-permute-done | bytes 655392 | tf_op jit(solution)/shard_map/ppermute | solution.py:307
  20.0 1.3 %collective-permute-start.7 = (f32[5,32,512]{2,1,0:T(8,128)S(1)}, f32[5,32,512]{2,1,0:T(8,128)S(1)}, u32[]{:S(2)}, u32[]{:S(2)}) collective-permute-start(f32[5,32,512]{2,1,0:T(8,128)S(1)} %get-tuple-element.45), channel_id=1, source_target_pairs={{1,0},{2,1},{3,2},{5,4},{6,5},{7,6},{9,8},{10,9},{11,10},{13,12},{... | collective-permute-start | bytes 983048 | tf_op jit(solution)/shard_map/ppermute | solution.py:317
  21.3 5.7 %collective-permute-done.3.refs_5_ = f32[1,2,5,32,512]{4,3,2,1,0:T(8,128)S(1)} collective-permute-done((f32[1,2,5,32,512]{4,3,2,1,0:T(8,128)S(1)}, f32[1,2,5,32,512]{4,3,2,1,0:T(8,128)S(1)}, u32[]{:S(2)}, u32[]{:S(2)}) %collective-permute-start.3) | collective-permute-done | bytes 655392 | tf_op jit(solution)/shard_map/ppermute | solution.py:307
  26.9 3.5 %collective-permute-start.6 = (f32[5,32,512]{2,1,0:T(8,128)S(1)}, f32[5,32,512]{2,1,0:T(8,128)S(1)}, u32[]{:S(2)}, u32[]{:S(2)}) collective-permute-start(f32[5,32,512]{2,1,0:T(8,128)S(1)} %get-tuple-element.46), channel_id=1, source_target_pairs={{0,1},{1,2},{2,3},{4,5},{5,6},{6,7},{8,9},{9,10},{10,11},{12,13},{... | collective-permute-start | bytes 983048 | tf_op jit(solution)/shard_map/ppermute | solution.py:316
  30.5 3.5 %collective-permute-done.4.refs_6_ = f32[1,2,5,32,512]{4,3,2,1,0:T(8,128)S(1)} collective-permute-done((f32[1,2,5,32,512]{4,3,2,1,0:T(8,128)S(1)}, f32[1,2,5,32,512]{4,3,2,1,0:T(8,128)S(1)}, u32[]{:S(2)}, u32[]{:S(2)}) %collective-permute-start.4) | collective-permute-done | bytes 655392 | tf_op jit(solution)/shard_map/ppermute | solution.py:307
  34.0 1.3 %collective-permute-start.13 = (f32[2,32,512]{2,1,0:T(8,128)S(1)}, f32[2,32,512]{2,1,0:T(8,128)S(1)}, u32[]{:S(2)}, u32[]{:S(2)}) collective-permute-start(f32[2,32,512]{2,1,0:T(8,128)S(1)} %get-tuple-element.37), channel_id=1, source_target_pairs={{1,0},{2,1},{3,2},{5,4},{6,5},{7,6},{9,8},{10,9},{11,10},{13,12},{... | collective-permute-start | bytes 393224 | tf_op jit(solution)/shard_map/ppermute | solution.py:312
  35.3 1.3 %collective-permute-start.9 = (f32[5,32,512]{2,1,0:T(8,128)S(1)}, f32[5,32,512]{2,1,0:T(8,128)S(1)}, u32[]{:S(2)}, u32[]{:S(2)}) collective-permute-start(f32[5,32,512]{2,1,0:T(8,128)S(1)} %get-tuple-element.43), channel_id=1, source_target_pairs={{1,0},{2,1},{3,2},{5,4},{6,5},{7,6},{9,8},{10,9},{11,10},{13,12},{... | collective-permute-start | bytes 983048 | tf_op jit(solution)/shard_map/ppermute | solution.py:317
  36.6 5.5 %collective-permute-done.13.refs_15_ = f32[2,32,512]{2,1,0:T(8,128)S(1)} collective-permute-done((f32[2,32,512]{2,1,0:T(8,128)S(1)}, f32[2,32,512]{2,1,0:T(8,128)S(1)}, u32[]{:S(2)}, u32[]{:S(2)}) %collective-permute-start.13) | collective-permute-done | bytes 131104 | tf_op jit(solution)/shard_map/ppermute | solution.py:312
  42.2 3.5 %collective-permute-start.8 = (f32[5,32,512]{2,1,0:T(8,128)S(1)}, f32[5,32,512]{2,1,0:T(8,128)S(1)}, u32[]{:S(2)}, u32[]{:S(2)}) collective-permute-start(f32[5,32,512]{2,1,0:T(8,128)S(1)} %get-tuple-element.44), channel_id=1, source_target_pairs={{0,1},{1,2},{2,3},{4,5},{5,6},{6,7},{8,9},{9,10},{10,11},{12,13},{... | collective-permute-start | bytes 983048 | tf_op jit(solution)/shard_map/ppermute | solution.py:316
  45.7 1.3 %collective-permute-start.11 = (f32[5,32,512]{2,1,0:T(8,128)S(1)}, f32[5,32,512]{2,1,0:T(8,128)S(1)}, u32[]{:S(2)}, u32[]{:S(2)}) collective-permute-start(f32[5,32,512]{2,1,0:T(8,128)S(1)} %get-tuple-element.41), channel_id=1, source_target_pairs={{1,0},{2,1},{3,2},{5,4},{6,5},{7,6},{9,8},{10,9},{11,10},{13,12},{... | collective-permute-start | bytes 983048 | tf_op jit(solution)/shard_map/ppermute | solution.py:317
  47.0 4.6 %collective-permute-start.10 = (f32[5,32,512]{2,1,0:T(8,128)S(1)}, f32[5,32,512]{2,1,0:T(8,128)S(1)}, u32[]{:S(2)}, u32[]{:S(2)}) collective-permute-start(f32[5,32,512]{2,1,0:T(8,128)S(1)} %get-tuple-element.42), channel_id=1, source_target_pairs={{0,1},{1,2},{2,3},{4,5},{5,6},{6,7},{8,9},{9,10},{10,11},{12,13},{... | collective-permute-start | bytes 983048 | tf_op jit(solution)/shard_map/ppermute | solution.py:316
  51.6 1.4 %pad_maximum_fusion.refs_1_ = bf16[1536,512]{1,0:T(8,128)(2,1)} fusion(bf16[512,512]{1,0:T(8,128)(2,1)S(1)} %get-tuple-element.40, bf16[512,512]{1,0:T(8,128)(2,1)S(1)} %get-tuple-element.39), kind=kLoop, calls=%fused_computation.1 | loop fusion | flops 4718592 | bytes 2621440 | tf_op jit(solution)/shard_map/concatenate | solution.py:321
  53.8 2.3 %collective-permute-done.11.refs_13_ = f32[5,32,512]{2,1,0:T(8,128)S(1)} collective-permute-done((f32[5,32,512]{2,1,0:T(8,128)S(1)}, f32[5,32,512]{2,1,0:T(8,128)S(1)}, u32[]{:S(2)}, u32[]{:S(2)}) %collective-permute-start.11) | collective-permute-done | bytes 327712 | tf_op jit(solution)/shard_map/ppermute | solution.py:317
  56.1 2.9 %collective-permute-done.10.refs_12_ = f32[5,32,512]{2,1,0:T(8,128)S(1)} collective-permute-done((f32[5,32,512]{2,1,0:T(8,128)S(1)}, f32[5,32,512]{2,1,0:T(8,128)S(1)}, u32[]{:S(2)}, u32[]{:S(2)}) %collective-permute-start.10) | collective-permute-done | bytes 327712 | tf_op jit(solution)/shard_map/ppermute | solution.py:316
  59.7 1.1 copy-done.5
  60.8 23.8 %stage_first.1 = (f32[1,5,16,32,512]{4,3,2,1,0:T(8,128)}, f32[20,4,48,128]{3,2,1,0:T(8,128)}, f32[20,4,48,128]{3,2,1,0:T(8,128)}, f32[20,4,48,128]{3,2,1,0:T(8,128)}) custom-call(f32[5,5]{1,0:T(8,128)} %refs_0_.5, bf16[1536,512]{1,0:T(8,128)(2,1)} %pad_maximum_fusion.refs_1_, f32[1,5,16,32,512]{4,3,2,1,0:T(8,128)} %refs_2_.5, f32[1,16,32,512]{3,2,1,0:T(8,128)} %refs_3_.5, ...), custom_call_target="tpu_custom_call" | custom-call | flops 18119393280 | bytes 10485760 | tf_op jit(solution)/shard_map/stage_first/pallas_call | solution.py:269
  84.6 1.1 copy-done.6
  85.7 11.6 %stage_middle.1 = (f32[1,5,16,32,512]{4,3,2,1,0:T(8,128)}, f32[20,4,48,128]{3,2,1,0:T(8,128)}, f32[20,4,48,128]{3,2,1,0:T(8,128)}, f32[20,4,48,128]{3,2,1,0:T(8,128)}) custom-call(f32[5,5]{1,0:T(8,128)} %refs_0_.5, bf16[1536,512]{1,0:T(8,128)(2,1)} %pad_maximum_fusion.refs_1_, f32[1,5,16,32,512]{4,3,2,1,0:T(8,128)} %refs_2_.5, ...), custom_call_target="tpu_custom_call", output_to_operand_aliasing={{0}: (8, {})} | custom-call | flops 6039797760 | bytes 2621440 | tf_op jit(solution)/shard_map/stage_middle/pallas_call | solution.py:269
  98.1 12.6 %stage_last.1 = f32[1,5,16,32,512]{4,3,2,1,0:T(8,128)} custom-call(f32[5,5]{1,0:T(8,128)} %refs_0_.5, bf16[1536,512]{1,0:T(8,128)(2,1)} %pad_maximum_fusion.refs_1_, f32[1,5,16,32,512]{4,3,2,1,0:T(8,128)} %refs_2_.5, f32[1,16,32,512]{3,2,1,0:T(8,128)} %refs_3_.5, f32[1,2,5,32,512]{4,3,2,1,0:T(8,128)} %copy-done.1, ...), custom_call_target="tpu_custom_call", output_to_operand_aliasing={{}: (8, {})} | custom-call | flops 6039797760 | bytes 1310720 | tf_op jit(solution)/shard_map/stage_last/pallas_call | solution.py:269
  (52 shorter events, 5.3 us)
Async XLA Ops:
  1.0 34.3 %collective-permute-start.12 = (f32[2,32,512]{2,1,0:T(8,128)S(1)}, f32[2,32,512]{2,1,0:T(8,128)S(1)}, u32[]{:S(2)}, u32[]{:S(2)}) collective-permute-start(f32[2,32,512]{2,1,0:T(8,128)S(1)} %rev.4), channel_id=1, source_target_pairs={{0,1},{1,2},{2,3},{4,5},{5,6},{6,7},{8,9},{9,10},{10,11},{12,13},{... | collective-permute-start | bytes 393224 | tf_op jit(solution)/shard_map/ppermute | solution.py:311
  10.1 9.8 %collective-permute-start.2 = (f32[1,2,5,32,512]{4,3,2,1,0:T(8,128)S(1)}, f32[1,2,5,32,512]{4,3,2,1,0:T(8,128)S(1)}, u32[]{:S(2)}, u32[]{:S(2)}) collective-permute-start(f32[1,2,5,32,512]{4,3,2,1,0:T(8,128)S(1)} %maximum_bitcast_fusion.1), channel_id=1, source_target_pairs={{4,0},{8,4},{12,8},{16,12},{20,16},{24,20},{28,24},{0,28},{5,1},{9... | collective-permute-start | bytes 1966088 | tf_op jit(solution)/shard_map/ppermute | solution.py:307
  11.9 15.1 %collective-permute-start.3 = (f32[1,2,5,32,512]{4,3,2,1,0:T(8,128)S(1)}, f32[1,2,5,32,512]{4,3,2,1,0:T(8,128)S(1)}, u32[]{:S(2)}, u32[]{:S(2)}) collective-permute-start(f32[1,2,5,32,512]{4,3,2,1,0:T(8,128)S(1)} %maximum_bitcast_fusion.2), channel_id=1, source_target_pairs={{4,0},{8,4},{12,8},{16,12},{20,16},{24,20},{28,24},{0,28},{5,1},{9... | collective-permute-start | bytes 1966088 | tf_op jit(solution)/shard_map/ppermute | solution.py:307
  12.9 21.0 %collective-permute-start.4 = (f32[1,2,5,32,512]{4,3,2,1,0:T(8,128)S(1)}, f32[1,2,5,32,512]{4,3,2,1,0:T(8,128)S(1)}, u32[]{:S(2)}, u32[]{:S(2)}) collective-permute-start(f32[1,2,5,32,512]{4,3,2,1,0:T(8,128)S(1)} %maximum_bitcast_fusion.3), channel_id=1, source_target_pairs={{4,0},{8,4},{12,8},{16,12},{20,16},{24,20},{28,24},{0,28},{5,1},{9... | collective-permute-start | bytes 1966088 | tf_op jit(solution)/shard_map/ppermute | solution.py:307
  13.2 45.8 %collective-permute-start.5 = (f32[2,2,5,32,512]{4,3,2,1,0:T(8,128)S(1)}, f32[2,2,5,32,512]{4,3,2,1,0:T(8,128)S(1)}, u32[]{:S(2)}, u32[]{:S(2)}) collective-permute-start(f32[2,2,5,32,512]{4,3,2,1,0:T(8,128)S(1)} %bitcast.63), channel_id=1, source_target_pairs={{4,0},{8,4},{12,8},{16,12},{20,16},{24,20},{28,24},{0,28},{5,1},{9... | collective-permute-start | bytes 3932168 | tf_op jit(solution)/shard_map/ppermute | solution.py:307
  19.9 15.4 %copy-start.2 = (f32[1,2,5,32,512]{4,3,2,1,0:T(8,128)}, f32[1,2,5,32,512]{4,3,2,1,0:T(8,128)S(1)}, u32[]{:S(2)}) copy-start(f32[1,2,5,32,512]{4,3,2,1,0:T(8,128)S(1)} %collective-permute-done.2.refs_4_) | copy-start | bytes 1966084
  20.0 25.7 %collective-permute-start.7 = (f32[5,32,512]{2,1,0:T(8,128)S(1)}, f32[5,32,512]{2,1,0:T(8,128)S(1)}, u32[]{:S(2)}, u32[]{:S(2)}) collective-permute-start(f32[5,32,512]{2,1,0:T(8,128)S(1)} %get-tuple-element.45), channel_id=1, source_target_pairs={{1,0},{2,1},{3,2},{5,4},{6,5},{7,6},{9,8},{10,9},{11,10},{13,12},{... | collective-permute-start | bytes 983048 | tf_op jit(solution)/shard_map/ppermute | solution.py:317
  26.9 24.7 %copy-start.3 = (f32[1,2,5,32,512]{4,3,2,1,0:T(8,128)}, f32[1,2,5,32,512]{4,3,2,1,0:T(8,128)S(1)}, u32[]{:S(2)}) copy-start(f32[1,2,5,32,512]{4,3,2,1,0:T(8,128)S(1)} %collective-permute-done.3.refs_5_) | copy-start | bytes 1966084
  26.9 20.0 %collective-permute-start.6 = (f32[5,32,512]{2,1,0:T(8,128)S(1)}, f32[5,32,512]{2,1,0:T(8,128)S(1)}, u32[]{:S(2)}, u32[]{:S(2)}) collective-permute-start(f32[5,32,512]{2,1,0:T(8,128)S(1)} %get-tuple-element.46), channel_id=1, source_target_pairs={{0,1},{1,2},{2,3},{4,5},{5,6},{6,7},{8,9},{9,10},{10,11},{12,13},{... | collective-permute-start | bytes 983048 | tf_op jit(solution)/shard_map/ppermute | solution.py:316
  34.0 19.0 %copy-start.4 = (f32[1,2,5,32,512]{4,3,2,1,0:T(8,128)}, f32[1,2,5,32,512]{4,3,2,1,0:T(8,128)S(1)}, u32[]{:S(2)}) copy-start(f32[1,2,5,32,512]{4,3,2,1,0:T(8,128)S(1)} %collective-permute-done.4.refs_6_) | copy-start | bytes 1966084
  34.0 8.2 %collective-permute-start.13 = (f32[2,32,512]{2,1,0:T(8,128)S(1)}, f32[2,32,512]{2,1,0:T(8,128)S(1)}, u32[]{:S(2)}, u32[]{:S(2)}) collective-permute-start(f32[2,32,512]{2,1,0:T(8,128)S(1)} %get-tuple-element.37), channel_id=1, source_target_pairs={{1,0},{2,1},{3,2},{5,4},{6,5},{7,6},{9,8},{10,9},{11,10},{13,12},{... | collective-permute-start | bytes 393224 | tf_op jit(solution)/shard_map/ppermute | solution.py:312
  35.3 17.7 %copy-start.13 = (f32[2,32,512]{2,1,0:T(8,128)}, f32[2,32,512]{2,1,0:T(8,128)S(1)}, u32[]{:S(2)}) copy-start(f32[2,32,512]{2,1,0:T(8,128)S(1)} %collective-permute-done.12.refs_14_) | copy-start | bytes 393220
  35.3 17.7 %collective-permute-start.9 = (f32[5,32,512]{2,1,0:T(8,128)S(1)}, f32[5,32,512]{2,1,0:T(8,128)S(1)}, u32[]{:S(2)}, u32[]{:S(2)}) collective-permute-start(f32[5,32,512]{2,1,0:T(8,128)S(1)} %get-tuple-element.43), channel_id=1, source_target_pairs={{1,0},{2,1},{3,2},{5,4},{6,5},{7,6},{9,8},{10,9},{11,10},{13,12},{... | collective-permute-start | bytes 983048 | tf_op jit(solution)/shard_map/ppermute | solution.py:317
  42.2 10.8 %copy-start.14 = (f32[2,32,512]{2,1,0:T(8,128)}, f32[2,32,512]{2,1,0:T(8,128)S(1)}, u32[]{:S(2)}) copy-start(f32[2,32,512]{2,1,0:T(8,128)S(1)} %collective-permute-done.13.refs_15_) | copy-start | bytes 393220
  42.2 11.4 %collective-permute-start.8 = (f32[5,32,512]{2,1,0:T(8,128)S(1)}, f32[5,32,512]{2,1,0:T(8,128)S(1)}, u32[]{:S(2)}, u32[]{:S(2)}) collective-permute-start(f32[5,32,512]{2,1,0:T(8,128)S(1)} %get-tuple-element.44), channel_id=1, source_target_pairs={{0,1},{1,2},{2,3},{4,5},{5,6},{6,7},{8,9},{9,10},{10,11},{12,13},{... | collective-permute-start | bytes 983048 | tf_op jit(solution)/shard_map/ppermute | solution.py:316
  45.6 7.3 %copy-start.7 = (f32[5,32,512]{2,1,0:T(8,128)}, f32[5,32,512]{2,1,0:T(8,128)S(1)}, u32[]{:S(2)}) copy-start(f32[5,32,512]{2,1,0:T(8,128)S(1)} %collective-permute-done.7.refs_9_) | copy-start | bytes 983044
  45.7 10.5 %collective-permute-start.11 = (f32[5,32,512]{2,1,0:T(8,128)S(1)}, f32[5,32,512]{2,1,0:T(8,128)S(1)}, u32[]{:S(2)}, u32[]{:S(2)}) collective-permute-start(f32[5,32,512]{2,1,0:T(8,128)S(1)} %get-tuple-element.41), channel_id=1, source_target_pairs={{1,0},{2,1},{3,2},{5,4},{6,5},{7,6},{9,8},{10,9},{11,10},{13,12},{... | collective-permute-start | bytes 983048 | tf_op jit(solution)/shard_map/ppermute | solution.py:317
  47.0 6.0 %copy-start.8 = (f32[5,32,512]{2,1,0:T(8,128)}, f32[5,32,512]{2,1,0:T(8,128)S(1)}, u32[]{:S(2)}) copy-start(f32[5,32,512]{2,1,0:T(8,128)S(1)} %collective-permute-done.6.refs_8_) | copy-start | bytes 983044
  47.0 12.0 %collective-permute-start.10 = (f32[5,32,512]{2,1,0:T(8,128)S(1)}, f32[5,32,512]{2,1,0:T(8,128)S(1)}, u32[]{:S(2)}, u32[]{:S(2)}) collective-permute-start(f32[5,32,512]{2,1,0:T(8,128)S(1)} %get-tuple-element.42), channel_id=1, source_target_pairs={{0,1},{1,2},{2,3},{4,5},{5,6},{6,7},{8,9},{9,10},{10,11},{12,13},{... | collective-permute-start | bytes 983048 | tf_op jit(solution)/shard_map/ppermute | solution.py:316
  53.0 6.0 %copy-start.9 = (f32[5,32,512]{2,1,0:T(8,128)}, f32[5,32,512]{2,1,0:T(8,128)S(1)}, u32[]{:S(2)}) copy-start(f32[5,32,512]{2,1,0:T(8,128)S(1)} %collective-permute-done.9.refs_11_) | copy-start | bytes 983044
  53.0 44.3 %collective-permute-start = (f32[1,2,5,32,512]{4,3,2,1,0:T(8,128)S(1)}, f32[1,2,5,32,512]{4,3,2,1,0:T(8,128)S(1)}, u32[]{:S(2)}, u32[]{:S(2)}) collective-permute-start(f32[1,2,5,32,512]{4,3,2,1,0:T(8,128)S(1)} %maximum_bitcast_fusion), channel_id=1, source_target_pairs={{4,0},{8,4},{12,8},{16,12},{20,16},{24,20},{28,24},{0,28},{5,1},{9... | collective-permute-start | bytes 1966088 | tf_op jit(solution)/shard_map/ppermute | solution.py:307
  53.6 5.4 %copy-start.10 = (f32[5,32,512]{2,1,0:T(8,128)}, f32[5,32,512]{2,1,0:T(8,128)S(1)}, u32[]{:S(2)}) copy-start(f32[5,32,512]{2,1,0:T(8,128)S(1)} %collective-permute-done.8.refs_10_) | copy-start | bytes 983044
  53.6 31.0 %collective-permute-start.1 = (f32[2,2,5,32,512]{4,3,2,1,0:T(8,128)S(1)}, f32[2,2,5,32,512]{4,3,2,1,0:T(8,128)S(1)}, u32[]{:S(2)}, u32[]{:S(2)}) collective-permute-start(f32[2,2,5,32,512]{4,3,2,1,0:T(8,128)S(1)} %bitcast.62), channel_id=1, source_target_pairs={{4,0},{8,4},{12,8},{16,12},{20,16},{24,20},{28,24},{0,28},{5,1},{9... | collective-permute-start | bytes 3932168 | tf_op jit(solution)/shard_map/ppermute | solution.py:307
  56.1 2.9 %copy-start.11 = (f32[5,32,512]{2,1,0:T(8,128)}, f32[5,32,512]{2,1,0:T(8,128)S(1)}, u32[]{:S(2)}) copy-start(f32[5,32,512]{2,1,0:T(8,128)S(1)} %collective-permute-done.11.refs_13_) | copy-start | bytes 983044
  (5 other events, 4.9 us)
where the time goes:
time: 111 us
  Pallas kernels  48 us (43%)
  waiting for transfers between devices  25.7 us (23%)
  starting transfers between devices  25.5 us (23%)
  local copies, waits for them, and re-layouts  9.3 us (8%)
  other arithmetic  1.98 us (2%)
    pallas_call x3, Pallas kernels, run_stage(): pl.pallas_call(functools.partial(stage_kernel, stage, fields, planes, gro...  48 us
    ppermute x6, waiting for transfers between devices, shards(): chunks.append(lax.ppermute(packed, 'seg', back))  14.6 us
    ppermute x3, starting transfers between devices, shards(): halos.append(lax.ppermute(chunks[h][0, 1], 'gx', up))  11.5 us
    unnamed x31, local copies, waits for them, and re-layouts  7.1 us
    ppermute x1, waiting for transfers between devices, shards(): lax.ppermute(sensor[0, :STEPS - 1], 'gx', down)  5.53 us
    ppermute x1, starting transfers between devices, shards(): lax.ppermute(jnp.flip(sensor[0, planes - (STEPS - 1):], 0), 'gx', up)  4.94 us
    ppermute x3, starting transfers between devices, shards(): halos.append(lax.ppermute(chunks[h][0, 0], 'gx', down))  3.88 us
    ppermute x6, starting transfers between devices, shards(): chunks.append(lax.ppermute(packed, 'seg', back))  3.86 us
  transfers between devices with their start and end apart: 14, of which 7 were waited for; matrix products, arithmetic and copies ran while one was open for 6% of the time, Pallas kernels for 32%

commit v1 on v0

v1 whole, which is shorter than its diff:
```python
import functools
import math

import jax
import jax.numpy as jnp
from jax import lax
from jax.experimental import pallas as pl
from jax.experimental.pallas import tpu as pltpu
from jax.sharding import PartitionSpec as P

STEPS = 3
LANES = 128
PAD = 8
ROWS = 16
GROUPS = (1, 1, 1, 2, 2)
VMEM_SPARE = 6 * 1024 * 1024
VMEM_MOST = 60 * 1024 * 1024


class Stage:
    def __init__(self, start, stop, half):
        self.start, self.stop, self.half = start, stop, half
        self.first, self.last = start == -STEPS, stop == half
        self.todo = {}
        for level in range(1, STEPS + 2):
            lag = level - 1
            low = start + lag if self.first else start - lag
            self.todo[level] = (low, stop if self.last else stop - lag)
        self.base = {}
        self.slots = {}
        for level in range(1, STEPS + 1):
            low, high = self.todo[level]
            self.base[level] = low if self.first else low - 2
            self.slots[level] = high - self.base[level]
        self.sensor_low = self.todo[STEPS + 1][0] if not self.first else self.todo[2][0]
        self.sensor_high = self.todo[2][1]


def pack_kernel(plan, *refs):
    sems = refs[-1]
    made = []
    for i, (operand, source, result, target) in enumerate(plan):
        made.append(pltpu.make_async_copy(refs[operand].at[source], refs[result].at[target], sems.at[i]))
        made[-1].start()
    for one in made:
        one.wait()


def stage_kernel(stage, fields, planes, groups, *refs):
    refs = list(refs)

    def take(count):
        got = refs[:count]
        del refs[:count]
        return got

    (coupling, odd_ref, weights_in, own_in, sensor_in) = take(5)
    chunks_in = take(len(groups))
    halos_in = take(2 * STEPS) if stage.first else []
    sensor_halo_in = take(2) if stage.first else []
    carries_in = [] if stage.first else take(STEPS)
    if not stage.first:
        take(1)
    (out,) = take(1)
    carries_out = [] if stage.last else take(STEPS)
    (weights, own, sensor, raw) = take(4)
    filtered = dict(zip(range(1, STEPS + 1), take(STEPS)))
    highs = take(2)
    lows = take(2)
    (sems,) = take(1)

    sides = 2 * fields
    nth = raw.shape[-2]
    blocks = raw.shape[-1] // LANES
    used = [0]

    def copy(source, target):
        made = pltpu.make_async_copy(source, target, sems.at[used[0]])
        used[0] += 1
        made.start()
        return made

    waits = {level: [] for level in range(1, STEPS + 2)}
    low = stage.todo[1][0]
    depth = max(low, 0)
    for ref, count in zip(chunks_in, groups):
        waits[1].append(copy(ref, raw.at[pl.ds(depth - low, count)]))
        depth += count
    waits[1].append(copy(weights_in, weights))
    odd = odd_ref[0]
    if stage.first:
        for h in range(STEPS):
            waits[1].append(copy(halos_in[2 * h].at[0], raw.at[-1 - h - low, 1 - odd]))
            waits[1].append(copy(halos_in[2 * h + 1].at[0], raw.at[-1 - h - low, odd]))
    if not stage.first:
        for level in range(1, STEPS + 1):
            waits[level + 1].append(
                copy(carries_in[level - 1], filtered[level].at[pl.ds(0, 2 * sides)])
            )
    for q in range(stage.sensor_high - 1, stage.sensor_low - 1, -1):
        for s in range(2):
            if q < 0:
                side = 1 - odd if s == 0 else odd
                source, target = sensor_halo_in[s].at[-1 - q], sensor.at[q - stage.sensor_low, side]
            else:
                source, target = sensor_in.at[0, planes - 1 - q if s else q], sensor.at[q - stage.sensor_low, s]
            waits[2].append(copy(source, target))
    out_low, out_high = stage.todo[STEPS + 1]
    for q in range(out_low, out_high):
        for s in range(2):
            plane = planes - 1 - q if s else q
            waits[STEPS + 1].append(copy(own_in.at[0, :, plane], own.at[q - out_low, s]))

    blank = jnp.zeros((PAD, LANES), jnp.float32)
    for level in range(1, STEPS + 1):
        skip = 0 if stage.first else 2 * sides
        ref = filtered[level]

        def clear(i, ref=ref):
            for b in range(blocks):
                ref[i, b, 0:PAD] = blank
                ref[i, b, PAD + nth : 2 * PAD + nth] = blank

        pl.loop(skip, ref.shape[0])(clear)

    lane = lax.broadcasted_iota(jnp.int32, (ROWS, LANES), 1)
    at_start = lane == 0
    at_end = lane == LANES - 1
    weight = [[coupling[g, f] for f in range(fields)] for g in range(fields)]

    def put(value, place, row, b):
        at = (pl.ds(pl.multiple_of(row, ROWS), ROWS), slice(b * LANES, (b + 1) * LANES))
        high = value.astype(jnp.bfloat16)
        highs[place][at] = high
        lows[place][at] = (value - high.astype(jnp.float32)).astype(jnp.bfloat16)

    def split_raw(q, place, t):
        slot = q - stage.todo[1][0]
        for s in range(2):
            for f in range(fields):
                for b in range(blocks):
                    value = raw[slot, s, f, pl.ds(t, ROWS), b * LANES : (b + 1) * LANES]
                    put(value, place, (s * fields + f) * nth + t, b)

    def advance(level, q, place, t):
        ref = filtered[level - 1]
        slot = q - stage.base[level - 1]
        row = pl.multiple_of(PAD + t, PAD)
        for s in range(2):
            here = slot * sides + s * fields
            before = here - sides
            after = here + sides if q < stage.half - 1 else slot * sides + (1 - s) * fields
            for b in range(blocks):
                middles, laps = [], []
                for f in range(fields):
                    middle = ref[here + f, b, pl.ds(row, ROWS)]
                    lower = ref[here + f, b - 1, pl.ds(row, ROWS)] if b else 0.0
                    upper = ref[here + f, b + 1, pl.ds(row, ROWS)] if b + 1 < blocks else 0.0
                    left = pltpu.roll(jnp.where(at_end, lower, middle), 1, 1)
                    right = pltpu.roll(jnp.where(at_start, upper, middle), LANES - 1, 1)
                    axial = ref[before + f, b, pl.ds(row, ROWS)] + ref[after + f, b, pl.ds(row, ROWS)]
                    around = ref[here + f, b, pl.ds(PAD + t - 1, ROWS)] + ref[here + f, b, pl.ds(PAD + t + 1, ROWS)]
                    middles.append(middle)
                    laps.append((axial + around) + (left + right) - 6.0 * middle)
                sens = sensor[q - stage.sensor_low, s, pl.ds(t, ROWS), b * LANES : (b + 1) * LANES]
                for f in range(fields):
                    mixed = weight[0][f] * laps[0]
                    for g in range(1, fields):
                        mixed = mixed + weight[g][f] * laps[g]
                    value = middles[f] + sens * mixed
                    if level == STEPS + 1:
                        at = (q - out_low, s, f, pl.ds(t, ROWS), slice(b * LANES, (b + 1) * LANES))
                        own[at] = value - own[at]
                    else:
                        put(value, place, (s * fields + f) * nth + t, b)

    parts = nth // ROWS
    width = weights.shape[-1]

    def project(level, q, place, j):
        ref = filtered[level]
        slot = q - stage.base[level]
        high = highs[place][...]
        left = jnp.concatenate([high, lows[place][...], high], axis=1)
        result = jnp.dot(left, weights[j], preferred_element_type=jnp.float32)
        for i in range(sides):
            for b in range(width // LANES):
                ref[slot * sides + i, j * (width // LANES) + b, PAD : PAD + nth] = result[
                    i * nth : (i + 1) * nth, b * LANES : (b + 1) * LANES
                ]

    def together(task, held):
        def part(j):
            if held is not None:
                project(*held, j)
            if task is not None:
                level, q, place = task
                t = pl.multiple_of(j * ROWS, ROWS)
                if level == 1:
                    split_raw(q, place, t)
                else:
                    advance(level, q, place, t)

        pl.loop(0, parts)(part)

    finish = []

    def carry_out(level):
        if not stage.last:
            ref = filtered[level]
            finish.append(
                copy(ref.at[pl.ds(ref.shape[0] - 2 * sides, 2 * sides)], carries_out[level - 1])
            )

    held = None
    for level in range(1, STEPS + 2):
        for made in waits[level]:
            made.wait()
        for q in range(*stage.todo[level]):
            if held is not None and held[0] == level - 1 and held[1] <= q + 1:
                together(None, held)
                held = None
            place = 0 if held is None else 1 - held[2]
            together((level, q, place), held)
            held = (level, q, place) if level <= STEPS else None
            if level == STEPS + 1:
                for s in range(2):
                    plane = planes - 1 - q if s else q
                    finish.append(copy(own.at[q - out_low, s], out.at[0, :, plane]))
    for level in range(1, STEPS + 1):
        carry_out(level)
    for made in finish:
        made.wait()


def pack(operands, moves, shapes):
    anywhere = pl.BlockSpec(memory_space=pl.ANY)
    plan = [(o, source, len(operands) + result, target) for o, source, result, target in moves]
    return pl.pallas_call(
        functools.partial(pack_kernel, plan),
        out_shape=[jax.ShapeDtypeStruct(shape, jnp.float32) for shape in shapes],
        in_specs=[anywhere] * len(operands),
        out_specs=[anywhere] * len(shapes),
        scratch_shapes=[pltpu.SemaphoreType.DMA((len(plan),))],
        cost_estimate=pl.CostEstimate(
            flops=0, bytes_accessed=8 * sum(math.prod(shape) for shape in shapes), transcendentals=0
        ),
        compiler_params=pltpu.CompilerParams(vmem_limit_bytes=VMEM_MOST),
        name="pack",
    )(*operands)


def run_stage(stage, groups, coupling, odd, weights, own, sensor, chunks, halos, sensor_halos, carries, out):
    fields, planes, nth, nr = own.shape[1:]
    sides = 2 * fields
    blocks = nr // LANES
    held = nth + 2 * PAD
    anywhere = pl.BlockSpec(memory_space=pl.ANY)
    operands = [coupling, odd, weights, own, sensor, *chunks]
    if stage.first:
        operands += [*halos, *sensor_halos]
    else:
        operands += [*carries, out]
    in_specs = [pl.BlockSpec(memory_space=pltpu.SMEM)] * 2 + [anywhere] * (len(operands) - 2)
    out_shape = [jax.ShapeDtypeStruct(own.shape, jnp.float32)]
    if not stage.last:
        out_shape += [jax.ShapeDtypeStruct((2 * sides, blocks, held, LANES), jnp.float32)] * STEPS
    low, high = stage.todo[1]
    outs = stage.todo[STEPS + 1][1] - stage.todo[STEPS + 1][0]
    depths = stage.sensor_high - stage.sensor_low
    copies = 1 + len(chunks) + 2 * STEPS + 2 + STEPS * 2 + 2 * depths + 4 * outs
    scratch = [
        pltpu.VMEM(weights.shape, jnp.bfloat16),
        pltpu.VMEM((outs, 2, fields, nth, nr), jnp.float32),
        pltpu.VMEM((depths, 2, nth, nr), jnp.float32),
        pltpu.VMEM((high - low, 2, fields, nth, nr), jnp.float32),
        *[
            pltpu.VMEM((stage.slots[level] * sides, blocks, held, LANES), jnp.float32)
            for level in range(1, STEPS + 1)
        ],
        *[pltpu.VMEM((sides * nth, nr), jnp.bfloat16)] * 4,
        pltpu.SemaphoreType.DMA((copies,)),
    ]
    limit = VMEM_SPARE + sum(math.prod(s.shape) * s.dtype.itemsize for s in scratch[:-1])
    return pl.pallas_call(
        functools.partial(stage_kernel, stage, fields, planes, groups),
        out_shape=out_shape,
        in_specs=in_specs,
        out_specs=[anywhere] * len(out_shape),
        scratch_shapes=scratch,
        input_output_aliases={} if stage.first else {len(operands) - 1: 0},
        cost_estimate=pl.CostEstimate(flops=0, bytes_accessed=0, transcendentals=0),
        compiler_params=pltpu.CompilerParams(vmem_limit_bytes=limit),
        name=f"stage_{'first' if stage.first else 'last' if stage.last else 'middle'}",
    )(*operands)


def shards(adjoint_in, sensor, filter_matrix, coupling):
    fields, planes, nth, nr = adjoint_in.shape[1:]
    half = planes // 2
    segs = lax.axis_size("seg")
    slabs = lax.axis_size("gx")
    back = [((i + 1) % segs, i) for i in range(segs)]

    groups = []
    for count in GROUPS:
        if sum(groups) + count < half:
            groups.append(count)
    groups.append(half - sum(groups))

    starts = [sum(groups[:i]) for i in range(len(groups))]
    shapes = [(count, 2, fields, nth, nr) for count in groups]
    moves = []
    for i, (start, count) in enumerate(zip(starts, groups)):
        moves.append([])
        for k in range(count):
            for s, plane in enumerate((start + k, planes - 1 - start - k)):
                moves[i].append((0, (0, slice(None), plane), i, (k, s)))
    (first_chunk,) = pack([adjoint_in], moves[0], shapes[:1])
    edge = STEPS - 1
    sensor_moves = [
        (1, (0, plane), len(groups), (k, s))
        for k in range(edge)
        for s, plane in enumerate((k, planes - 1 - k))
    ]
    *rest, sensor_edges = pack(
        [adjoint_in, sensor, first_chunk],
        [(o, a, r - 1, t) for o, a, r, t in sum(moves[1:], []) + sensor_moves],
        shapes[1:] + [(edge, 2, nth, nr)],
    )
    odd = lax.rem(lax.axis_index("gx"), 2)

    def swapped(edges):
        result = []
        for parity in range(2):
            pairs = [(i, i + 1) for i in range(parity, slabs - 1, 2)]
            side = 1 - odd if parity == 0 else odd
            mine = lax.dynamic_index_in_dim(edges, side, 1, keepdims=False)
            result.append(lax.ppermute(mine, "gx", pairs + [(j, i) for i, j in pairs]))
        return result

    high = lax.reduce_precision(filter_matrix, 8, 7)
    low = filter_matrix - high
    weights = jnp.concatenate([high, high, low], axis=0).astype(jnp.bfloat16)
    parts = nth // ROWS
    weights = weights.reshape(STEPS * nr, parts, nr // parts).transpose(1, 0, 2)

    chunks, exchanged = [], []
    for i, packed in enumerate([first_chunk, *rest]):
        if i > 1:
            tied = (packed, weights, chunks[i - 2], *exchanged[i - 2])
            packed, weights, chunks[i - 2], *exchanged[i - 2] = lax.optimization_barrier(tied)
        chunks.append(lax.ppermute(packed, "seg", back))
        if i == 0:
            exchanged.append(swapped(sensor_edges))
        elif i <= STEPS:
            exchanged.append(swapped(chunks[i - 1][:1]))
    sensor_halos, *halos = exchanged
    halos = sum(halos, [])

    odd = odd.astype(jnp.int32)[None]

    cuts = [0, len(groups) - 2, len(groups) - 1, len(groups)]
    carries, out = None, None
    depth = 0
    for low_cut, high_cut in zip(cuts[:-1], cuts[1:]):
        mine = groups[low_cut:high_cut]
        stage = Stage(depth if low_cut else -STEPS, depth + sum(mine), half)
        depth += sum(mine)
        out, *carries = run_stage(
            stage, mine, coupling, odd, weights, adjoint_in, sensor,
            chunks[low_cut:high_cut], halos, sensor_halos, carries, out,
        )
    return out


def solution(mesh):
    in_specs = (P("seg", None, "gx", None, None), P("seg", "gx", None, None), P(), P())
    out_specs = P("seg", None, "gx", None, None)
    return jax.shard_map(shards, mesh=mesh, in_specs=in_specs, out_specs=out_specs, check_vma=False)
```

time: 111 us -> 274 us (2.47)
  Pallas kernels: 48 us -> 220 us
  waiting for transfers between devices: 25.7 us -> 17.3 us
  starting transfers between devices: 25.5 us -> 20.6 us
  local copies, waits for them, and re-layouts: 9.3 us -> 12.7 us
    pallas_call x0 -> x2, Pallas kernels: none -> 169 us  [pack(): pl.pallas_call(functools.partial(pack_kernel, plan), out_shape=[jax.Shape...]
    ppermute x6, waiting for transfers between devices: 14.6 us -> 0.02 us  [shards(): chunks.append(lax.ppermute(packed, 'seg', back))]
    ppermute x8, waiting for transfers between devices: 11.1 us -> 17.3 us  [swapped(): result.append(lax.ppermute(mine, 'gx', pairs + [(j, i) for i, j in pairs]))]
    ppermute x8, starting transfers between devices: 21.6 us -> 17.1 us  [swapped(): result.append(lax.ppermute(mine, 'gx', pairs + [(j, i) for i, j in pairs]))]
    pallas_call x3, Pallas kernels: 48 us -> 51 us  [run_stage(): pl.pallas_call(functools.partial(stage_kernel, stage, fields, planes, gro...]
    unnamed x31 -> x21, local copies, waits for them, and re-layouts: 7.1 us -> 6.45 us
  transfers between devices with their start and end apart: 14 -> 14, of which waited for: 7 -> 3; matrix products, arithmetic and copies ran while one was open for 6% -> 4% of each run, Pallas kernels for 32% -> 68%
where the time goes in v1:
time: 274 us
  Pallas kernels  220 us (80%)
  starting transfers between devices  20.6 us (8%)
  waiting for transfers between devices  17.3 us (6%)
  local copies, waits for them, and re-layouts  12.7 us (5%)
  other arithmetic  2.74 us (1%)
    pallas_call x2, Pallas kernels, pack(): pl.pallas_call(functools.partial(pack_kernel, plan), out_shape=[jax.Shape...  169 us
    pallas_call x3, Pallas kernels, run_stage(): pl.pallas_call(functools.partial(stage_kernel, stage, fields, planes, gro...  51 us
    ppermute x8, waiting for transfers between devices, swapped(): result.append(lax.ppermute(mine, 'gx', pairs + [(j, i) for i, j in pairs]))  17.3 us
    ppermute x8, starting transfers between devices, swapped(): result.append(lax.ppermute(mine, 'gx', pairs + [(j, i) for i, j in pairs]))  17.1 us
    unnamed x21, local copies, waits for them, and re-layouts  6.45 us
  transfers between devices with their start and end apart: 14, of which 3 were waited for; matrix products, arithmetic and copies ran while one was open for 4% of the time, Pallas kernels for 68%

profile of v1, /device:TPU:0, one launch (start us, length us, event | category | flops | bytes accessed | tf_op | source)
XLA Modules:
  0.0 273.9 jit_solution(6204551076838516819)
XLA Ops:
  0.0 21.0 %pack.2.refs_2_ = f32[1,2,5,32,512]{4,3,2,1,0:T(8,128)} custom-call(f32[1,5,16,32,512]{4,3,2,1,0:T(8,128)} %refs_3_.5), custom_call_target="tpu_custom_call" | custom-call | bytes 1310720 | tf_op jit(solution)/shard_map/pack/pallas_call | solution.py:239
  21.0 3.4 %collective-permute-start = (f32[1,2,5,32,512]{4,3,2,1,0:T(8,128)}, f32[1,2,5,32,512]{4,3,2,1,0:T(8,128)S(1)}, u32[]{:S(2)}, u32[]{:S(2)}) collective-permute-start(f32[1,2,5,32,512]{4,3,2,1,0:T(8,128)} %pack.2.refs_2_), channel_id=1, source_target_pairs={{4,0},{8,4},{12,8},{16,12},{20,16},{24,20},{28,24},{0,28},{5,1},{9... | collective-permute-start | bytes 1966088 | tf_op jit(solution)/shard_map/ppermute | solution.py:353
  24.4 148.2 %pack.3 = (f32[1,2,5,32,512]{4,3,2,1,0:T(8,128)}, f32[1,2,5,32,512]{4,3,2,1,0:T(8,128)}, f32[2,2,5,32,512]{4,3,2,1,0:T(8,128)}, f32[2,2,5,32,512]{4,3,2,1,0:T(8,...) custom-call(f32[1,5,16,32,512]{4,3,2,1,0:T(8,128)} %refs_3_.5, f32[1,16,32,512]{3,2,1,0:T(8,128)} %refs_4_.5, ...), custom_call_target="tpu_custom_call" | custom-call | bytes 9699328 | tf_op jit(solution)/shard_map/pack/pallas_call | solution.py:239
  172.5 1.0 dynamic-slice_bitcast_fusion.6
  174.2 4.5 %collective-permute-start.1 = (f32[2,32,512]{2,1,0:T(8,128)S(1)}, f32[2,32,512]{2,1,0:T(8,128)S(1)}, u32[]{:S(2)}, u32[]{:S(2)}) collective-permute-start(f32[2,32,512]{2,1,0:T(8,128)S(1)} %get-tuple-element.82), channel_id=1, source_target_pairs={{0,1},{2,3},{1,0},{3,2},{4,5},{6,7},{5,4},{7,6},{8,9},{10,11},{9,8... | collective-permute-start | bytes 393224 | tf_op jit(solution)/shard_map/ppermute | solution.py:339
  178.8 1.6 copy.7
  180.4 1.0 dynamic-slice_bitcast_fusion.4
  182.0 2.1 collective-permute-start.4
  184.1 1.1 reduce-precision_convert_fusion
  185.2 2.1 copy.9
  187.3 2.1 copy.11
  189.4 1.6 maximum_bitcast_fusion.refs_2_
  191.2 1.1 collective-permute-done.4.refs_9_
  192.3 0.7 collective-permute-start.8
  193.0 4.3 %collective-permute-start.7 = (f32[1,5,32,512]{3,2,1,0:T(8,128)S(1)}, f32[1,5,32,512]{3,2,1,0:T(8,128)S(1)}, u32[]{:S(2)}, u32[]{:S(2)}) collective-permute-start(f32[1,5,32,512]{3,2,1,0:T(8,128)S(1)} %get-tuple-element.78), channel_id=1, source_target_pairs={{0,1},{2,3},{1,0},{3,2},{4,5},{6,7},{5,4},{7,6},{8,9},{10,11},{9,8... | collective-permute-start | bytes 983048 | tf_op jit(solution)/shard_map/ppermute | solution.py:339
  197.4 8.1 %collective-permute-done.7.refs_11_ = f32[1,5,32,512]{3,2,1,0:T(8,128)S(1)} collective-permute-done((f32[1,5,32,512]{3,2,1,0:T(8,128)S(1)}, f32[1,5,32,512]{3,2,1,0:T(8,128)S(1)}, u32[]{:S(2)}, u32[]{:S(2)}) %collective-permute-start.7) | collective-permute-done | bytes 327712 | tf_op jit(solution)/shard_map/ppermute | solution.py:339
  206.2 3.5 %collective-permute-start.10 = (f32[1,5,32,512]{3,2,1,0:T(8,128)S(1)}, f32[1,5,32,512]{3,2,1,0:T(8,128)S(1)}, u32[]{:S(2)}, u32[]{:S(2)}) collective-permute-start(f32[1,5,32,512]{3,2,1,0:T(8,128)S(1)} %get-tuple-element.76), channel_id=1, source_target_pairs={{0,1},{2,3},{1,0},{3,2},{4,5},{6,7},{5,4},{7,6},{8,9},{10,11},{9,8... | collective-permute-start | bytes 983048 | tf_op jit(solution)/shard_map/ppermute | solution.py:339
  209.7 8.1 %collective-permute-done.10.refs_13_ = f32[1,5,32,512]{3,2,1,0:T(8,128)S(1)} collective-permute-done((f32[1,5,32,512]{3,2,1,0:T(8,128)S(1)}, f32[1,5,32,512]{3,2,1,0:T(8,128)S(1)}, u32[]{:S(2)}, u32[]{:S(2)}) %collective-permute-start.10) | collective-permute-done | bytes 327712 | tf_op jit(solution)/shard_map/ppermute | solution.py:339
  217.9 2.5 copy-done
  220.3 24.9 %stage_first.1 = (f32[1,5,16,32,512]{4,3,2,1,0:T(8,128)}, f32[20,4,48,128]{3,2,1,0:T(8,128)S(1)}, f32[20,4,48,128]{3,2,1,0:T(8,128)S(1)}, f32[20,4,48,128]{3,2,1,0:T(8,128)S(1)}) custom-call(f32[5,5]{1,0:T(8,128)S(1)} %copy-done.4, s32[1]{0:T(128)} %bitcast.refs_1_, bf16[2,1536,256]{2,1,0:T(8,128)(2,1)S(1)} %maximum_bitcast_fusion.refs_2_, ...), custom_call_target="tpu_custom_call" | custom-call | tf_op jit(solution)/shard_map/stage_first/pallas_call | solution.py:285
  245.3 1.1 copy-done.2
  246.4 1.3 copy-done.3
  247.7 12.4 %stage_middle.1 = (f32[1,5,16,32,512]{4,3,2,1,0:T(8,128)}, f32[20,4,48,128]{3,2,1,0:T(8,128)S(1)}, f32[20,4,48,128]{3,2,1,0:T(8,128)S(1)}, f32[20,4,48,128]{3,2,1,0:T(8,128)S(1)}) custom-call(f32[5,5]{1,0:T(8,128)S(1)} %copy-done.4, s32[1]{0:T(128)} %bitcast.refs_1_, ...), custom_call_target="tpu_custom_call", output_to_operand_aliasing={{0}: (9, {})} | custom-call | tf_op jit(solution)/shard_map/stage_middle/pallas_call | solution.py:285
  260.1 13.6 %stage_last.1 = f32[1,5,16,32,512]{4,3,2,1,0:T(8,128)} custom-call(f32[5,5]{1,0:T(8,128)S(1)} %copy-done.4, s32[1]{0:T(128)} %bitcast.refs_1_, bf16[2,1536,256]{2,1,0:T(8,128)(2,1)S(1)} %maximum_bitcast_fusion.refs_2_, f32[1,5,16,32,512]{4,3,2,1,0:T(8,128)S(1)} %bitcast.22, f32[1,16,32,512]{3,2,1,0:T(8,128)S(1)} %copy-done.1, ...), custom_call_target="tpu_custom_call", output_to_operand_aliasing={{}: (9, {})} | custom-call | tf_op jit(solution)/shard_map/stage_last/pallas_call | solution.py:285
  (39 shorter events, 2.4 us)
Async XLA Ops:
  21.0 159.4 %collective-permute-start = (f32[1,2,5,32,512]{4,3,2,1,0:T(8,128)}, f32[1,2,5,32,512]{4,3,2,1,0:T(8,128)S(1)}, u32[]{:S(2)}, u32[]{:S(2)}) collective-permute-start(f32[1,2,5,32,512]{4,3,2,1,0:T(8,128)} %pack.2.refs_2_), channel_id=1, source_target_pairs={{4,0},{8,4},{12,8},{16,12},{20,16},{24,20},{28,24},{0,28},{5,1},{9... | collective-permute-start | bytes 1966088 | tf_op jit(solution)/shard_map/ppermute | solution.py:353
  173.5 17.5 %collective-permute-start.2 = (f32[2,32,512]{2,1,0:T(8,128)S(1)}, f32[2,32,512]{2,1,0:T(8,128)S(1)}, u32[]{:S(2)}, u32[]{:S(2)}) collective-permute-start(f32[2,32,512]{2,1,0:T(8,128)S(1)} %get-tuple-element.81), channel_id=1, source_target_pairs={{1,2},{2,1},{5,6},{6,5},{9,10},{10,9},{13,14},{14,13},{17,18},{18,... | collective-permute-start | bytes 393224 | tf_op jit(solution)/shard_map/ppermute | solution.py:339
  174.2 16.9 %collective-permute-start.1 = (f32[2,32,512]{2,1,0:T(8,128)S(1)}, f32[2,32,512]{2,1,0:T(8,128)S(1)}, u32[]{:S(2)}, u32[]{:S(2)}) collective-permute-start(f32[2,32,512]{2,1,0:T(8,128)S(1)} %get-tuple-element.82), channel_id=1, source_target_pairs={{0,1},{2,3},{1,0},{3,2},{4,5},{6,7},{5,4},{7,6},{8,9},{10,11},{9,8... | collective-permute-start | bytes 393224 | tf_op jit(solution)/shard_map/ppermute | solution.py:339
  178.7 12.5 %collective-permute-start.3 = (f32[1,2,5,32,512]{4,3,2,1,0:T(8,128)}, f32[1,2,5,32,512]{4,3,2,1,0:T(8,128)S(1)}, u32[]{:S(2)}, u32[]{:S(2)}) collective-permute-start(f32[1,2,5,32,512]{4,3,2,1,0:T(8,128)} %get-tuple-element.45), channel_id=1, source_target_pairs={{4,0},{8,4},{12,8},{16,12},{20,16},{24,20},{28,24},{0,28},{5,1},{9... | collective-permute-start | bytes 1966088 | tf_op jit(solution)/shard_map/ppermute | solution.py:353
  181.3 9.8 %collective-permute-start.5 = (f32[1,5,32,512]{3,2,1,0:T(8,128)}, f32[1,5,32,512]{3,2,1,0:T(8,128)S(1)}, u32[]{:S(2)}, u32[]{:S(2)}) collective-permute-start(f32[1,5,32,512]{3,2,1,0:T(8,128)} %get-tuple-element.79), channel_id=1, source_target_pairs={{1,2},{2,1},{5,6},{6,5},{9,10},{10,9},{13,14},{14,13},{17,18},{18,... | collective-permute-start | bytes 983048 | tf_op jit(solution)/shard_map/ppermute | solution.py:339
  182.0 10.3 %collective-permute-start.4 = (f32[1,5,32,512]{3,2,1,0:T(8,128)}, f32[1,5,32,512]{3,2,1,0:T(8,128)S(1)}, u32[]{:S(2)}, u32[]{:S(2)}) collective-permute-start(f32[1,5,32,512]{3,2,1,0:T(8,128)} %get-tuple-element.80), channel_id=1, source_target_pairs={{0,1},{2,3},{1,0},{3,2},{4,5},{6,7},{5,4},{7,6},{8,9},{10,11},{9,8... | collective-permute-start | bytes 983048 | tf_op jit(solution)/shard_map/ppermute | solution.py:339
  187.3 59.1 %slice-start = ((s8[5242880]{0:T(1024)(128)(4,1)}), s8[1048576]{0:T(1024)(128)(4,1)S(1)}, s32[]{:S(2)}) async-start(s8[5242880]{0:T(1024)(128)(4,1)} %bitcast.21), calls=%async_computation | async-start | bytes 2097152
  189.4 2.9 %copy-start.6 = (f32[2,2,5,32,512]{4,3,2,1,0:T(8,128)S(1)}, f32[2,2,5,32,512]{4,3,2,1,0:T(8,128)}, u32[]{:S(2)}) copy-start(f32[2,2,5,32,512]{4,3,2,1,0:T(8,128)} %get-tuple-element.49) | copy-start | bytes 3932164
  189.4 16.1 %copy-start.5 = (f32[2,2,5,32,512]{4,3,2,1,0:T(8,128)S(1)}, f32[2,2,5,32,512]{4,3,2,1,0:T(8,128)}, u32[]{:S(2)}) copy-start(f32[2,2,5,32,512]{4,3,2,1,0:T(8,128)} %get-tuple-element.52) | copy-start | bytes 3932164
  191.0 26.8 %copy-start.7 = (f32[1,2,5,32,512]{4,3,2,1,0:T(8,128)S(1)}, f32[1,2,5,32,512]{4,3,2,1,0:T(8,128)}, u32[]{:S(2)}) copy-start(f32[1,2,5,32,512]{4,3,2,1,0:T(8,128)} %get-tuple-element.51) | copy-start | bytes 1966084
  191.0 26.8 %copy-start.1 = (f32[1,16,32,512]{3,2,1,0:T(8,128)S(1)}, f32[1,16,32,512]{3,2,1,0:T(8,128)}, u32[]{:S(2)}) copy-start(f32[1,16,32,512]{3,2,1,0:T(8,128)} %refs_4_.5) | copy-start | bytes 3145732
  191.1 26.8 %copy-start.4 = (f32[5,5]{1,0:T(8,128)S(1)}, f32[5,5]{1,0:T(8,128)}, u32[]{:S(2)}) copy-start(f32[5,5]{1,0:T(8,128)} %refs_0_.9) | copy-start | bytes 304
  191.1 14.4 %collective-permute-start.6 = (f32[1,2,5,32,512]{4,3,2,1,0:T(8,128)}, f32[1,2,5,32,512]{4,3,2,1,0:T(8,128)S(1)}, u32[]{:S(2)}, u32[]{:S(2)}) collective-permute-start(f32[1,2,5,32,512]{4,3,2,1,0:T(8,128)} %get-tuple-element.47), channel_id=1, source_target_pairs={{4,0},{8,4},{12,8},{16,12},{20,16},{24,20},{28,24},{0,28},{5,1},{9... | collective-permute-start | bytes 1966088 | tf_op jit(solution)/shard_map/ppermute | solution.py:353
  192.3 25.5 %collective-permute-start.9 = (f32[2,2,5,32,512]{4,3,2,1,0:T(8,128)S(1)}, f32[2,2,5,32,512]{4,3,2,1,0:T(8,128)S(1)}, u32[]{:S(2)}, u32[]{:S(2)}) collective-permute-start(f32[2,2,5,32,512]{4,3,2,1,0:T(8,128)S(1)} %copy-done.6), channel_id=1, source_target_pairs={{4,0},{8,4},{12,8},{16,12},{20,16},{24,20},{28,24},{0,28},{5,1},{9... | collective-permute-start | bytes 3932168 | tf_op jit(solution)/shard_map/ppermute | solution.py:353
  192.3 5.0 %collective-permute-start.8 = (f32[1,5,32,512]{3,2,1,0:T(8,128)S(1)}, f32[1,5,32,512]{3,2,1,0:T(8,128)S(1)}, u32[]{:S(2)}, u32[]{:S(2)}) collective-permute-start(f32[1,5,32,512]{3,2,1,0:T(8,128)S(1)} %get-tuple-element.77), channel_id=1, source_target_pairs={{1,2},{2,1},{5,6},{6,5},{9,10},{10,9},{13,14},{14,13},{17,18},{18,... | collective-permute-start | bytes 983048 | tf_op jit(solution)/shard_map/ppermute | solution.py:339
  193.0 12.4 %collective-permute-start.7 = (f32[1,5,32,512]{3,2,1,0:T(8,128)S(1)}, f32[1,5,32,512]{3,2,1,0:T(8,128)S(1)}, u32[]{:S(2)}, u32[]{:S(2)}) collective-permute-start(f32[1,5,32,512]{3,2,1,0:T(8,128)S(1)} %get-tuple-element.78), channel_id=1, source_target_pairs={{0,1},{2,3},{1,0},{3,2},{4,5},{6,7},{5,4},{7,6},{8,9},{10,11},{9,8... | collective-permute-start | bytes 983048 | tf_op jit(solution)/shard_map/ppermute | solution.py:339
  205.5 39.8 %collective-permute-start.13 = (f32[2,2,5,32,512]{4,3,2,1,0:T(8,128)S(1)}, f32[2,2,5,32,512]{4,3,2,1,0:T(8,128)S(1)}, u32[]{:S(2)}, u32[]{:S(2)}) collective-permute-start(f32[2,2,5,32,512]{4,3,2,1,0:T(8,128)S(1)} %copy-done.5), channel_id=1, source_target_pairs={{4,0},{8,4},{12,8},{16,12},{20,16},{24,20},{28,24},{0,28},{5,1},{9... | collective-permute-start | bytes 3932168 | tf_op jit(solution)/shard_map/ppermute | solution.py:353
  205.5 4.2 %collective-permute-start.11 = (f32[1,5,32,512]{3,2,1,0:T(8,128)S(1)}, f32[1,5,32,512]{3,2,1,0:T(8,128)S(1)}, u32[]{:S(2)}, u32[]{:S(2)}) collective-permute-start(f32[1,5,32,512]{3,2,1,0:T(8,128)S(1)} %get-tuple-element.75), channel_id=1, source_target_pairs={{1,2},{2,1},{5,6},{6,5},{9,10},{10,9},{13,14},{14,13},{17,18},{18,... | collective-permute-start | bytes 983048 | tf_op jit(solution)/shard_map/ppermute | solution.py:339
  206.2 11.6 %collective-permute-start.10 = (f32[1,5,32,512]{3,2,1,0:T(8,128)S(1)}, f32[1,5,32,512]{3,2,1,0:T(8,128)S(1)}, u32[]{:S(2)}, u32[]{:S(2)}) collective-permute-start(f32[1,5,32,512]{3,2,1,0:T(8,128)S(1)} %get-tuple-element.76), channel_id=1, source_target_pairs={{0,1},{2,3},{1,0},{3,2},{4,5},{6,7},{5,4},{7,6},{8,9},{10,11},{9,8... | collective-permute-start | bytes 983048 | tf_op jit(solution)/shard_map/ppermute | solution.py:339
  217.8 42.3 %collective-permute-start.12 = (f32[1,2,5,32,512]{4,3,2,1,0:T(8,128)S(1)}, f32[1,2,5,32,512]{4,3,2,1,0:T(8,128)S(1)}, u32[]{:S(2)}, u32[]{:S(2)}) collective-permute-start(f32[1,2,5,32,512]{4,3,2,1,0:T(8,128)S(1)} %copy-done.7), channel_id=1, source_target_pairs={{4,0},{8,4},{12,8},{16,12},{20,16},{24,20},{28,24},{0,28},{5,1},{9... | collective-permute-start | bytes 1966088 | tf_op jit(solution)/shard_map/ppermute | solution.py:353
  217.8 2.5 copy-start
  220.3 26.0 %slice-start.1 = ((s8[5242880]{0:T(1024)(128)(4,1)}), s8[4194304]{0:T(1024)(128)(4,1)S(1)}, s32[]{:S(2)}) async-start(s8[5242880]{0:T(1024)(128)(4,1)} %bitcast.21), calls=%async_computation.1 | async-start | bytes 8388608
  245.3 1.1 copy-start.2
  246.4 1.3 copy-start.3

commit v2 on v1

v2 whole, which is shorter than its diff:
```python
import functools
import math

import jax
import jax.numpy as jnp
from jax import lax
from jax.experimental import pallas as pl
from jax.experimental.pallas import tpu as pltpu
from jax.sharding import PartitionSpec as P

STEPS = 3
LANES = 128
PAD = 8
ROWS = 16
GROUPS = (1, 1, 1, 1, 1, 1, 1)
TOGETHER = 2
VMEM_SPARE = 6 * 1024 * 1024
VMEM_MOST = 60 * 1024 * 1024


class Stage:
    def __init__(self, start, stop, half):
        self.half = half
        self.first, self.last = start == -STEPS, stop == half
        self.todo = {}
        for level in range(1, STEPS + 2):
            lag = level - 1
            low = start + lag if self.first else start - lag
            self.todo[level] = (low, stop if self.last else stop - lag)
        self.taken, self.given, self.kept = [], [], []
        for level in range(1, STEPS + 1):
            low, high = self.todo[level]
            if not self.first:
                self.taken += [(level, low - 2), (level, low - 1)]
            handed = high if self.last else high - 2
            self.kept += [(level, q) for q in range(low, min(handed, high))]
            self.given += [(level, q) for q in range(max(handed, low), high)]


def pack_first_kernel(planes, source, result, sems):
    made = []
    for s, plane in enumerate((0, planes - 1)):
        made.append(pltpu.make_async_copy(source.at[0, :, plane], result.at[0, s], sems.at[s]))
        made[-1].start()
    for one in made:
        one.wait()


def pack_rest_kernel(planes, groups, source, sensor, first, *results):
    del first
    depth = groups[0]
    for result, count in zip(results, groups[1:]):
        for k in range(count):
            for s, plane in enumerate((depth + k, planes - 1 - depth - k)):

                def field(f, result=result, k=k, s=s, plane=plane):
                    result[k, s, f] = source[0, f, plane]

                pl.loop(0, source.shape[1])(field)
        depth += count
    for k in range(STEPS - 1):
        for s, plane in enumerate((k, planes - 1 - k)):
            results[-1][k, s] = sensor[0, plane]


def stage_kernel(stage, fields, planes, groups, *refs):
    refs = list(refs)

    def take(count):
        got = refs[:count]
        del refs[:count]
        return got

    (coupling, odd_ref, weights, own, sensor) = take(5)
    chunks = take(len(groups))
    halos = take(2 * STEPS) if stage.first else []
    sensor_halos = take(2) if stage.first else []
    filtered = dict(zip(stage.taken, take(len(stage.taken))))
    if not stage.first:
        take(1)
    (out,) = take(1)
    fresh = dict(zip(stage.given, take(len(stage.given))))
    (result,) = take(1)
    fresh.update(zip(stage.kept, take(len(stage.kept))))
    filtered.update(fresh)
    highs = take(2)
    lows = take(2)
    (sems,) = take(1)

    sides = 2 * fields
    nth, nr = own.shape[-2:]
    blocks = nr // LANES
    stride = nth + PAD
    odd = odd_ref[0]

    blank = jnp.zeros((PAD, LANES), jnp.float32)
    for ref in fresh.values():

        def clear(i, ref=ref):
            for b in range(blocks):
                ref[b, pl.ds(pl.multiple_of(i * stride, PAD), PAD)] = blank

        pl.loop(0, sides + 1)(clear)

    lane = lax.broadcasted_iota(jnp.int32, (ROWS, LANES), 1)
    at_start = lane == 0
    at_end = lane == LANES - 1
    weight = [[coupling[g, f] for f in range(fields)] for g in range(fields)]

    def columns(b):
        return slice(b * LANES, (b + 1) * LANES)

    def put(value, place, row, b):
        at = (pl.ds(pl.multiple_of(row, ROWS), ROWS), columns(b))
        high = value.astype(jnp.bfloat16)
        highs[place][at] = high
        lows[place][at] = (value - high.astype(jnp.float32)).astype(jnp.bfloat16)

    def split_raw(q, place, t):
        for s in range(2):
            if q < 0:
                source = halos[2 * (-1 - q) + s].at[0]
                side = 1 - odd if s == 0 else odd
            else:
                chunk, k = starts[q]
                source, side = chunks[chunk].at[k, s], s
            for f in range(fields):
                for b in range(blocks):
                    put(source[f, pl.ds(t, ROWS), columns(b)], place, (side * fields + f) * nth + t, b)

    def sensor_at(q, s, t, b):
        if q >= 0:
            return sensor[0, planes - 1 - q if s else q, pl.ds(t, ROWS), columns(b)]
        pair = [ref[-1 - q, pl.ds(t, ROWS), columns(b)] for ref in sensor_halos]
        return jnp.where(odd == s, pair[1], pair[0])

    def advance(level, q, place, t):
        here = filtered[level - 1, q]
        before = filtered[level - 1, q - 1]
        inner = q < stage.half - 1
        after = filtered[level - 1, q + 1] if inner else here
        for s in range(2):
            rows = [(s * fields + f) * stride + PAD + t for f in range(fields)]
            beyond = rows if inner else [((1 - s) * fields + f) * stride + PAD + t for f in range(fields)]
            aligned = [pl.ds(pl.multiple_of(row, PAD), ROWS) for row in rows]
            beyond = [pl.ds(pl.multiple_of(row, PAD), ROWS) for row in beyond]
            middles = [[here[b, aligned[f]] for b in range(blocks)] for f in range(fields)]
            for b in range(blocks):
                laps = []
                for f in range(fields):
                    middle = middles[f][b]
                    lower = middles[f][b - 1] if b else 0.0
                    upper = middles[f][b + 1] if b + 1 < blocks else 0.0
                    left = pltpu.roll(jnp.where(at_end, lower, middle), 1, 1)
                    right = pltpu.roll(jnp.where(at_start, upper, middle), LANES - 1, 1)
                    axial = before[b, aligned[f]] + after[b, beyond[f]]
                    around = here[b, pl.ds(rows[f] - 1, ROWS)] + here[b, pl.ds(rows[f] + 1, ROWS)]
                    laps.append((axial + around) + (left + right) - 6.0 * middle)
                sens = sensor_at(q, s, t, b)
                for f in range(fields):
                    mixed = weight[0][f] * laps[0]
                    for g in range(1, fields):
                        mixed = mixed + weight[g][f] * laps[g]
                    value = middles[f][b] + sens * mixed
                    if level == STEPS + 1:
                        plane = planes - 1 - q if s else q
                        at = (pl.ds(t, ROWS), columns(b))
                        result[(q - out_low, s, f, *at)] = value - own[(0, f, plane, *at)]
                    else:
                        put(value, place, (s * fields + f) * nth + t, b)

    starts = {}
    depth = max(stage.todo[1][0], 0)
    for i, count in enumerate(groups):
        for k in range(count):
            starts[depth] = (i, k)
            depth += 1
    out_low = stage.todo[STEPS + 1][0]
    parts = nth // ROWS
    width = weights.shape[-1]

    def project(level, q, place, j):
        ref = filtered[level, q]
        high = highs[place][...]
        left = jnp.concatenate([high, lows[place][...], high], axis=1)
        product = jnp.dot(left, weights[j], preferred_element_type=jnp.float32)
        for i in range(sides):
            for b in range(width // LANES):
                ref[j * (width // LANES) + b, i * stride + PAD : (i + 1) * stride] = product[
                    i * nth : (i + 1) * nth, columns(b)
                ]

    def together(task, held):
        def part(j):
            if held is not None:
                project(*held, j)
            if task is not None:
                level, q, place = task
                t = pl.multiple_of(j * ROWS, ROWS)
                if level == 1:
                    split_raw(q, place, t)
                else:
                    advance(level, q, place, t)

        pl.loop(0, parts)(part)

    held = None
    sent = []
    for level in range(1, STEPS + 2):
        for q in range(*stage.todo[level]):
            if held is not None and held[0] == level - 1 and held[1] <= q + 1:
                together(None, held)
                held = None
            place = 0 if held is None else 1 - held[2]
            together((level, q, place), held)
            held = (level, q, place) if level <= STEPS else None
            if level == STEPS + 1:
                for s in range(2):
                    plane = planes - 1 - q if s else q
                    sent.append(
                        pltpu.make_async_copy(result.at[q - out_low, s], out.at[0, :, plane], sems.at[len(sent)])
                    )
                    sent[-1].start()
    if held is not None:
        together(None, held)
    for made in sent:
        made.wait()


ANYWHERE = pl.BlockSpec(memory_space=pl.ANY)
CLOSE = pl.BlockSpec(memory_space=pltpu.VMEM)
SCALARS = pl.BlockSpec(memory_space=pltpu.SMEM)


def size(*arrays):
    return sum(math.prod(array.shape) * array.dtype.itemsize for array in arrays)


def pack_first(adjoint_in):
    fields, planes, nth, nr = adjoint_in.shape[1:]
    return pl.pallas_call(
        functools.partial(pack_first_kernel, planes),
        out_shape=jax.ShapeDtypeStruct((1, 2, fields, nth, nr), jnp.float32),
        in_specs=[ANYWHERE],
        out_specs=CLOSE,
        scratch_shapes=[pltpu.SemaphoreType.DMA((2,))],
        compiler_params=pltpu.CompilerParams(vmem_limit_bytes=VMEM_MOST),
        name="pack_first",
    )(adjoint_in)


def pack_rest(adjoint_in, sensor, first, groups):
    fields, planes, nth, nr = adjoint_in.shape[1:]
    shapes = [(count, 2, fields, nth, nr) for count in groups[1:]] + [(STEPS - 1, 2, nth, nr)]
    out_shape = [jax.ShapeDtypeStruct(shape, jnp.float32) for shape in shapes]
    return pl.pallas_call(
        functools.partial(pack_rest_kernel, planes, groups),
        out_shape=out_shape,
        in_specs=[CLOSE, CLOSE, ANYWHERE],
        out_specs=[CLOSE] * len(shapes),
        cost_estimate=pl.CostEstimate(flops=0, bytes_accessed=2 * size(*out_shape), transcendentals=0),
        compiler_params=pltpu.CompilerParams(
            vmem_limit_bytes=VMEM_SPARE + size(adjoint_in, sensor, *out_shape)
        ),
        name="pack_rest",
    )(adjoint_in, sensor, first)


def run_stage(stage, groups, coupling, odd, weights, own, sensor, chunks, halos, sensor_halos, carried, out):
    fields, planes, nth, nr = own.shape[1:]
    sides = 2 * fields
    slot = (nr // LANES, sides * (nth + PAD) + PAD, LANES)
    close = [weights, own, sensor, *chunks]
    if stage.first:
        close += [*halos, *sensor_halos]
    close += [carried[key] for key in stage.taken]
    operands = [coupling, odd, *close] + ([] if stage.first else [out])
    in_specs = [SCALARS] * 2 + [CLOSE] * len(close) + ([] if stage.first else [ANYWHERE])
    given = [jax.ShapeDtypeStruct(slot, jnp.float32)] * len(stage.given)
    low, high = stage.todo[STEPS + 1]
    scratch = [
        pltpu.VMEM((high - low, 2, fields, nth, nr), jnp.float32),
        *[pltpu.VMEM(slot, jnp.float32)] * len(stage.kept),
        *[pltpu.VMEM((sides * nth, nr), jnp.bfloat16)] * 4,
    ]
    limit = VMEM_SPARE + size(*scratch, *close, *given)
    out, *fresh = pl.pallas_call(
        functools.partial(stage_kernel, stage, fields, planes, groups),
        out_shape=[jax.ShapeDtypeStruct(own.shape, jnp.float32), *given],
        in_specs=in_specs,
        out_specs=[ANYWHERE] + [CLOSE] * len(given),
        scratch_shapes=scratch + [pltpu.SemaphoreType.DMA((2 * max(high - low, 1),))],
        input_output_aliases={} if stage.first else {len(operands) - 1: 0},
        cost_estimate=pl.CostEstimate(
            flops=0, bytes_accessed=size(*close, *given) if stage.first else 0, transcendentals=0
        ),
        compiler_params=pltpu.CompilerParams(vmem_limit_bytes=limit),
        name=f"stage_{'first' if stage.first else 'last' if stage.last else 'middle'}",
    )(*operands)
    return out, dict(zip(stage.given, fresh))


def shards(adjoint_in, sensor, filter_matrix, coupling):
    fields, planes, nth, nr = adjoint_in.shape[1:]
    half = planes // 2
    segs = lax.axis_size("seg")
    slabs = lax.axis_size("gx")
    back = [((i + 1) % segs, i) for i in range(segs)]

    groups = []
    for count in GROUPS:
        if sum(groups) + count < half:
            groups.append(count)
    groups.append(half - sum(groups))

    first_chunk = pack_first(adjoint_in)
    *rest, sensor_edges = pack_rest(adjoint_in, sensor, first_chunk, groups)

    odd = lax.rem(lax.axis_index("gx"), 2)

    def swapped(edges):
        result = []
        for parity in range(2):
            pairs = [(i, i + 1) for i in range(parity, slabs - 1, 2)]
            side = 1 - odd if parity == 0 else odd
            mine = lax.dynamic_index_in_dim(edges, side, 1, keepdims=False)
            result.append(lax.ppermute(mine, "gx", pairs + [(j, i) for i, j in pairs]))
        return result

    high = lax.reduce_precision(filter_matrix, 8, 7)
    low = filter_matrix - high
    parts = nth // ROWS
    weights = [
        jnp.concatenate([high[:, at], high[:, at], low[:, at]], axis=0)
        for at in (slice(j * (nr // parts), (j + 1) * (nr // parts)) for j in range(parts))
    ]
    weights = jnp.stack(weights).astype(jnp.bfloat16)
    scalar = odd.astype(jnp.int32)[None]

    stages = [(0, STEPS)]
    while stages[-1][1] < len(groups):
        low_cut = stages[-1][1]
        stages.append((low_cut, max(min(low_cut + TOGETHER, len(groups) - 1), low_cut + 1)))
    cuts = [sum(groups[:i]) for i in range(len(groups) + 1)]
    carried, out = {}, None
    halos, sensor_halos = [], []

    def run(number):
        nonlocal out
        low_cut, high_cut = stages[number]
        mine = groups[low_cut:high_cut]
        stage = Stage(cuts[low_cut] if number else -STEPS, cuts[high_cut], half)
        out, fresh = run_stage(
            stage, mine, coupling, scalar, weights, adjoint_in, sensor,
            chunks[low_cut:high_cut], halos, sensor_halos, carried, out,
        )
        carried.update(fresh)

    chunks, exchanged = [], []
    ran = 0

    def unpack():
        nonlocal sensor_halos, halos
        sensor_halos, *halos = exchanged
        halos = sum(halos, [])

    for i, packed in enumerate([first_chunk, *rest]):
        if i >= STEPS + 3 and stages[ran][1] < i:
            if ran == 0:
                unpack()
            run(ran)
            ran += 1
            key = max(carried)
            packed, carried[key] = lax.optimization_barrier((packed, carried[key]))
        elif i > 1:
            ends = exchanged[i - 2] if i - 2 < len(exchanged) else []
            packed, weights, chunks[i - 2], *ends = lax.optimization_barrier((packed, weights, chunks[i - 2], *ends))
            if ends:
                exchanged[i - 2] = ends
        chunks.append(lax.ppermute(packed, "seg", back))
        if i == 0:
            exchanged.append(swapped(sensor_edges))
        elif i <= STEPS:
            exchanged.append(swapped(chunks[i - 1][:1]))
    for number in range(ran, len(stages)):
        if number == 0:
            unpack()
        run(number)
    return out


def solution(mesh):
    in_specs = (P("seg", None, "gx", None, None), P("seg", "gx", None, None), P(), P())
    out_specs = P("seg", None, "gx", None, None)
    return jax.shard_map(shards, mesh=mesh, in_specs=in_specs, out_specs=out_specs, check_vma=False)
```

time: 274 us -> 98.4 us (0.36)
  Pallas kernels: 220 us -> 42.8 us
  local copies, waits for them, and re-layouts: 12.7 us -> 8.17 us
  waiting for transfers between devices: 17.3 us -> 20.6 us
  starting transfers between devices: 20.6 us -> 23.6 us
    pallas_call x2, Pallas kernels: 169 us -> 2.5 us  [the longest x1 2.01 us: pack_first(): pl.pallas_call(functools.partial(pack_first_kernel, planes), out_shape=ja...]
    pallas_call x3 -> x4, Pallas kernels: 51 us -> 40.3 us  [run_stage(): pl.pallas_call(functools.partial(stage_kernel, stage, fields, planes, gro...]
    ppermute x6 -> x8, starting transfers between devices: 3.57 us -> 6.36 us  [shards(): chunks.append(lax.ppermute(packed, 'seg', back))]
    unnamed x21 -> x32, local copies, waits for them, and re-layouts: 6.45 us -> 7.95 us
  transfers between devices with their start and end apart: 14 -> 16, of which waited for: 3 -> 5; matrix products, arithmetic and copies ran while one was open for 4% -> 2% of each run, Pallas kernels for 68% -> 31%
where the time goes in v2:
time: 98.4 us; the launch traced here: 97.4 us
  Pallas kernels  42.8 us (43%)
  starting transfers between devices  23.6 us (24%)
  waiting for transfers between devices  20.6 us (21%)
  local copies, waits for them, and re-layouts  8.17 us (8%)
  other arithmetic  1.84 us (2%)
    pallas_call x4, Pallas kernels, run_stage(): pl.pallas_call(functools.partial(stage_kernel, stage, fields, planes, gro...  40.3 us
    ppermute x8, waiting for transfers between devices, swapped(): result.append(lax.ppermute(mine, 'gx', pairs + [(j, i) for i, j in pairs]))  20 us
    ppermute x8, starting transfers between devices, swapped(): result.append(lax.ppermute(mine, 'gx', pairs + [(j, i) for i, j in pairs]))  17.2 us
    unnamed x32, local copies, waits for them, and re-layouts  7.95 us
    ppermute x8, starting transfers between devices, shards(): chunks.append(lax.ppermute(packed, 'seg', back))  6.36 us
    pallas_call x1, Pallas kernels, pack_first(): pl.pallas_call(functools.partial(pack_first_kernel, planes), out_shape=ja...  2.01 us
  transfers between devices with their start and end apart: 16, of which 5 were waited for; matrix products, arithmetic and copies ran while one was open for 2% of the time, Pallas kernels for 31%

profile of v2, /device:TPU:0, one launch (start us, length us, event | category | flops | bytes accessed | tf_op | source)
XLA Modules:
  0.0 97.4 jit_solution(10972217027933382052)
XLA Ops:
  0.0 2.0 %pack_first.1.first = f32[1,2,5,32,512]{4,3,2,1,0:T(8,128)} custom-call(f32[1,5,16,32,512]{4,3,2,1,0:T(8,128)} %refs_3_.7), custom_call_target="tpu_custom_call" | custom-call | tf_op jit(solution)/shard_map/pack_first/pallas_call | solution.py:241
  2.0 3.4 %collective-permute-start = (f32[1,2,5,32,512]{4,3,2,1,0:T(8,128)}, f32[1,2,5,32,512]{4,3,2,1,0:T(8,128)S(1)}, u32[]{:S(2)}, u32[]{:S(2)}) collective-permute-start(f32[1,2,5,32,512]{4,3,2,1,0:T(8,128)} %pack_first.1.first), channel_id=1, source_target_pairs={{4,0},{8,4},{12,8},{16,12},{20,16},{24,20},{28,24},{0,28},{5,1},{9... | collective-permute-start | bytes 1966088 | tf_op jit(solution)/shard_map/ppermute | solution.py:380
  5.4 2.5 %copy-done = f32[1,5,16,32,512]{4,3,2,1,0:T(8,128)S(1)} copy-done((f32[1,5,16,32,512]{4,3,2,1,0:T(8,128)S(1)}, f32[1,5,16,32,512]{4,3,2,1,0:T(8,128)}, u32[]{:S(2)}) %copy-start) | copy-done | bytes 5242904
  7.9 1.1 %copy-done.2 = f32[1,2,5,32,512]{4,3,2,1,0:T(8,128)S(1)} copy-done((f32[1,2,5,32,512]{4,3,2,1,0:T(8,128)S(1)}, f32[1,2,5,32,512]{4,3,2,1,0:T(8,128)}, u32[]{:S(2)}) %copy-start.2) | copy-done | bytes 655384
  9.5 0.8 copy-done.4
  10.3 0.9 copy-done.6
  11.2 0.8 copy-done.8
  12.0 0.8 copy-done.10
  12.8 0.8 copy-done.12
  14.5 4.5 %collective-permute-start.1 = (f32[2,32,512]{2,1,0:T(8,128)S(1)}, f32[2,32,512]{2,1,0:T(8,128)S(1)}, u32[]{:S(2)}, u32[]{:S(2)}) collective-permute-start(f32[2,32,512]{2,1,0:T(8,128)S(1)} %get-tuple-element.122), channel_id=1, source_target_pairs={{0,1},{2,3},{1,0},{3,2},{4,5},{6,7},{5,4},{7,6},{8,9},{10,11},{9,8... | collective-permute-start | bytes 393224 | tf_op jit(solution)/shard_map/ppermute | solution.py:327
  19.1 1.5 %subtract_convert_fusion = bf16[512,512]{1,0:T(8,128)(2,1)S(1)} fusion(f32[512,512]{1,0:T(8,128)} %param.6), kind=kLoop, calls=%fused_computation.1 | loop fusion | flops 786432 | bytes 1572864 | tf_op jit(solution)/shard_map/convert.11
  21.1 0.8 collective-permute-done.1.refs_14_
  22.8 0.8 collective-permute-start.5
  23.6 3.3 %collective-permute-start.4 = (f32[1,5,32,512]{3,2,1,0:T(8,128)S(1)}, f32[1,5,32,512]{3,2,1,0:T(8,128)S(1)}, u32[]{:S(2)}, u32[]{:S(2)}) collective-permute-start(f32[1,5,32,512]{3,2,1,0:T(8,128)S(1)} %get-tuple-element.116), channel_id=1, source_target_pairs={{0,1},{2,3},{1,0},{3,2},{4,5},{6,7},{5,4},{7,6},{8,9},{10,11},{9,8... | collective-permute-start | bytes 983048 | tf_op jit(solution)/shard_map/ppermute | solution.py:327
  28.3 2.2 %collective-permute-start.7 = (f32[1,5,32,512]{3,2,1,0:T(8,128)S(1)}, f32[1,5,32,512]{3,2,1,0:T(8,128)S(1)}, u32[]{:S(2)}, u32[]{:S(2)}) collective-permute-start(f32[1,5,32,512]{3,2,1,0:T(8,128)S(1)} %get-tuple-element.114), channel_id=1, source_target_pairs={{0,1},{2,3},{1,0},{3,2},{4,5},{6,7},{5,4},{7,6},{8,9},{10,11},{9,8... | collective-permute-start | bytes 983048 | tf_op jit(solution)/shard_map/ppermute | solution.py:327
  30.4 5.0 %collective-permute-done.4.refs_8_ = f32[1,5,32,512]{3,2,1,0:T(8,128)S(1)} collective-permute-done((f32[1,5,32,512]{3,2,1,0:T(8,128)S(1)}, f32[1,5,32,512]{3,2,1,0:T(8,128)S(1)}, u32[]{:S(2)}, u32[]{:S(2)}) %collective-permute-start.4) | collective-permute-done | bytes 327712 | tf_op jit(solution)/shard_map/ppermute | solution.py:327
  35.5 6.3 %collective-permute-done.7.refs_10_ = f32[1,5,32,512]{3,2,1,0:T(8,128)S(1)} collective-permute-done((f32[1,5,32,512]{3,2,1,0:T(8,128)S(1)}, f32[1,5,32,512]{3,2,1,0:T(8,128)S(1)}, u32[]{:S(2)}, u32[]{:S(2)}) %collective-permute-start.7) | collective-permute-done | bytes 327712 | tf_op jit(solution)/shard_map/ppermute | solution.py:327
  43.0 4.3 %collective-permute-start.10 = (f32[1,5,32,512]{3,2,1,0:T(8,128)S(1)}, f32[1,5,32,512]{3,2,1,0:T(8,128)S(1)}, u32[]{:S(2)}, u32[]{:S(2)}) collective-permute-start(f32[1,5,32,512]{3,2,1,0:T(8,128)S(1)} %get-tuple-element.112), channel_id=1, source_target_pairs={{0,1},{2,3},{1,0},{3,2},{4,5},{6,7},{5,4},{7,6},{8,9},{10,11},{9,8... | collective-permute-start | bytes 983048 | tf_op jit(solution)/shard_map/ppermute | solution.py:327
  47.3 7.9 %collective-permute-done.10.refs_12_ = f32[1,5,32,512]{3,2,1,0:T(8,128)S(1)} collective-permute-done((f32[1,5,32,512]{3,2,1,0:T(8,128)S(1)}, f32[1,5,32,512]{3,2,1,0:T(8,128)S(1)}, u32[]{:S(2)}, u32[]{:S(2)}) %collective-permute-start.10) | collective-permute-done | bytes 327712 | tf_op jit(solution)/shard_map/ppermute | solution.py:327
  55.7 12.8 %stage_first.1 = (f32[1,5,16,32,512]{4,3,2,1,0:T(8,128)}, f32[4,408,128]{2,1,0:T(8,128)S(1)}, f32[4,408,128]{2,1,0:T(8,128)S(1)}, f32[4,408,128]{2,1,0:T(8,128)S...) custom-call(f32[5,5]{1,0:T(8,128)S(1)} %copy-done.3, s32[1]{0:T(128)} %bitcast.refs_1_, ...), custom_call_target="tpu_custom_call" | custom-call | bytes 17072128 | tf_op jit(solution)/shard_map/stage_first/pallas_call | solution.py:287
  68.6 0.8 collective-permute-start.15
  69.4 8.6 %stage_middle.2 = (f32[1,5,16,32,512]{4,3,2,1,0:T(8,128)}, f32[4,408,128]{2,1,0:T(8,128)S(1)}, f32[4,408,128]{2,1,0:T(8,128)S(1)}, f32[4,408,128]{2,1,0:T(8,128)...) custom-call(f32[5,5]{1,0:T(8,128)S(1)} %copy-done.3, ...), custom_call_target="tpu_custom_call", output_to_operand_aliasing={{0}: (13, {})} | custom-call | tf_op jit(solution)/shard_map/stage_middle/pallas_call | solution.py:287
  78.3 8.5 %stage_middle.3 = (f32[1,5,16,32,512]{4,3,2,1,0:T(8,128)}, f32[4,408,128]{2,1,0:T(8,128)S(1)}, f32[4,408,128]{2,1,0:T(8,128)S(1)}, f32[4,408,128]{2,1,0:T(8,128)...) custom-call(f32[5,5]{1,0:T(8,128)S(1)} %copy-done.3, ...), custom_call_target="tpu_custom_call", output_to_operand_aliasing={{0}: (13, {})} | custom-call | tf_op jit(solution)/shard_map/stage_middle/pallas_call | solution.py:287
  86.8 10.4 %stage_last.1 = f32[1,5,16,32,512]{4,3,2,1,0:T(8,128)} custom-call(f32[5,5]{1,0:T(8,128)S(1)} %copy-done.3, s32[1]{0:T(128)} %bitcast.refs_1_, bf16[2,1536,256]{2,1,0:T(8,128)(2,1)S(1)} %pad_maximum_fusion.refs_2_, f32[1,5,16,32,512]{4,3,2,1,0:T(8,128)S(1)} %bitcast.22, f32[1,16,32,512]{3,2,1,0:T(8,128)S(1)} %copy-done.1, ...), custom_call_target="tpu_custom_call", output_to_operand_aliasing={{}: (12, {})} | custom-call | tf_op jit(solution)/shard_map/stage_last/pallas_call | solution.py:287
  (57 shorter events, 6.2 us)
Async XLA Ops:
  0.0 5.4 %copy-start.1 = (f32[1,16,32,512]{3,2,1,0:T(8,128)S(1)}, f32[1,16,32,512]{3,2,1,0:T(8,128)}, u32[]{:S(2)}) copy-start(f32[1,16,32,512]{3,2,1,0:T(8,128)} %refs_4_.7) | copy-start | bytes 3145732
  2.0 19.9 %collective-permute-start = (f32[1,2,5,32,512]{4,3,2,1,0:T(8,128)}, f32[1,2,5,32,512]{4,3,2,1,0:T(8,128)S(1)}, u32[]{:S(2)}, u32[]{:S(2)}) collective-permute-start(f32[1,2,5,32,512]{4,3,2,1,0:T(8,128)} %pack_first.1.first), channel_id=1, source_target_pairs={{4,0},{8,4},{12,8},{16,12},{20,16},{24,20},{28,24},{0,28},{5,1},{9... | collective-permute-start | bytes 1966088 | tf_op jit(solution)/shard_map/ppermute | solution.py:380
  13.7 6.9 %copy-start.13 = (f32[512,512]{1,0:T(8,128)S(1)}, f32[512,512]{1,0:T(8,128)}, u32[]{:S(2)}) copy-start(f32[512,512]{1,0:T(8,128)} %param.6) | copy-start | bytes 3145732
  13.7 7.4 %collective-permute-start.2 = (f32[2,32,512]{2,1,0:T(8,128)S(1)}, f32[2,32,512]{2,1,0:T(8,128)S(1)}, u32[]{:S(2)}, u32[]{:S(2)}) collective-permute-start(f32[2,32,512]{2,1,0:T(8,128)S(1)} %get-tuple-element.121), channel_id=1, source_target_pairs={{1,2},{2,1},{5,6},{6,5},{9,10},{10,9},{13,14},{14,13},{17,18},{18,... | collective-permute-start | bytes 393224 | tf_op jit(solution)/shard_map/ppermute | solution.py:327
  14.5 7.4 %collective-permute-start.1 = (f32[2,32,512]{2,1,0:T(8,128)S(1)}, f32[2,32,512]{2,1,0:T(8,128)S(1)}, u32[]{:S(2)}, u32[]{:S(2)}) collective-permute-start(f32[2,32,512]{2,1,0:T(8,128)S(1)} %get-tuple-element.122), channel_id=1, source_target_pairs={{0,1},{2,3},{1,0},{3,2},{4,5},{6,7},{5,4},{7,6},{8,9},{10,11},{9,8... | collective-permute-start | bytes 393224 | tf_op jit(solution)/shard_map/ppermute | solution.py:327
  19.0 8.5 %collective-permute-start.3 = (f32[1,2,5,32,512]{4,3,2,1,0:T(8,128)}, f32[1,2,5,32,512]{4,3,2,1,0:T(8,128)S(1)}, u32[]{:S(2)}, u32[]{:S(2)}) collective-permute-start(f32[1,2,5,32,512]{4,3,2,1,0:T(8,128)} %copy-done.12), channel_id=1, source_target_pairs={{4,0},{8,4},{12,8},{16,12},{20,16},{24,20},{28,24},{0,28},{5,1},{9... | collective-permute-start | bytes 1966088 | tf_op jit(solution)/shard_map/ppermute | solution.py:380
  19.1 36.6 %slice-start = ((s8[5242880]{0:T(1024)(128)(4,1)}), s8[4194304]{0:T(1024)(128)(4,1)S(1)}, s32[]{:S(2)}) async-start(s8[5242880]{0:T(1024)(128)(4,1)} %bitcast.21), calls=%async_computation | async-start | bytes 8388608
  20.8 34.9 %slice-start.1 = ((s8[5242880]{0:T(1024)(128)(4,1)}), s8[1048576]{0:T(1024)(128)(4,1)S(1)}, s32[]{:S(2)}) async-start(s8[5242880]{0:T(1024)(128)(4,1)} %bitcast.21), calls=%async_computation.1 | async-start | bytes 2097152
  21.1 14.4 %copy-start.9 = (f32[1,2,5,32,512]{4,3,2,1,0:T(8,128)S(1)}, f32[1,2,5,32,512]{4,3,2,1,0:T(8,128)}, u32[]{:S(2)}) copy-start(f32[1,2,5,32,512]{4,3,2,1,0:T(8,128)} %copy-done.8) | copy-start | bytes 1966084
  21.1 20.6 %copy-start.7 = (f32[1,2,5,32,512]{4,3,2,1,0:T(8,128)S(1)}, f32[1,2,5,32,512]{4,3,2,1,0:T(8,128)}, u32[]{:S(2)}) copy-start(f32[1,2,5,32,512]{4,3,2,1,0:T(8,128)} %copy-done.6) | copy-start | bytes 1966084
  22.1 19.6 %collective-permute-start.6 = (f32[1,2,5,32,512]{4,3,2,1,0:T(8,128)S(1)}, f32[1,2,5,32,512]{4,3,2,1,0:T(8,128)S(1)}, u32[]{:S(2)}, u32[]{:S(2)}) collective-permute-start(f32[1,2,5,32,512]{4,3,2,1,0:T(8,128)S(1)} %copy-done.11), channel_id=1, source_target_pairs={{4,0},{8,4},{12,8},{16,12},{20,16},{24,20},{28,24},{0,28},{5,1},{9... | collective-permute-start | bytes 1966088 | tf_op jit(solution)/shard_map/ppermute | solution.py:380
  22.8 32.4 %copy-start.5 = (f32[1,2,5,32,512]{4,3,2,1,0:T(8,128)S(1)}, f32[1,2,5,32,512]{4,3,2,1,0:T(8,128)}, u32[]{:S(2)}) copy-start(f32[1,2,5,32,512]{4,3,2,1,0:T(8,128)} %copy-done.4) | copy-start | bytes 1966084
  22.8 32.9 %copy-start.3 = (f32[5,5]{1,0:T(8,128)S(1)}, f32[5,5]{1,0:T(8,128)}, u32[]{:S(2)}) copy-start(f32[5,5]{1,0:T(8,128)} %refs_0_.7) | copy-start | bytes 304
  22.8 7.6 %collective-permute-start.5 = (f32[1,5,32,512]{3,2,1,0:T(8,128)S(1)}, f32[1,5,32,512]{3,2,1,0:T(8,128)S(1)}, u32[]{:S(2)}, u32[]{:S(2)}) collective-permute-start(f32[1,5,32,512]{3,2,1,0:T(8,128)S(1)} %get-tuple-element.115), channel_id=1, source_target_pairs={{1,2},{2,1},{5,6},{6,5},{9,10},{10,9},{13,14},{14,13},{17,18},{18,... | collective-permute-start | bytes 983048 | tf_op jit(solution)/shard_map/ppermute | solution.py:327
  23.6 11.8 %collective-permute-start.4 = (f32[1,5,32,512]{3,2,1,0:T(8,128)S(1)}, f32[1,5,32,512]{3,2,1,0:T(8,128)S(1)}, u32[]{:S(2)}, u32[]{:S(2)}) collective-permute-start(f32[1,5,32,512]{3,2,1,0:T(8,128)S(1)} %get-tuple-element.116), channel_id=1, source_target_pairs={{0,1},{2,3},{1,0},{3,2},{4,5},{6,7},{5,4},{7,6},{8,9},{10,11},{9,8... | collective-permute-start | bytes 983048 | tf_op jit(solution)/shard_map/ppermute | solution.py:327
  27.6 7.9 %collective-permute-start.8 = (f32[1,5,32,512]{3,2,1,0:T(8,128)S(1)}, f32[1,5,32,512]{3,2,1,0:T(8,128)S(1)}, u32[]{:S(2)}, u32[]{:S(2)}) collective-permute-start(f32[1,5,32,512]{3,2,1,0:T(8,128)S(1)} %get-tuple-element.113), channel_id=1, source_target_pairs={{1,2},{2,1},{5,6},{6,5},{9,10},{10,9},{13,14},{14,13},{17,18},{18,... | collective-permute-start | bytes 983048 | tf_op jit(solution)/shard_map/ppermute | solution.py:327
  28.3 13.5 %collective-permute-start.7 = (f32[1,5,32,512]{3,2,1,0:T(8,128)S(1)}, f32[1,5,32,512]{3,2,1,0:T(8,128)S(1)}, u32[]{:S(2)}, u32[]{:S(2)}) collective-permute-start(f32[1,5,32,512]{3,2,1,0:T(8,128)S(1)} %get-tuple-element.114), channel_id=1, source_target_pairs={{0,1},{2,3},{1,0},{3,2},{4,5},{6,7},{5,4},{7,6},{8,9},{10,11},{9,8... | collective-permute-start | bytes 983048 | tf_op jit(solution)/shard_map/ppermute | solution.py:327
  35.4 19.7 %collective-permute-start.9 = (f32[1,2,5,32,512]{4,3,2,1,0:T(8,128)S(1)}, f32[1,2,5,32,512]{4,3,2,1,0:T(8,128)S(1)}, u32[]{:S(2)}, u32[]{:S(2)}) collective-permute-start(f32[1,2,5,32,512]{4,3,2,1,0:T(8,128)S(1)} %copy-done.9), channel_id=1, source_target_pairs={{4,0},{8,4},{12,8},{16,12},{20,16},{24,20},{28,24},{0,28},{5,1},{9... | collective-permute-start | bytes 1966088 | tf_op jit(solution)/shard_map/ppermute | solution.py:380
  41.7 27.7 %collective-permute-start.12 = (f32[1,2,5,32,512]{4,3,2,1,0:T(8,128)S(1)}, f32[1,2,5,32,512]{4,3,2,1,0:T(8,128)S(1)}, u32[]{:S(2)}, u32[]{:S(2)}) collective-permute-start(f32[1,2,5,32,512]{4,3,2,1,0:T(8,128)S(1)} %copy-done.7), channel_id=1, source_target_pairs={{4,0},{8,4},{12,8},{16,12},{20,16},{24,20},{28,24},{0,28},{5,1},{9... | collective-permute-start | bytes 1966088 | tf_op jit(solution)/shard_map/ppermute | solution.py:380
  42.3 5.0 %collective-permute-start.11 = (f32[1,5,32,512]{3,2,1,0:T(8,128)S(1)}, f32[1,5,32,512]{3,2,1,0:T(8,128)S(1)}, u32[]{:S(2)}, u32[]{:S(2)}) collective-permute-start(f32[1,5,32,512]{3,2,1,0:T(8,128)S(1)} %get-tuple-element.111), channel_id=1, source_target_pairs={{1,2},{2,1},{5,6},{6,5},{9,10},{10,9},{13,14},{14,13},{17,18},{18,... | collective-permute-start | bytes 983048 | tf_op jit(solution)/shard_map/ppermute | solution.py:327
  43.0 12.2 %collective-permute-start.10 = (f32[1,5,32,512]{3,2,1,0:T(8,128)S(1)}, f32[1,5,32,512]{3,2,1,0:T(8,128)S(1)}, u32[]{:S(2)}, u32[]{:S(2)}) collective-permute-start(f32[1,5,32,512]{3,2,1,0:T(8,128)S(1)} %get-tuple-element.112), channel_id=1, source_target_pairs={{0,1},{2,3},{1,0},{3,2},{4,5},{6,7},{5,4},{7,6},{8,9},{10,11},{9,8... | collective-permute-start | bytes 983048 | tf_op jit(solution)/shard_map/ppermute | solution.py:327
  55.2 23.1 %collective-permute-start.14 = (f32[1,2,5,32,512]{4,3,2,1,0:T(8,128)S(1)}, f32[1,2,5,32,512]{4,3,2,1,0:T(8,128)S(1)}, u32[]{:S(2)}, u32[]{:S(2)}) collective-permute-start(f32[1,2,5,32,512]{4,3,2,1,0:T(8,128)S(1)} %copy-done.5), channel_id=1, source_target_pairs={{4,0},{8,4},{12,8},{16,12},{20,16},{24,20},{28,24},{0,28},{5,1},{9... | collective-permute-start | bytes 1966088 | tf_op jit(solution)/shard_map/ppermute | solution.py:380
  68.6 9.7 %collective-permute-start.15 = (f32[1,2,5,32,512]{4,3,2,1,0:T(8,128)S(1)}, f32[1,2,5,32,512]{4,3,2,1,0:T(8,128)S(1)}, u32[]{:S(2)}, u32[]{:S(2)}) collective-permute-start(f32[1,2,5,32,512]{4,3,2,1,0:T(8,128)S(1)} %get-tuple-element.96), channel_id=1, source_target_pairs={{4,0},{8,4},{12,8},{16,12},{20,16},{24,20},{28,24},{0,28},{5,1},{9... | collective-permute-start | bytes 1966088 | tf_op jit(solution)/shard_map/ppermute | solution.py:380
  78.0 8.8 %collective-permute-start.13 = (f32[1,2,5,32,512]{4,3,2,1,0:T(8,128)S(1)}, f32[1,2,5,32,512]{4,3,2,1,0:T(8,128)S(1)}, u32[]{:S(2)}, u32[]{:S(2)}) collective-permute-start(f32[1,2,5,32,512]{4,3,2,1,0:T(8,128)S(1)} %get-tuple-element.94), channel_id=1, source_target_pairs={{4,0},{8,4},{12,8},{16,12},{20,16},{24,20},{28,24},{0,28},{5,1},{9... | collective-permute-start | bytes 1966088 | tf_op jit(solution)/shard_map/ppermute | solution.py:380
  (8 other events, 8.9 us)

commit v3 on v2

--- a/solution.py
+++ b/solution.py
@@ -46,21 +46,42 @@
         one.wait()
 
 
-def pack_rest_kernel(planes, groups, source, sensor, first, *results):
+def pack_rest_kernel(planes, groups, source, sensor, first, *refs):
     del first
+    *results, held, edges, sems = refs
+    plan = []
     depth = groups[0]
     for result, count in zip(results, groups[1:]):
         for k in range(count):
-            for s, plane in enumerate((depth + k, planes - 1 - depth - k)):
-
-                def field(f, result=result, k=k, s=s, plane=plane):
-                    result[k, s, f] = source[0, f, plane]
-
-                pl.loop(0, source.shape[1])(field)
+            place = held.at[depth - groups[0] + k]
+            plan.append(
+                ([(source.at[0, :, depth + k], place.at[0]), (source.at[0, :, planes - 1 - depth - k], place.at[1])],
+                 place, result.at[k])
+            )
         depth += count
-    for k in range(STEPS - 1):
-        for s, plane in enumerate((k, planes - 1 - k)):
-            results[-1][k, s] = sensor[0, plane]
+    ends = [
+        (sensor.at[0, plane], edges.at[k, s])
+        for k in range(STEPS - 1)
+        for s, plane in enumerate((k, planes - 1 - k))
+    ]
+    plan.append((ends, edges, results[-1]))
+    count = 0
+
+    def start(source, target):
+        nonlocal count
+        made = pltpu.make_async_copy(source, target, sems.at[count])
+        count += 1
+        made.start()
+        return made
+
+    inward = [[start(*pair) for pair in pairs] for pairs, _, _ in plan]
+    outward = []
+    for made, (_, place, result) in zip(inward, plan):
+        for one in made:
+            one.wait()
+        outward.append(start(place, result))
+    for one in outward:
+        one.wait()
 
 
 def stage_kernel(stage, fields, planes, groups, *refs):
@@ -74,7 +95,6 @@
     (coupling, odd_ref, weights, own, sensor) = take(5)
     chunks = take(len(groups))
     halos = take(2 * STEPS) if stage.first else []
-    sensor_halos = take(2) if stage.first else []
     filtered = dict(zip(stage.taken, take(len(stage.taken))))
     if not stage.first:
         take(1)
@@ -91,7 +111,7 @@
     nth, nr = own.shape[-2:]
     blocks = nr // LANES
     stride = nth + PAD
-    odd = odd_ref[0]
+    odd, base = odd_ref[0], odd_ref[1]
 
     blank = jnp.zeros((PAD, LANES), jnp.float32)
     for ref in fresh.values():
@@ -119,7 +139,7 @@
     def split_raw(q, place, t):
         for s in range(2):
             if q < 0:
-                source = halos[2 * (-1 - q) + s].at[0]
+                source = halos[2 * (-1 - q) + s]
                 side = 1 - odd if s == 0 else odd
             else:
                 chunk, k = starts[q]
@@ -131,7 +151,7 @@
     def sensor_at(q, s, t, b):
         if q >= 0:
             return sensor[0, planes - 1 - q if s else q, pl.ds(t, ROWS), columns(b)]
-        pair = [ref[-1 - q, pl.ds(t, ROWS), columns(b)] for ref in sensor_halos]
+        pair = [ref[fields, pl.ds(t, ROWS), columns(b)] for ref in halos[2 * (-1 - q) : 2 * (-q)]]
         return jnp.where(odd == s, pair[1], pair[0])
 
     def advance(level, q, place, t):
@@ -154,7 +174,7 @@
                     left = pltpu.roll(jnp.where(at_end, lower, middle), 1, 1)
                     right = pltpu.roll(jnp.where(at_start, upper, middle), LANES - 1, 1)
                     axial = before[b, aligned[f]] + after[b, beyond[f]]
-                    around = here[b, pl.ds(rows[f] - 1, ROWS)] + here[b, pl.ds(rows[f] + 1, ROWS)]
+                    around = here[b, pl.ds(base + (rows[f] - 1), ROWS)] + here[b, pl.ds(base + (rows[f] + 1), ROWS)]
                     laps.append((axial + around) + (left + right) - 6.0 * middle)
                 sens = sensor_at(q, s, t, b)
                 for f in range(fields):
@@ -176,33 +196,26 @@
             starts[depth] = (i, k)
             depth += 1
     out_low = stage.todo[STEPS + 1][0]
-    parts = nth // ROWS
-    width = weights.shape[-1]
-
-    def project(level, q, place, j):
+
+    def project(level, q, place):
         ref = filtered[level, q]
         high = highs[place][...]
         left = jnp.concatenate([high, lows[place][...], high], axis=1)
-        product = jnp.dot(left, weights[j], preferred_element_type=jnp.float32)
+        product = jnp.dot(left, weights[...], preferred_element_type=jnp.float32)
         for i in range(sides):
-            for b in range(width // LANES):
-                ref[j * (width // LANES) + b, i * stride + PAD : (i + 1) * stride] = product[
-                    i * nth : (i + 1) * nth, columns(b)
-                ]
+            for b in range(blocks):
+                ref[b, i * stride + PAD : (i + 1) * stride] = product[i * nth : (i + 1) * nth, columns(b)]
 
     def together(task, held):
-        def part(j):
-            if held is not None:
-                project(*held, j)
-            if task is not None:
-                level, q, place = task
-                t = pl.multiple_of(j * ROWS, ROWS)
+        if held is not None:
+            project(*held)
+        if task is not None:
+            level, q, place = task
+            for t in range(0, nth, ROWS):
                 if level == 1:
                     split_raw(q, place, t)
                 else:
                     advance(level, q, place, t)
-
-        pl.loop(0, parts)(part)
 
     held = None
     sent = []
@@ -251,28 +264,33 @@
 
 def pack_rest(adjoint_in, sensor, first, groups):
     fields, planes, nth, nr = adjoint_in.shape[1:]
-    shapes = [(count, 2, fields, nth, nr) for count in groups[1:]] + [(STEPS - 1, 2, nth, nr)]
+    depths = sum(groups[1:])
+    edges = (STEPS - 1, 2, nth, nr)
+    shapes = [(count, 2, fields, nth, nr) for count in groups[1:]] + [edges]
     out_shape = [jax.ShapeDtypeStruct(shape, jnp.float32) for shape in shapes]
     return pl.pallas_call(
         functools.partial(pack_rest_kernel, planes, groups),
         out_shape=out_shape,
-        in_specs=[CLOSE, CLOSE, ANYWHERE],
-        out_specs=[CLOSE] * len(shapes),
+        in_specs=[ANYWHERE] * 3,
+        out_specs=[ANYWHERE] * len(shapes),
+        scratch_shapes=[
+            pltpu.VMEM((depths, 2, fields, nth, nr), jnp.float32),
+            pltpu.VMEM(edges, jnp.float32),
+            pltpu.SemaphoreType.DMA((3 * depths + 2 * STEPS,)),
+        ],
         cost_estimate=pl.CostEstimate(flops=0, bytes_accessed=2 * size(*out_shape), transcendentals=0),
-        compiler_params=pltpu.CompilerParams(
-            vmem_limit_bytes=VMEM_SPARE + size(adjoint_in, sensor, *out_shape)
-        ),
+        compiler_params=pltpu.CompilerParams(vmem_limit_bytes=VMEM_MOST),
         name="pack_rest",
     )(adjoint_in, sensor, first)
 
 
-def run_stage(stage, groups, coupling, odd, weights, own, sensor, chunks, halos, sensor_halos, carried, out):
+def run_stage(stage, groups, coupling, odd, weights, own, sensor, chunks, halos, carried, out):
     fields, planes, nth, nr = own.shape[1:]
     sides = 2 * fields
     slot = (nr // LANES, sides * (nth + PAD) + PAD, LANES)
     close = [weights, own, sensor, *chunks]
     if stage.first:
-        close += [*halos, *sensor_halos]
+        close += halos
     close += [carried[key] for key in stage.taken]
     operands = [coupling, odd, *close] + ([] if stage.first else [out])
     in_specs = [SCALARS] * 2 + [CLOSE] * len(close) + ([] if stage.first else [ANYWHERE])
@@ -323,19 +341,14 @@
         for parity in range(2):
             pairs = [(i, i + 1) for i in range(parity, slabs - 1, 2)]
             side = 1 - odd if parity == 0 else odd
-            mine = lax.dynamic_index_in_dim(edges, side, 1, keepdims=False)
+            mine = jnp.concatenate([lax.dynamic_index_in_dim(part, side, 0, keepdims=False) for part in edges])
             result.append(lax.ppermute(mine, "gx", pairs + [(j, i) for i, j in pairs]))
         return result
 
     high = lax.reduce_precision(filter_matrix, 8, 7)
     low = filter_matrix - high
-    parts = nth // ROWS
-    weights = [
-        jnp.concatenate([high[:, at], high[:, at], low[:, at]], axis=0)
-        for at in (slice(j * (nr // parts), (j + 1) * (nr // parts)) for j in range(parts))
-    ]
-    weights = jnp.stack(weights).astype(jnp.bfloat16)
-    scalar = odd.astype(jnp.int32)[None]
+    weights = jnp.concatenate([high, high, low], axis=0).astype(jnp.bfloat16)
+    scalar = jnp.stack([odd, 0 * odd]).astype(jnp.int32)
 
     stages = [(0, STEPS)]
     while stages[-1][1] < len(groups):
@@ -343,7 +356,7 @@
         stages.append((low_cut, max(min(low_cut + TOGETHER, len(groups) - 1), low_cut + 1)))
     cuts = [sum(groups[:i]) for i in range(len(groups) + 1)]
     carried, out = {}, None
-    halos, sensor_halos = [], []
+    halos = []
 
     def run(number):
         nonlocal out
@@ -352,7 +365,7 @@
         stage = Stage(cuts[low_cut] if number else -STEPS, cuts[high_cut], half)
         out, fresh = run_stage(
             stage, mine, coupling, scalar, weights, adjoint_in, sensor,
-            chunks[low_cut:high_cut], halos, sensor_halos, carried, out,
+            chunks[low_cut:high_cut], halos, carried, out,
         )
         carried.update(fresh)
 
@@ -360,9 +373,8 @@
     ran = 0
 
     def unpack():
-        nonlocal sensor_halos, halos
-        sensor_halos, *halos = exchanged
-        halos = sum(halos, [])
+        nonlocal halos
+        halos = sum(exchanged, [])
 
     for i, packed in enumerate([first_chunk, *rest]):
         if i >= STEPS + 3 and stages[ran][1] < i:
@@ -373,15 +385,14 @@
             key = max(carried)
             packed, carried[key] = lax.optimization_barrier((packed, carried[key]))
         elif i > 1:
-            ends = exchanged[i - 2] if i - 2 < len(exchanged) else []
+            ends = exchanged[i - STEPS] if STEPS <= i < len(exchanged) + STEPS else []
             packed, weights, chunks[i - 2], *ends = lax.optimization_barrier((packed, weights, chunks[i - 2], *ends))
             if ends:
-                exchanged[i - 2] = ends
+                exchanged[i - STEPS] = ends
         chunks.append(lax.ppermute(packed, "seg", back))
-        if i == 0:
-            exchanged.append(swapped(sensor_edges))
-        elif i <= STEPS:
-            exchanged.append(swapped(chunks[i - 1][:1]))
+        if 1 <= i <= STEPS:
+            edges = [chunks[i - 1][0]] + ([sensor_edges[i - 1][:, None]] if i < STEPS else [])
+            exchanged.append(swapped(edges))
     for number in range(ran, len(stages)):
         if number == 0:
             unpack()

time: 98.4 us -> 90.7 us (0.922)
  local copies, waits for them, and re-layouts: 8.17 us -> 2.76 us
  waiting for transfers between devices: 20.6 us -> 17 us
  starting transfers between devices: 23.6 us -> 25.4 us
  Pallas kernels: 42.8 us -> 44.4 us
  other arithmetic: 1.84 us -> 0.46 us
    unnamed x32 -> x22, local copies, waits for them, and re-layouts: 7.95 us -> 0.05 us
    ppermute x8 -> x6, waiting for transfers between devices: 20 us -> 14.4 us  [swapped(): result.append(lax.ppermute(mine, 'gx', pairs + [(j, i) for i, j in pairs]))]
    ppermute x8, starting transfers between devices: 6.36 us -> 11.7 us  [shards(): chunks.append(lax.ppermute(packed, 'seg', back))]
    pallas_call x1, Pallas kernels: 0.48 us -> 4.26 us  [pack_rest(): pl.pallas_call(functools.partial(pack_rest_kernel, planes, groups), out_s...]
    ppermute x8 -> x6, starting transfers between devices: 17.2 us -> 13.7 us  [swapped(): result.append(lax.ppermute(mine, 'gx', pairs + [(j, i) for i, j in pairs]))]
    pallas_call x4, Pallas kernels: 40.3 us -> 38.2 us  [run_stage(): pl.pallas_call(functools.partial(stage_kernel, stage, fields, planes, gro...]
    ppermute x8, waiting for transfers between devices: 0.62 us -> 2.57 us  [shards(): chunks.append(lax.ppermute(packed, 'seg', back))]
    slice x2 -> x1, local copies, waits for them, and re-layouts: 0.07 us -> 1.65 us  [shards(): sensor_edges[i - 1][:, None]]
  transfers between devices with their start and end apart: 16 -> 14, of which waited for: 5 -> 5; matrix products, arithmetic and copies ran while one was open for 2% -> 3% of each run, Pallas kernels for 31% -> 36%
where the time goes in v3:
time: 90.7 us; the launch traced here: 90.5 us
  Pallas kernels  44.4 us (49%)
  starting transfers between devices  25.4 us (28%)
  waiting for transfers between devices  17 us (19%)
  local copies, waits for them, and re-layouts  2.76 us (3%)
    pallas_call x4, Pallas kernels, run_stage(): pl.pallas_call(functools.partial(stage_kernel, stage, fields, planes, gro...  38.2 us
    ppermute x6, waiting for transfers between devices, swapped(): result.append(lax.ppermute(mine, 'gx', pairs + [(j, i) for i, j in pairs]))  14.4 us
    ppermute x6, starting transfers between devices, swapped(): result.append(lax.ppermute(mine, 'gx', pairs + [(j, i) for i, j in pairs]))  13.7 us
    ppermute x8, starting transfers between devices, shards(): chunks.append(lax.ppermute(packed, 'seg', back))  11.7 us
    pallas_call x1, Pallas kernels, pack_rest(): pl.pallas_call(functools.partial(pack_rest_kernel, planes, groups), out_s...  4.26 us
    ppermute x8, waiting for transfers between devices, shards(): chunks.append(lax.ppermute(packed, 'seg', back))  2.57 us
    pallas_call x1, Pallas kernels, pack_first(): pl.pallas_call(functools.partial(pack_first_kernel, planes), out_shape=ja...  1.92 us
  transfers between devices with their start and end apart: 14, of which 5 were waited for; matrix products, arithmetic and copies ran while one was open for 3% of the time, Pallas kernels for 36%

profile of v3, /device:TPU:0, one launch (start us, length us, event | category | flops | bytes accessed | tf_op | source)
XLA Modules:
  0.0 90.5 jit_solution(13840923360733463176)
XLA Ops:
  0.0 1.9 %pack_first.1.first = f32[1,2,5,32,512]{4,3,2,1,0:T(8,128)} custom-call(f32[1,5,16,32,512]{4,3,2,1,0:T(8,128)} %refs_3_.7), custom_call_target="tpu_custom_call" | custom-call | tf_op jit(solution)/shard_map/pack_first/pallas_call | solution.py:254
  1.9 3.4 %collective-permute-start = (f32[1,2,5,32,512]{4,3,2,1,0:T(8,128)}, f32[1,2,5,32,512]{4,3,2,1,0:T(8,128)S(1)}, u32[]{:S(2)}, u32[]{:S(2)}) collective-permute-start(f32[1,2,5,32,512]{4,3,2,1,0:T(8,128)} %pack_first.1.first), channel_id=1, source_target_pairs={{4,0},{8,4},{12,8},{16,12},{20,16},{24,20},{28,24},{0,28},{5,1},{9... | collective-permute-start | bytes 1966088 | tf_op jit(solution)/shard_map/ppermute | solution.py:392
  5.3 4.3 %pack_rest.1 = (f32[1,2,5,32,512]{4,3,2,1,0:T(8,128)}, f32[1,2,5,32,512]{4,3,2,1,0:T(8,128)}, f32[1,2,5,32,512]{4,3,2,1,0:T(8,128)}, f32[1,2,5,32,512]{4,3,2,1,0...) custom-call(f32[1,5,16,32,512]{4,3,2,1,0:T(8,128)} %refs_3_.7, ...), custom_call_target="tpu_custom_call" | custom-call | bytes 9699328 | tf_op jit(solution)/shard_map/pack_rest/pallas_call | solution.py:271
  9.6 0.7 collective-permute-start.1
  10.3 1.6 %fusion.1 = (f32[1,2,32,512]{3,2,1,0:T(8,128)}, f32[1,2,32,512]{3,2,1,0:T(8,128)S(1)}) fusion(f32[2,2,32,512]{3,2,1,0:T(8,128)} %get-tuple-element.62), kind=kLoop, calls=%fused_computation.19 | loop fusion | bytes 524288 | tf_op jit(solution)/shard_map/slice | solution.py:394
  12.0 0.9 dynamic-slice_bitcast_fusion.6
  13.9 1.6 %collective-permute-start.2 = (f32[6,32,512]{2,1,0:T(8,128)S(1)}, f32[6,32,512]{2,1,0:T(8,128)S(1)}, u32[]{:S(2)}, u32[]{:S(2)}) collective-permute-start(f32[6,32,512]{2,1,0:T(8,128)S(1)} %pad_maximum_fusion.1), channel_id=1, source_target_pairs={{0,1},{2,3},{1,0},{3,2},{4,5},{6,7},{5,4},{7,6},{8,9},{10,11},{9,8... | collective-permute-start | bytes 1179656 | tf_op jit(solution)/shard_map/ppermute | solution.py:345
  15.6 0.7 collective-permute-start.3
  16.3 2.5 %collective-permute-start.4 = (f32[1,2,5,32,512]{4,3,2,1,0:T(8,128)S(1)}, f32[1,2,5,32,512]{4,3,2,1,0:T(8,128)S(1)}, u32[]{:S(2)}, u32[]{:S(2)}) collective-permute-start(f32[1,2,5,32,512]{4,3,2,1,0:T(8,128)S(1)} %copy-done.8), channel_id=1, source_target_pairs={{4,0},{8,4},{12,8},{16,12},{20,16},{24,20},{28,24},{0,28},{5,1},{9... | collective-permute-start | bytes 1966088 | tf_op jit(solution)/shard_map/ppermute | solution.py:392
  18.7 2.0 %collective-permute-done.1.refs_6_ = f32[1,2,5,32,512]{4,3,2,1,0:T(8,128)S(1)} collective-permute-done((f32[1,2,5,32,512]{4,3,2,1,0:T(8,128)}, f32[1,2,5,32,512]{4,3,2,1,0:T(8,128)S(1)}, u32[]{:S(2)}, u32[]{:S(2)}) %collective-permute-start.1) | collective-permute-done | bytes 655392 | tf_op jit(solution)/shard_map/ppermute | solution.py:392
  20.9 2.1 %collective-permute-start.5 = (f32[6,32,512]{2,1,0:T(8,128)S(1)}, f32[6,32,512]{2,1,0:T(8,128)S(1)}, u32[]{:S(2)}, u32[]{:S(2)}) collective-permute-start(f32[6,32,512]{2,1,0:T(8,128)S(1)} %pad_maximum_fusion.3), channel_id=1, source_target_pairs={{0,1},{2,3},{1,0},{3,2},{4,5},{6,7},{5,4},{7,6},{8,9},{10,11},{9,8... | collective-permute-start | bytes 1179656 | tf_op jit(solution)/shard_map/ppermute | solution.py:345
  23.0 0.7 collective-permute-start.6
  23.7 2.1 %collective-permute-done.2.refs_8_ = f32[6,32,512]{2,1,0:T(8,128)S(1)} collective-permute-done((f32[6,32,512]{2,1,0:T(8,128)S(1)}, f32[6,32,512]{2,1,0:T(8,128)S(1)}, u32[]{:S(2)}, u32[]{:S(2)}) %collective-permute-start.2) | collective-permute-done | bytes 393248 | tf_op jit(solution)/shard_map/ppermute | solution.py:345
  25.8 1.8 %collective-permute-start.7 = (f32[1,2,5,32,512]{4,3,2,1,0:T(8,128)S(1)}, f32[1,2,5,32,512]{4,3,2,1,0:T(8,128)S(1)}, u32[]{:S(2)}, u32[]{:S(2)}) collective-permute-start(f32[1,2,5,32,512]{4,3,2,1,0:T(8,128)S(1)} %copy-done.7), channel_id=1, source_target_pairs={{4,0},{8,4},{12,8},{16,12},{20,16},{24,20},{28,24},{0,28},{5,1},{9... | collective-permute-start | bytes 1966088 | tf_op jit(solution)/shard_map/ppermute | solution.py:392
  27.6 5.6 %collective-permute-done.5.refs_10_ = f32[6,32,512]{2,1,0:T(8,128)S(1)} collective-permute-done((f32[6,32,512]{2,1,0:T(8,128)S(1)}, f32[6,32,512]{2,1,0:T(8,128)S(1)}, u32[]{:S(2)}, u32[]{:S(2)}) %collective-permute-start.5) | collective-permute-done | bytes 393248 | tf_op jit(solution)/shard_map/ppermute | solution.py:345
  33.2 1.2 %collective-permute-start.10 = (f32[1,2,5,32,512]{4,3,2,1,0:T(8,128)S(1)}, f32[1,2,5,32,512]{4,3,2,1,0:T(8,128)S(1)}, u32[]{:S(2)}, u32[]{:S(2)}) collective-permute-start(f32[1,2,5,32,512]{4,3,2,1,0:T(8,128)S(1)} %copy-done.6), channel_id=1, source_target_pairs={{4,0},{8,4},{12,8},{16,12},{20,16},{24,20},{28,24},{0,28},{5,1},{9... | collective-permute-start | bytes 1966088 | tf_op jit(solution)/shard_map/ppermute | solution.py:392
  34.5 0.7 collective-permute-start.9
  35.2 7.9 %collective-permute-start.8 = (f32[5,32,512]{2,1,0:T(8,128)S(1)}, f32[5,32,512]{2,1,0:T(8,128)S(1)}, u32[]{:S(2)}, u32[]{:S(2)}) collective-permute-start(f32[5,32,512]{2,1,0:T(8,128)S(1)} %get-tuple-element.110), channel_id=1, source_target_pairs={{0,1},{2,3},{1,0},{3,2},{4,5},{6,7},{5,4},{7,6},{8,9},{10,11},{9,8... | collective-permute-start | bytes 983048 | tf_op jit(solution)/shard_map/ppermute | solution.py:345
  43.1 6.7 %collective-permute-done.8.refs_12_ = f32[5,32,512]{2,1,0:T(8,128)S(1)} collective-permute-done((f32[5,32,512]{2,1,0:T(8,128)S(1)}, f32[5,32,512]{2,1,0:T(8,128)S(1)}, u32[]{:S(2)}, u32[]{:S(2)}) %collective-permute-start.8) | collective-permute-done | bytes 327712 | tf_op jit(solution)/shard_map/ppermute | solution.py:345
  50.0 11.6 %stage_first.1 = (f32[1,5,16,32,512]{4,3,2,1,0:T(8,128)}, f32[4,408,128]{2,1,0:T(8,128)S(1)}, f32[4,408,128]{2,1,0:T(8,128)S(1)}, f32[4,408,128]{2,1,0:T(8,128)S...) custom-call(f32[5,5]{1,0:T(8,128)S(1)} %copy-done.1, ...), custom_call_target="tpu_custom_call" | custom-call | bytes 17072128 | tf_op jit(solution)/shard_map/stage_first/pallas_call | solution.py:305
  61.6 1.5 %collective-permute-start.13 = (f32[1,2,5,32,512]{4,3,2,1,0:T(8,128)S(1)}, f32[1,2,5,32,512]{4,3,2,1,0:T(8,128)S(1)}, u32[]{:S(2)}, u32[]{:S(2)}) collective-permute-start(f32[1,2,5,32,512]{4,3,2,1,0:T(8,128)S(1)} %copy-done.4), channel_id=1, source_target_pairs={{4,0},{8,4},{12,8},{16,12},{20,16},{24,20},{28,24},{0,28},{5,1},{9... | collective-permute-start | bytes 1966088 | tf_op jit(solution)/shard_map/ppermute | solution.py:392
  63.1 8.5 %stage_middle.2 = (f32[1,5,16,32,512]{4,3,2,1,0:T(8,128)}, f32[4,408,128]{2,1,0:T(8,128)S(1)}, f32[4,408,128]{2,1,0:T(8,128)S(1)}, f32[4,408,128]{2,1,0:T(8,128)...) custom-call(f32[5,5]{1,0:T(8,128)S(1)} %copy-done.1, ...), custom_call_target="tpu_custom_call", output_to_operand_aliasing={{0}: (13, {})} | custom-call | tf_op jit(solution)/shard_map/stage_middle/pallas_call | solution.py:305
  72.1 8.5 %stage_middle.3 = (f32[1,5,16,32,512]{4,3,2,1,0:T(8,128)}, f32[4,408,128]{2,1,0:T(8,128)S(1)}, f32[4,408,128]{2,1,0:T(8,128)S(1)}, f32[4,408,128]{2,1,0:T(8,128)...) custom-call(f32[5,5]{1,0:T(8,128)S(1)} %copy-done.1, ...), custom_call_target="tpu_custom_call", output_to_operand_aliasing={{0}: (13, {})} | custom-call | tf_op jit(solution)/shard_map/stage_middle/pallas_call | solution.py:305
  80.6 9.6 %stage_last.1 = f32[1,5,16,32,512]{4,3,2,1,0:T(8,128)} custom-call(f32[5,5]{1,0:T(8,128)S(1)} %copy-done.1, s32[2]{0:T(128)S(1)} %pad_add_fusion.refs_1_, bf16[1536,512]{1,0:T(8,128)(2,1)S(1)} %pad_maximum_fusion.refs_2_, f32[1,5,16,32,512]{4,3,2,1,0:T(8,128)S(1)} %bitcast.22, f32[1,16,32,512]{3,2,1,0:T(8,128)S(1)} %copy-done, ...), custom_call_target="tpu_custom_call", output_to_operand_aliasing={{}: (12, {})} | custom-call | tf_op jit(solution)/shard_map/stage_last/pallas_call | solution.py:305
  (46 shorter events, 1.8 us)
Async XLA Ops:
  1.9 10.9 %copy-start.2 = (f32[512,512]{1,0:T(8,128)S(1)}, f32[512,512]{1,0:T(8,128)}, u32[]{:S(2)}) copy-start(f32[512,512]{1,0:T(8,128)} %param.6) | copy-start | bytes 3145732
  1.9 11.8 %collective-permute-start = (f32[1,2,5,32,512]{4,3,2,1,0:T(8,128)}, f32[1,2,5,32,512]{4,3,2,1,0:T(8,128)S(1)}, u32[]{:S(2)}, u32[]{:S(2)}) collective-permute-start(f32[1,2,5,32,512]{4,3,2,1,0:T(8,128)} %pack_first.1.first), channel_id=1, source_target_pairs={{4,0},{8,4},{12,8},{16,12},{20,16},{24,20},{28,24},{0,28},{5,1},{9... | collective-permute-start | bytes 1966088 | tf_op jit(solution)/shard_map/ppermute | solution.py:392
  5.3 44.6 %slice-start = ((s8[5242880]{0:T(1024)(128)(4,1)}), s8[1048576]{0:T(1024)(128)(4,1)S(1)}, s32[]{:S(2)}) async-start(s8[5242880]{0:T(1024)(128)(4,1)} %bitcast.21), calls=%async_computation | async-start | bytes 2097152
  9.6 11.2 %collective-permute-start.1 = (f32[1,2,5,32,512]{4,3,2,1,0:T(8,128)}, f32[1,2,5,32,512]{4,3,2,1,0:T(8,128)S(1)}, u32[]{:S(2)}, u32[]{:S(2)}) collective-permute-start(f32[1,2,5,32,512]{4,3,2,1,0:T(8,128)} %get-tuple-element.61), channel_id=1, source_target_pairs={{4,0},{8,4},{12,8},{16,12},{20,16},{24,20},{28,24},{0,28},{5,1},{9... | collective-permute-start | bytes 1966088 | tf_op jit(solution)/shard_map/ppermute | solution.py:392
  13.0 36.9 %slice-start.1 = ((s8[5242880]{0:T(1024)(128)(4,1)}), s8[4194304]{0:T(1024)(128)(4,1)S(1)}, s32[]{:S(2)}) async-start(s8[5242880]{0:T(1024)(128)(4,1)} %bitcast.21), calls=%async_computation.1 | async-start | bytes 8388608
  13.2 12.6 %copy-start.7 = (f32[1,2,5,32,512]{4,3,2,1,0:T(8,128)S(1)}, f32[1,2,5,32,512]{4,3,2,1,0:T(8,128)}, u32[]{:S(2)}) copy-start(f32[1,2,5,32,512]{4,3,2,1,0:T(8,128)} %get-tuple-element.66) | copy-start | bytes 1966084
  13.2 20.0 %copy-start.6 = (f32[1,2,5,32,512]{4,3,2,1,0:T(8,128)S(1)}, f32[1,2,5,32,512]{4,3,2,1,0:T(8,128)}, u32[]{:S(2)}) copy-start(f32[1,2,5,32,512]{4,3,2,1,0:T(8,128)} %get-tuple-element.70) | copy-start | bytes 1966084
  13.8 36.0 %copy-start.5 = (f32[1,2,5,32,512]{4,3,2,1,0:T(8,128)S(1)}, f32[1,2,5,32,512]{4,3,2,1,0:T(8,128)}, u32[]{:S(2)}) copy-start(f32[1,2,5,32,512]{4,3,2,1,0:T(8,128)} %get-tuple-element.91) | copy-start | bytes 1966084
  13.8 36.1 %copy-start = (f32[1,16,32,512]{3,2,1,0:T(8,128)S(1)}, f32[1,16,32,512]{3,2,1,0:T(8,128)}, u32[]{:S(2)}) copy-start(f32[1,16,32,512]{3,2,1,0:T(8,128)} %refs_4_.7) | copy-start | bytes 3145732
  13.8 36.1 %copy-start.1 = (f32[5,5]{1,0:T(8,128)S(1)}, f32[5,5]{1,0:T(8,128)}, u32[]{:S(2)}) copy-start(f32[5,5]{1,0:T(8,128)} %refs_0_.7) | copy-start | bytes 304
  13.9 12.0 %collective-permute-start.2 = (f32[6,32,512]{2,1,0:T(8,128)S(1)}, f32[6,32,512]{2,1,0:T(8,128)S(1)}, u32[]{:S(2)}, u32[]{:S(2)}) collective-permute-start(f32[6,32,512]{2,1,0:T(8,128)S(1)} %pad_maximum_fusion.1), channel_id=1, source_target_pairs={{0,1},{2,3},{1,0},{3,2},{4,5},{6,7},{5,4},{7,6},{8,9},{10,11},{9,8... | collective-permute-start | bytes 1179656 | tf_op jit(solution)/shard_map/ppermute | solution.py:345
  15.6 10.3 %collective-permute-start.3 = (f32[6,32,512]{2,1,0:T(8,128)S(1)}, f32[6,32,512]{2,1,0:T(8,128)S(1)}, u32[]{:S(2)}, u32[]{:S(2)}) collective-permute-start(f32[6,32,512]{2,1,0:T(8,128)S(1)} %pad_maximum_fusion.2), channel_id=1, source_target_pairs={{1,2},{2,1},{5,6},{6,5},{9,10},{10,9},{13,14},{14,13},{17,18},{18,... | collective-permute-start | bytes 1179656 | tf_op jit(solution)/shard_map/ppermute | solution.py:345
  16.3 16.9 %collective-permute-start.4 = (f32[1,2,5,32,512]{4,3,2,1,0:T(8,128)S(1)}, f32[1,2,5,32,512]{4,3,2,1,0:T(8,128)S(1)}, u32[]{:S(2)}, u32[]{:S(2)}) collective-permute-start(f32[1,2,5,32,512]{4,3,2,1,0:T(8,128)S(1)} %copy-done.8), channel_id=1, source_target_pairs={{4,0},{8,4},{12,8},{16,12},{20,16},{24,20},{28,24},{0,28},{5,1},{9... | collective-permute-start | bytes 1966088 | tf_op jit(solution)/shard_map/ppermute | solution.py:392
  20.9 12.3 %collective-permute-start.5 = (f32[6,32,512]{2,1,0:T(8,128)S(1)}, f32[6,32,512]{2,1,0:T(8,128)S(1)}, u32[]{:S(2)}, u32[]{:S(2)}) collective-permute-start(f32[6,32,512]{2,1,0:T(8,128)S(1)} %pad_maximum_fusion.3), channel_id=1, source_target_pairs={{0,1},{2,3},{1,0},{3,2},{4,5},{6,7},{5,4},{7,6},{8,9},{10,11},{9,8... | collective-permute-start | bytes 1179656 | tf_op jit(solution)/shard_map/ppermute | solution.py:345
  23.0 10.2 %collective-permute-start.6 = (f32[6,32,512]{2,1,0:T(8,128)S(1)}, f32[6,32,512]{2,1,0:T(8,128)S(1)}, u32[]{:S(2)}, u32[]{:S(2)}) collective-permute-start(f32[6,32,512]{2,1,0:T(8,128)S(1)} %pad_maximum_fusion.4), channel_id=1, source_target_pairs={{1,2},{2,1},{5,6},{6,5},{9,10},{10,9},{13,14},{14,13},{17,18},{18,... | collective-permute-start | bytes 1179656 | tf_op jit(solution)/shard_map/ppermute | solution.py:345
  25.8 24.0 %collective-permute-start.7 = (f32[1,2,5,32,512]{4,3,2,1,0:T(8,128)S(1)}, f32[1,2,5,32,512]{4,3,2,1,0:T(8,128)S(1)}, u32[]{:S(2)}, u32[]{:S(2)}) collective-permute-start(f32[1,2,5,32,512]{4,3,2,1,0:T(8,128)S(1)} %copy-done.7), channel_id=1, source_target_pairs={{4,0},{8,4},{12,8},{16,12},{20,16},{24,20},{28,24},{0,28},{5,1},{9... | collective-permute-start | bytes 1966088 | tf_op jit(solution)/shard_map/ppermute | solution.py:392
  33.2 29.9 %collective-permute-start.10 = (f32[1,2,5,32,512]{4,3,2,1,0:T(8,128)S(1)}, f32[1,2,5,32,512]{4,3,2,1,0:T(8,128)S(1)}, u32[]{:S(2)}, u32[]{:S(2)}) collective-permute-start(f32[1,2,5,32,512]{4,3,2,1,0:T(8,128)S(1)} %copy-done.6), channel_id=1, source_target_pairs={{4,0},{8,4},{12,8},{16,12},{20,16},{24,20},{28,24},{0,28},{5,1},{9... | collective-permute-start | bytes 1966088 | tf_op jit(solution)/shard_map/ppermute | solution.py:392
  34.5 8.7 %collective-permute-start.9 = (f32[5,32,512]{2,1,0:T(8,128)S(1)}, f32[5,32,512]{2,1,0:T(8,128)S(1)}, u32[]{:S(2)}, u32[]{:S(2)}) collective-permute-start(f32[5,32,512]{2,1,0:T(8,128)S(1)} %get-tuple-element.109), channel_id=1, source_target_pairs={{1,2},{2,1},{5,6},{6,5},{9,10},{10,9},{13,14},{14,13},{17,18},{18,... | collective-permute-start | bytes 983048 | tf_op jit(solution)/shard_map/ppermute | solution.py:345
  35.2 14.7 %collective-permute-start.8 = (f32[5,32,512]{2,1,0:T(8,128)S(1)}, f32[5,32,512]{2,1,0:T(8,128)S(1)}, u32[]{:S(2)}, u32[]{:S(2)}) collective-permute-start(f32[5,32,512]{2,1,0:T(8,128)S(1)} %get-tuple-element.110), channel_id=1, source_target_pairs={{0,1},{2,3},{1,0},{3,2},{4,5},{6,7},{5,4},{7,6},{8,9},{10,11},{9,8... | collective-permute-start | bytes 983048 | tf_op jit(solution)/shard_map/ppermute | solution.py:345
  49.8 11.8 %copy-start.4 = (f32[1,2,5,32,512]{4,3,2,1,0:T(8,128)S(1)}, f32[1,2,5,32,512]{4,3,2,1,0:T(8,128)}, u32[]{:S(2)}) copy-start(f32[1,2,5,32,512]{4,3,2,1,0:T(8,128)} %get-tuple-element.92) | copy-start | bytes 1966084
  49.9 22.3 %collective-permute-start.12 = (f32[1,2,5,32,512]{4,3,2,1,0:T(8,128)S(1)}, f32[1,2,5,32,512]{4,3,2,1,0:T(8,128)S(1)}, u32[]{:S(2)}, u32[]{:S(2)}) collective-permute-start(f32[1,2,5,32,512]{4,3,2,1,0:T(8,128)S(1)} %copy-done.5), channel_id=1, source_target_pairs={{4,0},{8,4},{12,8},{16,12},{20,16},{24,20},{28,24},{0,28},{5,1},{9... | collective-permute-start | bytes 1966088 | tf_op jit(solution)/shard_map/ppermute | solution.py:392
  61.6 10.5 %collective-permute-start.13 = (f32[1,2,5,32,512]{4,3,2,1,0:T(8,128)S(1)}, f32[1,2,5,32,512]{4,3,2,1,0:T(8,128)S(1)}, u32[]{:S(2)}, u32[]{:S(2)}) collective-permute-start(f32[1,2,5,32,512]{4,3,2,1,0:T(8,128)S(1)} %copy-done.4), channel_id=1, source_target_pairs={{4,0},{8,4},{12,8},{16,12},{20,16},{24,20},{28,24},{0,28},{5,1},{9... | collective-permute-start | bytes 1966088 | tf_op jit(solution)/shard_map/ppermute | solution.py:392
  63.1 8.5 %copy-start.3 = (f32[1,2,5,32,512]{4,3,2,1,0:T(8,128)S(1)}, f32[1,2,5,32,512]{4,3,2,1,0:T(8,128)}, u32[]{:S(2)}) copy-start(f32[1,2,5,32,512]{4,3,2,1,0:T(8,128)} %get-tuple-element.90) | copy-start | bytes 1966084
  71.6 9.0 %collective-permute-start.11 = (f32[1,2,5,32,512]{4,3,2,1,0:T(8,128)S(1)}, f32[1,2,5,32,512]{4,3,2,1,0:T(8,128)S(1)}, u32[]{:S(2)}, u32[]{:S(2)}) collective-permute-start(f32[1,2,5,32,512]{4,3,2,1,0:T(8,128)S(1)} %copy-done.3), channel_id=1, source_target_pairs={{4,0},{8,4},{12,8},{16,12},{20,16},{24,20},{28,24},{0,28},{5,1},{9... | collective-permute-start | bytes 1966088 | tf_op jit(solution)/shard_map/ppermute | solution.py:392
  (1 other events, 3.2 us)

commit v4 on v3

--- a/solution.py
+++ b/solution.py
@@ -11,6 +11,7 @@
 STEPS = 3
 LANES = 128
 PAD = 8
+LATE = 1
 ROWS = 16
 GROUPS = (1, 1, 1, 1, 1, 1, 1)
 TOGETHER = 2
@@ -92,7 +93,7 @@
         del refs[:count]
         return got
 
-    (coupling, odd_ref, weights, own, sensor) = take(5)
+    (coupling, odd_ref, weights_in, own, sensor) = take(5)
     chunks = take(len(groups))
     halos = take(2 * STEPS) if stage.first else []
     filtered = dict(zip(stage.taken, take(len(stage.taken))))
@@ -100,7 +101,7 @@
         take(1)
     (out,) = take(1)
     fresh = dict(zip(stage.given, take(len(stage.given))))
-    (result,) = take(1)
+    (result, weights) = take(2)
     fresh.update(zip(stage.kept, take(len(stage.kept))))
     filtered.update(fresh)
     highs = take(2)
@@ -122,6 +123,14 @@
 
         pl.loop(0, sides + 1)(clear)
 
+    step = 4 * ROWS
+
+    def fetch(i):
+        at = pl.ds(pl.multiple_of(i * step, step), step)
+        weights[at] = weights_in[at]
+
+    pl.loop(0, weights.shape[0] // step)(fetch)
+
     lane = lax.broadcasted_iota(jnp.int32, (ROWS, LANES), 1)
     at_start = lane == 0
     at_end = lane == LANES - 1
@@ -129,12 +138,24 @@
 
     def columns(b):
         return slice(b * LANES, (b + 1) * LANES)
+
+    waiting = []
+
+    def store_late(stores=None):
+        if stores is not None:
+            waiting.append(stores)
+        while len(waiting) > (LATE if stores is not None else 0):
+            for store in waiting.pop(0):
+                store()
 
     def put(value, place, row, b):
         at = (pl.ds(pl.multiple_of(row, ROWS), ROWS), columns(b))
         high = value.astype(jnp.bfloat16)
         highs[place][at] = high
         lows[place][at] = (value - high.astype(jnp.float32)).astype(jnp.bfloat16)
+
+    def keep(value, at):
+        result[at] = value
 
     def split_raw(q, place, t):
         for s in range(2):
@@ -145,8 +166,11 @@
                 chunk, k = starts[q]
                 source, side = chunks[chunk].at[k, s], s
             for f in range(fields):
+                stores = []
                 for b in range(blocks):
-                    put(source[f, pl.ds(t, ROWS), columns(b)], place, (side * fields + f) * nth + t, b)
+                    value = source[f, pl.ds(t, ROWS), columns(b)]
+                    stores.append(functools.partial(put, value, place, (side * fields + f) * nth + t, b))
+                store_late(stores)
 
     def sensor_at(q, s, t, b):
         if q >= 0:
@@ -177,6 +201,7 @@
                     around = here[b, pl.ds(base + (rows[f] - 1), ROWS)] + here[b, pl.ds(base + (rows[f] + 1), ROWS)]
                     laps.append((axial + around) + (left + right) - 6.0 * middle)
                 sens = sensor_at(q, s, t, b)
+                stores = []
                 for f in range(fields):
                     mixed = weight[0][f] * laps[0]
                     for g in range(1, fields):
@@ -185,9 +210,11 @@
                     if level == STEPS + 1:
                         plane = planes - 1 - q if s else q
                         at = (pl.ds(t, ROWS), columns(b))
-                        result[(q - out_low, s, f, *at)] = value - own[(0, f, plane, *at)]
+                        value = value - own[(0, f, plane, *at)]
+                        stores.append(functools.partial(keep, value, (q - out_low, s, f, *at)))
                     else:
-                        put(value, place, (s * fields + f) * nth + t, b)
+                        stores.append(functools.partial(put, value, place, (s * fields + f) * nth + t, b))
+                store_late(stores)
 
     starts = {}
     depth = max(stage.todo[1][0], 0)
@@ -197,25 +224,32 @@
             depth += 1
     out_low = stage.todo[STEPS + 1][0]
 
-    def project(level, q, place):
-        ref = filtered[level, q]
+    parts = nth // ROWS
+    width = nr // parts
+
+    def project(level, q, place, j):
         high = highs[place][...]
         left = jnp.concatenate([high, lows[place][...], high], axis=1)
-        product = jnp.dot(left, weights[...], preferred_element_type=jnp.float32)
+        return jnp.dot(left, weights[:, j * width : (j + 1) * width], preferred_element_type=jnp.float32)
+
+    def hold(level, q, product, j):
         for i in range(sides):
-            for b in range(blocks):
-                ref[b, i * stride + PAD : (i + 1) * stride] = product[i * nth : (i + 1) * nth, columns(b)]
+            for b in range(width // LANES):
+                at = (j * (width // LANES) + b, slice(i * stride + PAD, (i + 1) * stride))
+                filtered[level, q][at] = product[i * nth : (i + 1) * nth, columns(b)]
 
     def together(task, held):
-        if held is not None:
-            project(*held)
-        if task is not None:
-            level, q, place = task
-            for t in range(0, nth, ROWS):
+        for j in range(parts):
+            product = None if held is None else project(*held, j)
+            if task is not None:
+                level, q, place = task
                 if level == 1:
-                    split_raw(q, place, t)
+                    split_raw(q, place, j * ROWS)
                 else:
-                    advance(level, q, place, t)
+                    advance(level, q, place, j * ROWS)
+                store_late()
+            if held is not None:
+                hold(held[0], held[1], product, j)
 
     held = None
     sent = []
@@ -298,6 +332,7 @@
     low, high = stage.todo[STEPS + 1]
     scratch = [
         pltpu.VMEM((high - low, 2, fields, nth, nr), jnp.float32),
+        pltpu.VMEM(weights.shape, weights.dtype),
         *[pltpu.VMEM(slot, jnp.float32)] * len(stage.kept),
         *[pltpu.VMEM((sides * nth, nr), jnp.bfloat16)] * 4,
     ]
@@ -385,10 +420,11 @@
             key = max(carried)
             packed, carried[key] = lax.optimization_barrier((packed, carried[key]))
         elif i > 1:
-            ends = exchanged[i - STEPS] if STEPS <= i < len(exchanged) + STEPS else []
+            k = {STEPS: 0, STEPS + 2: 1}.get(i)
+            ends = [] if k is None else exchanged[k]
             packed, weights, chunks[i - 2], *ends = lax.optimization_barrier((packed, weights, chunks[i - 2], *ends))
             if ends:
-                exchanged[i - STEPS] = ends
+                exchanged[k] = ends
         chunks.append(lax.ppermute(packed, "seg", back))
         if 1 <= i <= STEPS:
             edges = [chunks[i - 1][0]] + ([sensor_edges[i - 1][:, None]] if i < STEPS else [])

time: 90.7 us -> 94 us (1.036)
  the two profiles are of different devices: /device:TPU:0 before, /device:TPU:9 now
where the time goes in v4:
time: 94 us; the launch traced here: 93.8 us
  Pallas kernels  45.2 us (48%)
  starting transfers between devices  23.7 us (25%)
  waiting for transfers between devices  21.2 us (23%)
  local copies, waits for them, and re-layouts  2.72 us (3%)
    pallas_call x4, Pallas kernels, run_stage(): pl.pallas_call(functools.partial(stage_kernel, stage, fields, planes, gro...  39.1 us
    ppermute x6, waiting for transfers between devices, swapped(): result.append(lax.ppermute(mine, 'gx', pairs + [(j, i) for i, j in pairs]))  15.1 us
    ppermute x8, starting transfers between devices, shards(): chunks.append(lax.ppermute(packed, 'seg', back))  13.5 us
    ppermute x6, starting transfers between devices, swapped(): result.append(lax.ppermute(mine, 'gx', pairs + [(j, i) for i, j in pairs]))  10.2 us
    ppermute x8, waiting for transfers between devices, shards(): chunks.append(lax.ppermute(packed, 'seg', back))  6.17 us
    pallas_call x1, Pallas kernels, pack_rest(): pl.pallas_call(functools.partial(pack_rest_kernel, planes, groups), out_s...  4.18 us
    unnamed x22, local copies, waits for them, and re-layouts  2.53 us
    pallas_call x1, Pallas kernels, pack_first(): pl.pallas_call(functools.partial(pack_first_kernel, planes), out_shape=ja...  1.92 us
  transfers between devices with their start and end apart: 14, of which 7 were waited for; matrix products, arithmetic and copies ran while one was open for 1% of the time, Pallas kernels for 36%

profile of v4, /device:TPU:9, one launch (start us, length us, event | category | flops | bytes accessed | tf_op | source)
XLA Modules:
  0.0 93.8 jit_solution(16503370482983688241)
XLA Ops:
  0.0 1.9 %pack_first.1.first = f32[1,2,5,32,512]{4,3,2,1,0:T(8,128)} custom-call(f32[1,5,16,32,512]{4,3,2,1,0:T(8,128)} %refs_3_.7), custom_call_target="tpu_custom_call" | custom-call | tf_op jit(solution)/shard_map/pack_first/pallas_call | solution.py:288
  1.9 0.7 collective-permute-start
  2.7 4.2 %pack_rest.1 = (f32[1,2,5,32,512]{4,3,2,1,0:T(8,128)}, f32[1,2,5,32,512]{4,3,2,1,0:T(8,128)}, f32[1,2,5,32,512]{4,3,2,1,0:T(8,128)}, f32[1,2,5,32,512]{4,3,2,1,0...) custom-call(f32[1,5,16,32,512]{4,3,2,1,0:T(8,128)} %refs_3_.7, ...), custom_call_target="tpu_custom_call" | custom-call | bytes 9699328 | tf_op jit(solution)/shard_map/pack_rest/pallas_call | solution.py:305
  6.9 1.9 %collective-permute-start.1 = (f32[1,2,5,32,512]{4,3,2,1,0:T(8,128)}, f32[1,2,5,32,512]{4,3,2,1,0:T(8,128)S(1)}, u32[]{:S(2)}, u32[]{:S(2)}) collective-permute-start(f32[1,2,5,32,512]{4,3,2,1,0:T(8,128)} %get-tuple-element.59), channel_id=1, source_target_pairs={{4,0},{8,4},{12,8},{16,12},{20,16},{24,20},{28,24},{0,28},{5,1},{9... | collective-permute-start | bytes 1966088 | tf_op jit(solution)/shard_map/ppermute | solution.py:428
  9.2 3.1 %collective-permute-done.refs_5_ = f32[1,2,5,32,512]{4,3,2,1,0:T(8,128)S(1)} collective-permute-done((f32[1,2,5,32,512]{4,3,2,1,0:T(8,128)}, f32[1,2,5,32,512]{4,3,2,1,0:T(8,128)S(1)}, u32[]{:S(2)}, u32[]{:S(2)}) %collective-permute-start) | collective-permute-done | bytes 655392 | tf_op jit(solution)/shard_map/ppermute | solution.py:428
  12.2 0.7 collective-permute-start.4
  13.4 4.3 %collective-permute-start.3 = (f32[6,32,512]{2,1,0:T(8,128)S(1)}, f32[6,32,512]{2,1,0:T(8,128)S(1)}, u32[]{:S(2)}, u32[]{:S(2)}) collective-permute-start(f32[6,32,512]{2,1,0:T(8,128)S(1)} %pad_maximum_fusion.2), channel_id=1, source_target_pairs={{1,2},{2,1},{5,6},{6,5},{9,10},{10,9},{13,14},{14,13},{17,18},{18,... | collective-permute-start | bytes 1179656 | tf_op jit(solution)/shard_map/ppermute | solution.py:380
  17.7 1.8 %collective-permute-done.1.refs_6_ = f32[1,2,5,32,512]{4,3,2,1,0:T(8,128)S(1)} collective-permute-done((f32[1,2,5,32,512]{4,3,2,1,0:T(8,128)}, f32[1,2,5,32,512]{4,3,2,1,0:T(8,128)S(1)}, u32[]{:S(2)}, u32[]{:S(2)}) %collective-permute-start.1) | collective-permute-done | bytes 655392 | tf_op jit(solution)/shard_map/ppermute | solution.py:428
  19.9 1.2 %collective-permute-done.2.refs_8_ = f32[6,32,512]{2,1,0:T(8,128)S(1)} collective-permute-done((f32[6,32,512]{2,1,0:T(8,128)S(1)}, f32[6,32,512]{2,1,0:T(8,128)S(1)}, u32[]{:S(2)}, u32[]{:S(2)}) %collective-permute-start.2) | collective-permute-done | bytes 393248 | tf_op jit(solution)/shard_map/ppermute | solution.py:380
  21.1 3.1 %collective-permute-done.3.refs_9_ = f32[6,32,512]{2,1,0:T(8,128)S(1)} collective-permute-done((f32[6,32,512]{2,1,0:T(8,128)S(1)}, f32[6,32,512]{2,1,0:T(8,128)S(1)}, u32[]{:S(2)}, u32[]{:S(2)}) %collective-permute-start.3) | collective-permute-done | bytes 393248 | tf_op jit(solution)/shard_map/ppermute | solution.py:380
  24.1 3.6 %collective-permute-start.5 = (f32[1,2,5,32,512]{4,3,2,1,0:T(8,128)S(1)}, f32[1,2,5,32,512]{4,3,2,1,0:T(8,128)S(1)}, u32[]{:S(2)}, u32[]{:S(2)}) collective-permute-start(f32[1,2,5,32,512]{4,3,2,1,0:T(8,128)S(1)} %copy-done.10), channel_id=1, source_target_pairs={{4,0},{8,4},{12,8},{16,12},{20,16},{24,20},{28,24},{0,28},{5,1},{9... | collective-permute-start | bytes 1966088 | tf_op jit(solution)/shard_map/ppermute | solution.py:428
  27.8 2.1 %collective-permute-start.8 = (f32[1,2,5,32,512]{4,3,2,1,0:T(8,128)S(1)}, f32[1,2,5,32,512]{4,3,2,1,0:T(8,128)S(1)}, u32[]{:S(2)}, u32[]{:S(2)}) collective-permute-start(f32[1,2,5,32,512]{4,3,2,1,0:T(8,128)S(1)} %copy-done.9), channel_id=1, source_target_pairs={{4,0},{8,4},{12,8},{16,12},{20,16},{24,20},{28,24},{0,28},{5,1},{9... | collective-permute-start | bytes 1966088 | tf_op jit(solution)/shard_map/ppermute | solution.py:428
  29.9 3.2 %collective-permute-start.7 = (f32[6,32,512]{2,1,0:T(8,128)S(1)}, f32[6,32,512]{2,1,0:T(8,128)S(1)}, u32[]{:S(2)}, u32[]{:S(2)}) collective-permute-start(f32[6,32,512]{2,1,0:T(8,128)S(1)} %pad_maximum_fusion.4), channel_id=1, source_target_pairs={{1,2},{2,1},{5,6},{6,5},{9,10},{10,9},{13,14},{14,13},{17,18},{18,... | collective-permute-start | bytes 1179656 | tf_op jit(solution)/shard_map/ppermute | solution.py:380
  33.1 2.1 %collective-permute-start.10 = (f32[5,32,512]{2,1,0:T(8,128)S(1)}, f32[5,32,512]{2,1,0:T(8,128)S(1)}, u32[]{:S(2)}, u32[]{:S(2)}) collective-permute-start(f32[5,32,512]{2,1,0:T(8,128)S(1)} %get-tuple-element.105), channel_id=1, source_target_pairs={{1,2},{2,1},{5,6},{6,5},{9,10},{10,9},{13,14},{14,13},{17,18},{18,... | collective-permute-start | bytes 983048 | tf_op jit(solution)/shard_map/ppermute | solution.py:380
  35.4 6.4 %collective-permute-done.7.refs_11_ = f32[6,32,512]{2,1,0:T(8,128)S(1)} collective-permute-done((f32[6,32,512]{2,1,0:T(8,128)S(1)}, f32[6,32,512]{2,1,0:T(8,128)S(1)}, u32[]{:S(2)}, u32[]{:S(2)}) %collective-permute-start.7) | collective-permute-done | bytes 393248 | tf_op jit(solution)/shard_map/ppermute | solution.py:380
  41.8 2.6 %collective-permute-start.12 = (f32[1,2,5,32,512]{4,3,2,1,0:T(8,128)S(1)}, f32[1,2,5,32,512]{4,3,2,1,0:T(8,128)S(1)}, u32[]{:S(2)}, u32[]{:S(2)}) collective-permute-start(f32[1,2,5,32,512]{4,3,2,1,0:T(8,128)S(1)} %copy-done.8), channel_id=1, source_target_pairs={{4,0},{8,4},{12,8},{16,12},{20,16},{24,20},{28,24},{0,28},{5,1},{9... | collective-permute-start | bytes 1966088 | tf_op jit(solution)/shard_map/ppermute | solution.py:428
  44.4 4.4 %collective-permute-done.10.refs_13_ = f32[5,32,512]{2,1,0:T(8,128)S(1)} collective-permute-done((f32[5,32,512]{2,1,0:T(8,128)S(1)}, f32[5,32,512]{2,1,0:T(8,128)S(1)}, u32[]{:S(2)}, u32[]{:S(2)}) %collective-permute-start.10) | collective-permute-done | bytes 327712 | tf_op jit(solution)/shard_map/ppermute | solution.py:380
  48.8 2.5 %copy-done = f32[1,5,16,32,512]{4,3,2,1,0:T(8,128)S(1)} copy-done((f32[1,5,16,32,512]{4,3,2,1,0:T(8,128)S(1)}, f32[1,5,16,32,512]{4,3,2,1,0:T(8,128)}, u32[]{:S(2)}) %copy-start) | copy-done | bytes 5242904
  51.3 11.8 %stage_first.1 = (f32[1,5,16,32,512]{4,3,2,1,0:T(8,128)}, f32[4,408,128]{2,1,0:T(8,128)S(1)}, f32[4,408,128]{2,1,0:T(8,128)S(1)}, f32[4,408,128]{2,1,0:T(8,128)S...) custom-call(f32[5,5]{1,0:T(8,128)S(1)} %copy-done.3, ...), custom_call_target="tpu_custom_call" | custom-call | bytes 17072128 | tf_op jit(solution)/shard_map/stage_first/pallas_call | solution.py:340
  63.2 1.7 %collective-permute-start.13 = (f32[1,2,5,32,512]{4,3,2,1,0:T(8,128)S(1)}, f32[1,2,5,32,512]{4,3,2,1,0:T(8,128)S(1)}, u32[]{:S(2)}, u32[]{:S(2)}) collective-permute-start(f32[1,2,5,32,512]{4,3,2,1,0:T(8,128)S(1)} %copy-done.7), channel_id=1, source_target_pairs={{4,0},{8,4},{12,8},{16,12},{20,16},{24,20},{28,24},{0,28},{5,1},{9... | collective-permute-start | bytes 1966088 | tf_op jit(solution)/shard_map/ppermute | solution.py:428
  64.9 8.8 %stage_middle.2 = (f32[1,5,16,32,512]{4,3,2,1,0:T(8,128)}, f32[4,408,128]{2,1,0:T(8,128)S(1)}, f32[4,408,128]{2,1,0:T(8,128)S(1)}, f32[4,408,128]{2,1,0:T(8,128)...) custom-call(f32[5,5]{1,0:T(8,128)S(1)} %copy-done.3, ...), custom_call_target="tpu_custom_call", output_to_operand_aliasing={{0}: (13, {})} | custom-call | tf_op jit(solution)/shard_map/stage_middle/pallas_call | solution.py:340
  73.8 8.7 %stage_middle.3 = (f32[1,5,16,32,512]{4,3,2,1,0:T(8,128)}, f32[4,408,128]{2,1,0:T(8,128)S(1)}, f32[4,408,128]{2,1,0:T(8,128)S(1)}, f32[4,408,128]{2,1,0:T(8,128)...) custom-call(f32[5,5]{1,0:T(8,128)S(1)} %copy-done.3, ...), custom_call_target="tpu_custom_call", output_to_operand_aliasing={{0}: (13, {})} | custom-call | tf_op jit(solution)/shard_map/stage_middle/pallas_call | solution.py:340
  82.5 1.3 %collective-permute-done.11.refs_5_ = f32[1,2,5,32,512]{4,3,2,1,0:T(8,128)S(1)} collective-permute-done((f32[1,2,5,32,512]{4,3,2,1,0:T(8,128)S(1)}, f32[1,2,5,32,512]{4,3,2,1,0:T(8,128)S(1)}, u32[]{:S(2)}, u32[]{:S(2)}) %collective-permute-start.11) | collective-permute-done | bytes 655392 | tf_op jit(solution)/shard_map/ppermute | solution.py:428
  83.7 9.9 %stage_last.1 = f32[1,5,16,32,512]{4,3,2,1,0:T(8,128)} custom-call(f32[5,5]{1,0:T(8,128)S(1)} %copy-done.3, s32[2]{0:T(128)S(1)} %pad_add_fusion.refs_1_, bf16[1536,512]{1,0:T(8,128)(2,1)S(1)} %pad_maximum_fusion.refs_2_, f32[1,5,16,32,512]{4,3,2,1,0:T(8,128)S(1)} %copy-done.1, f32[1,16,32,512]{3,2,1,0:T(8,128)S(1)} %copy-done.2, ...), custom_call_target="tpu_custom_call", output_to_operand_aliasing={{}: (12, {})} | custom-call | tf_op jit(solution)/shard_map/stage_last/pallas_call | solution.py:340
  (45 shorter events, 1.4 us)
Async XLA Ops:
  1.9 6.9 %copy-start.4 = (f32[512,512]{1,0:T(8,128)S(1)}, f32[512,512]{1,0:T(8,128)}, u32[]{:S(2)}) copy-start(f32[512,512]{1,0:T(8,128)} %param.6) | copy-start | bytes 3145732
  1.9 10.3 %collective-permute-start = (f32[1,2,5,32,512]{4,3,2,1,0:T(8,128)}, f32[1,2,5,32,512]{4,3,2,1,0:T(8,128)S(1)}, u32[]{:S(2)}, u32[]{:S(2)}) collective-permute-start(f32[1,2,5,32,512]{4,3,2,1,0:T(8,128)} %pack_first.1.first), channel_id=1, source_target_pairs={{4,0},{8,4},{12,8},{16,12},{20,16},{24,20},{28,24},{0,28},{5,1},{9... | collective-permute-start | bytes 1966088 | tf_op jit(solution)/shard_map/ppermute | solution.py:428
  6.9 12.7 %collective-permute-start.1 = (f32[1,2,5,32,512]{4,3,2,1,0:T(8,128)}, f32[1,2,5,32,512]{4,3,2,1,0:T(8,128)S(1)}, u32[]{:S(2)}, u32[]{:S(2)}) collective-permute-start(f32[1,2,5,32,512]{4,3,2,1,0:T(8,128)} %get-tuple-element.59), channel_id=1, source_target_pairs={{4,0},{8,4},{12,8},{16,12},{20,16},{24,20},{28,24},{0,28},{5,1},{9... | collective-permute-start | bytes 1966088 | tf_op jit(solution)/shard_map/ppermute | solution.py:428
  9.1 15.0 %copy-start.10 = (f32[1,2,5,32,512]{4,3,2,1,0:T(8,128)S(1)}, f32[1,2,5,32,512]{4,3,2,1,0:T(8,128)}, u32[]{:S(2)}) copy-start(f32[1,2,5,32,512]{4,3,2,1,0:T(8,128)} %get-tuple-element.64) | copy-start | bytes 1966084
  9.2 18.6 %copy-start.9 = (f32[1,2,5,32,512]{4,3,2,1,0:T(8,128)S(1)}, f32[1,2,5,32,512]{4,3,2,1,0:T(8,128)}, u32[]{:S(2)}) copy-start(f32[1,2,5,32,512]{4,3,2,1,0:T(8,128)} %get-tuple-element.68) | copy-start | bytes 1966084
  12.2 15.5 %collective-permute-start.4 = (f32[1,2,5,32,512]{4,3,2,1,0:T(8,128)}, f32[1,2,5,32,512]{4,3,2,1,0:T(8,128)S(1)}, u32[]{:S(2)}, u32[]{:S(2)}) collective-permute-start(f32[1,2,5,32,512]{4,3,2,1,0:T(8,128)} %get-tuple-element.62), channel_id=1, source_target_pairs={{4,0},{8,4},{12,8},{16,12},{20,16},{24,20},{28,24},{0,28},{5,1},{9... | collective-permute-start | bytes 1966088 | tf_op jit(solution)/shard_map/ppermute | solution.py:428
  13.0 28.8 %copy-start.8 = (f32[1,2,5,32,512]{4,3,2,1,0:T(8,128)S(1)}, f32[1,2,5,32,512]{4,3,2,1,0:T(8,128)}, u32[]{:S(2)}) copy-start(f32[1,2,5,32,512]{4,3,2,1,0:T(8,128)} %get-tuple-element.87) | copy-start | bytes 1966084
  13.0 35.8 %copy-start.2 = (f32[1,16,32,512]{3,2,1,0:T(8,128)S(1)}, f32[1,16,32,512]{3,2,1,0:T(8,128)}, u32[]{:S(2)}) copy-start(f32[1,16,32,512]{3,2,1,0:T(8,128)} %refs_4_.7) | copy-start | bytes 3145732
  13.0 35.8 %copy-start.3 = (f32[5,5]{1,0:T(8,128)S(1)}, f32[5,5]{1,0:T(8,128)}, u32[]{:S(2)}) copy-start(f32[5,5]{1,0:T(8,128)} %refs_0_.7) | copy-start | bytes 304
  13.1 8.0 %collective-permute-start.2 = (f32[6,32,512]{2,1,0:T(8,128)S(1)}, f32[6,32,512]{2,1,0:T(8,128)S(1)}, u32[]{:S(2)}, u32[]{:S(2)}) collective-permute-start(f32[6,32,512]{2,1,0:T(8,128)S(1)} %pad_maximum_fusion.1), channel_id=1, source_target_pairs={{0,1},{2,3},{1,0},{3,2},{4,5},{6,7},{5,4},{7,6},{8,9},{10,11},{9,8... | collective-permute-start | bytes 1179656 | tf_op jit(solution)/shard_map/ppermute | solution.py:380
  13.4 10.8 %collective-permute-start.3 = (f32[6,32,512]{2,1,0:T(8,128)S(1)}, f32[6,32,512]{2,1,0:T(8,128)S(1)}, u32[]{:S(2)}, u32[]{:S(2)}) collective-permute-start(f32[6,32,512]{2,1,0:T(8,128)S(1)} %pad_maximum_fusion.2), channel_id=1, source_target_pairs={{1,2},{2,1},{5,6},{6,5},{9,10},{10,9},{13,14},{14,13},{17,18},{18,... | collective-permute-start | bytes 1179656 | tf_op jit(solution)/shard_map/ppermute | solution.py:380
  19.7 15.6 %collective-permute-start.6 = (f32[6,32,512]{2,1,0:T(8,128)S(1)}, f32[6,32,512]{2,1,0:T(8,128)S(1)}, u32[]{:S(2)}, u32[]{:S(2)}) collective-permute-start(f32[6,32,512]{2,1,0:T(8,128)S(1)} %pad_maximum_fusion.3), channel_id=1, source_target_pairs={{0,1},{2,3},{1,0},{3,2},{4,5},{6,7},{5,4},{7,6},{8,9},{10,11},{9,8... | collective-permute-start | bytes 1179656 | tf_op jit(solution)/shard_map/ppermute | solution.py:380
  24.1 17.7 %collective-permute-start.5 = (f32[1,2,5,32,512]{4,3,2,1,0:T(8,128)S(1)}, f32[1,2,5,32,512]{4,3,2,1,0:T(8,128)S(1)}, u32[]{:S(2)}, u32[]{:S(2)}) collective-permute-start(f32[1,2,5,32,512]{4,3,2,1,0:T(8,128)S(1)} %copy-done.10), channel_id=1, source_target_pairs={{4,0},{8,4},{12,8},{16,12},{20,16},{24,20},{28,24},{0,28},{5,1},{9... | collective-permute-start | bytes 1966088 | tf_op jit(solution)/shard_map/ppermute | solution.py:428
  27.8 37.1 %collective-permute-start.8 = (f32[1,2,5,32,512]{4,3,2,1,0:T(8,128)S(1)}, f32[1,2,5,32,512]{4,3,2,1,0:T(8,128)S(1)}, u32[]{:S(2)}, u32[]{:S(2)}) collective-permute-start(f32[1,2,5,32,512]{4,3,2,1,0:T(8,128)S(1)} %copy-done.9), channel_id=1, source_target_pairs={{4,0},{8,4},{12,8},{16,12},{20,16},{24,20},{28,24},{0,28},{5,1},{9... | collective-permute-start | bytes 1966088 | tf_op jit(solution)/shard_map/ppermute | solution.py:428
  29.9 11.9 %collective-permute-start.7 = (f32[6,32,512]{2,1,0:T(8,128)S(1)}, f32[6,32,512]{2,1,0:T(8,128)S(1)}, u32[]{:S(2)}, u32[]{:S(2)}) collective-permute-start(f32[6,32,512]{2,1,0:T(8,128)S(1)} %pad_maximum_fusion.4), channel_id=1, source_target_pairs={{1,2},{2,1},{5,6},{6,5},{9,10},{10,9},{13,14},{14,13},{17,18},{18,... | collective-permute-start | bytes 1179656 | tf_op jit(solution)/shard_map/ppermute | solution.py:380
  33.1 15.7 %collective-permute-start.10 = (f32[5,32,512]{2,1,0:T(8,128)S(1)}, f32[5,32,512]{2,1,0:T(8,128)S(1)}, u32[]{:S(2)}, u32[]{:S(2)}) collective-permute-start(f32[5,32,512]{2,1,0:T(8,128)S(1)} %get-tuple-element.105), channel_id=1, source_target_pairs={{1,2},{2,1},{5,6},{6,5},{9,10},{10,9},{13,14},{14,13},{17,18},{18,... | collective-permute-start | bytes 983048 | tf_op jit(solution)/shard_map/ppermute | solution.py:380
  35.2 13.6 %collective-permute-start.9 = (f32[5,32,512]{2,1,0:T(8,128)S(1)}, f32[5,32,512]{2,1,0:T(8,128)S(1)}, u32[]{:S(2)}, u32[]{:S(2)}) collective-permute-start(f32[5,32,512]{2,1,0:T(8,128)S(1)} %get-tuple-element.106), channel_id=1, source_target_pairs={{0,1},{2,3},{1,0},{3,2},{4,5},{6,7},{5,4},{7,6},{8,9},{10,11},{9,8... | collective-permute-start | bytes 983048 | tf_op jit(solution)/shard_map/ppermute | solution.py:380
  41.8 32.0 %collective-permute-start.12 = (f32[1,2,5,32,512]{4,3,2,1,0:T(8,128)S(1)}, f32[1,2,5,32,512]{4,3,2,1,0:T(8,128)S(1)}, u32[]{:S(2)}, u32[]{:S(2)}) collective-permute-start(f32[1,2,5,32,512]{4,3,2,1,0:T(8,128)S(1)} %copy-done.8), channel_id=1, source_target_pairs={{4,0},{8,4},{12,8},{16,12},{20,16},{24,20},{28,24},{0,28},{5,1},{9... | collective-permute-start | bytes 1966088 | tf_op jit(solution)/shard_map/ppermute | solution.py:428
  48.8 2.5 %copy-start = (f32[1,5,16,32,512]{4,3,2,1,0:T(8,128)S(1)}, f32[1,5,16,32,512]{4,3,2,1,0:T(8,128)}, u32[]{:S(2)}) copy-start(f32[1,5,16,32,512]{4,3,2,1,0:T(8,128)} %refs_3_.7) | copy-start | bytes 15728644
  51.3 11.8 %copy-start.7 = (f32[1,2,5,32,512]{4,3,2,1,0:T(8,128)S(1)}, f32[1,2,5,32,512]{4,3,2,1,0:T(8,128)}, u32[]{:S(2)}) copy-start(f32[1,2,5,32,512]{4,3,2,1,0:T(8,128)} %get-tuple-element.88) | copy-start | bytes 1966084
  51.3 13.6 %copy-start.1 = (f32[1,5,16,32,512]{4,3,2,1,0:T(8,128)S(1)}, f32[1,5,16,32,512]{4,3,2,1,0:T(8,128)}, u32[]{:S(2)}) copy-start(f32[1,5,16,32,512]{4,3,2,1,0:T(8,128)} %refs_3_.7) | copy-start | bytes 15728644
  63.2 10.6 %collective-permute-start.13 = (f32[1,2,5,32,512]{4,3,2,1,0:T(8,128)S(1)}, f32[1,2,5,32,512]{4,3,2,1,0:T(8,128)S(1)}, u32[]{:S(2)}, u32[]{:S(2)}) collective-permute-start(f32[1,2,5,32,512]{4,3,2,1,0:T(8,128)S(1)} %copy-done.7), channel_id=1, source_target_pairs={{4,0},{8,4},{12,8},{16,12},{20,16},{24,20},{28,24},{0,28},{5,1},{9... | collective-permute-start | bytes 1966088 | tf_op jit(solution)/shard_map/ppermute | solution.py:428
  64.9 8.8 %copy-start.6 = (f32[1,2,5,32,512]{4,3,2,1,0:T(8,128)S(1)}, f32[1,2,5,32,512]{4,3,2,1,0:T(8,128)}, u32[]{:S(2)}) copy-start(f32[1,2,5,32,512]{4,3,2,1,0:T(8,128)} %get-tuple-element.86) | copy-start | bytes 1966084
  73.7 10.1 %collective-permute-start.11 = (f32[1,2,5,32,512]{4,3,2,1,0:T(8,128)S(1)}, f32[1,2,5,32,512]{4,3,2,1,0:T(8,128)S(1)}, u32[]{:S(2)}, u32[]{:S(2)}) collective-permute-start(f32[1,2,5,32,512]{4,3,2,1,0:T(8,128)S(1)} %copy-done.6), channel_id=1, source_target_pairs={{4,0},{8,4},{12,8},{16,12},{20,16},{24,20},{28,24},{0,28},{5,1},{9... | collective-permute-start | bytes 1966088 | tf_op jit(solution)/shard_map/ppermute | solution.py:428
  (1 other events, 2.2 us)

commit v5 on v4

--- a/solution.py
+++ b/solution.py
@@ -20,22 +20,33 @@
 
 
 class Stage:
-    def __init__(self, start, stop, half):
+    def __init__(self, region, known, half):
         self.half = half
-        self.first, self.last = start == -STEPS, stop == half
+        self.region, self.known = region, known
+        self.halos = region[0] < 0 <= known[0]
         self.todo = {}
         for level in range(1, STEPS + 2):
-            lag = level - 1
-            low = start + lag if self.first else start - lag
-            self.todo[level] = (low, stop if self.last else stop - lag)
-        self.taken, self.given, self.kept = [], [], []
-        for level in range(1, STEPS + 1):
-            low, high = self.todo[level]
-            if not self.first:
-                self.taken += [(level, low - 2), (level, low - 1)]
-            handed = high if self.last else high - 2
-            self.kept += [(level, q) for q in range(low, min(handed, high))]
-            self.given += [(level, q) for q in range(max(handed, low), high)]
+            done = self.reach(known, level)
+            self.todo[level] = [q for q in self.reach(region, level) if q not in done]
+        made = [(level, q) for level in range(1, STEPS + 1) for q in self.todo[level]]
+        self.needs = {
+            (level - 1, other)
+            for level in range(2, STEPS + 2)
+            for q in self.todo[level]
+            for other in range(q - 1, min(q + 2, half))
+        }
+        self.made = made
+        self.taken = sorted(self.needs - set(made))
+        self.given, self.kept = [], made
+
+    def reach(self, region, level):
+        low, high = region
+        return range(low + level - 1, high if high == self.half else high - level + 1)
+
+    def hand_on(self, later):
+        wanted = set().union(*(stage.needs for stage in later))
+        self.given = [key for key in self.made if key in wanted]
+        self.kept = [key for key in self.made if key not in wanted]
 
 
 def pack_first_kernel(planes, source, result, sems):
@@ -85,7 +96,7 @@
         one.wait()
 
 
-def stage_kernel(stage, fields, planes, groups, *refs):
+def stage_kernel(stage, fields, planes, aliased, groups, *refs):
     refs = list(refs)
 
     def take(count):
@@ -93,13 +104,14 @@
         del refs[:count]
         return got
 
-    (coupling, odd_ref, weights_in, own, sensor) = take(5)
+    (coupling, odd_ref, weights_in, sensor) = take(4)
     chunks = take(len(groups))
-    halos = take(2 * STEPS) if stage.first else []
+    halos = take(2 * STEPS) if stage.halos else []
     filtered = dict(zip(stage.taken, take(len(stage.taken))))
-    if not stage.first:
-        take(1)
-    (out,) = take(1)
+    outs = stage.todo[STEPS + 1]
+    (own,) = take(1) if outs else [None]
+    take(1 if aliased else 0)
+    (out,) = take(1) if outs else [None]
     fresh = dict(zip(stage.given, take(len(stage.given))))
     (result, weights) = take(2)
     fresh.update(zip(stage.kept, take(len(stage.kept))))
@@ -109,7 +121,7 @@
     (sems,) = take(1)
 
     sides = 2 * fields
-    nth, nr = own.shape[-2:]
+    nth, nr = sensor.shape[-2:]
     blocks = nr // LANES
     stride = nth + PAD
     odd, base = odd_ref[0], odd_ref[1]
@@ -211,18 +223,17 @@
                         plane = planes - 1 - q if s else q
                         at = (pl.ds(t, ROWS), columns(b))
                         value = value - own[(0, f, plane, *at)]
-                        stores.append(functools.partial(keep, value, (q - out_low, s, f, *at)))
+                        stores.append(functools.partial(keep, value, (outs.index(q), s, f, *at)))
                     else:
                         stores.append(functools.partial(put, value, place, (s * fields + f) * nth + t, b))
                 store_late(stores)
 
     starts = {}
-    depth = max(stage.todo[1][0], 0)
+    depth = stage.known[1]
     for i, count in enumerate(groups):
         for k in range(count):
             starts[depth] = (i, k)
             depth += 1
-    out_low = stage.todo[STEPS + 1][0]
 
     parts = nth // ROWS
     width = nr // parts
@@ -254,8 +265,8 @@
     held = None
     sent = []
     for level in range(1, STEPS + 2):
-        for q in range(*stage.todo[level]):
-            if held is not None and held[0] == level - 1 and held[1] <= q + 1:
+        for q in stage.todo[level]:
+            if held is not None and held[0] == level - 1 and abs(held[1] - q) <= 1:
                 together(None, held)
                 held = None
             place = 0 if held is None else 1 - held[2]
@@ -265,7 +276,7 @@
                 for s in range(2):
                     plane = planes - 1 - q if s else q
                     sent.append(
-                        pltpu.make_async_copy(result.at[q - out_low, s], out.at[0, :, plane], sems.at[len(sent)])
+                        pltpu.make_async_copy(result.at[outs.index(q), s], out.at[0, :, plane], sems.at[len(sent)])
                     )
                     sent[-1].start()
     if held is not None:
@@ -322,34 +333,38 @@
     fields, planes, nth, nr = own.shape[1:]
     sides = 2 * fields
     slot = (nr // LANES, sides * (nth + PAD) + PAD, LANES)
-    close = [weights, own, sensor, *chunks]
-    if stage.first:
+    outs = len(stage.todo[STEPS + 1])
+    close = [weights, sensor, *chunks]
+    if stage.halos:
         close += halos
     close += [carried[key] for key in stage.taken]
-    operands = [coupling, odd, *close] + ([] if stage.first else [out])
-    in_specs = [SCALARS] * 2 + [CLOSE] * len(close) + ([] if stage.first else [ANYWHERE])
+    if outs:
+        close.append(own)
+    aliased = bool(outs) and out is not None
+    operands = [coupling, odd, *close] + ([out] if aliased else [])
+    in_specs = [SCALARS] * 2 + [CLOSE] * len(close) + ([ANYWHERE] if aliased else [])
     given = [jax.ShapeDtypeStruct(slot, jnp.float32)] * len(stage.given)
-    low, high = stage.todo[STEPS + 1]
+    written = [jax.ShapeDtypeStruct(own.shape, jnp.float32)] if outs else []
     scratch = [
-        pltpu.VMEM((high - low, 2, fields, nth, nr), jnp.float32),
+        pltpu.VMEM((max(outs, 1), 2, fields, nth, nr), jnp.float32),
         pltpu.VMEM(weights.shape, weights.dtype),
         *[pltpu.VMEM(slot, jnp.float32)] * len(stage.kept),
         *[pltpu.VMEM((sides * nth, nr), jnp.bfloat16)] * 4,
     ]
     limit = VMEM_SPARE + size(*scratch, *close, *given)
-    out, *fresh = pl.pallas_call(
-        functools.partial(stage_kernel, stage, fields, planes, groups),
-        out_shape=[jax.ShapeDtypeStruct(own.shape, jnp.float32), *given],
+    fresh = pl.pallas_call(
+        functools.partial(stage_kernel, stage, fields, planes, aliased, groups),
+        out_shape=[*written, *given],
         in_specs=in_specs,
-        out_specs=[ANYWHERE] + [CLOSE] * len(given),
-        scratch_shapes=scratch + [pltpu.SemaphoreType.DMA((2 * max(high - low, 1),))],
-        input_output_aliases={} if stage.first else {len(operands) - 1: 0},
-        cost_estimate=pl.CostEstimate(
-            flops=0, bytes_accessed=size(*close, *given) if stage.first else 0, transcendentals=0
-        ),
+        out_specs=[ANYWHERE] * len(written) + [CLOSE] * len(given),
+        scratch_shapes=scratch + [pltpu.SemaphoreType.DMA((2 * max(outs, 1),))],
+        input_output_aliases={len(operands) - 1: 0} if aliased else {},
+        cost_estimate=pl.CostEstimate(flops=0, bytes_accessed=0, transcendentals=0),
         compiler_params=pltpu.CompilerParams(vmem_limit_bytes=limit),
-        name=f"stage_{'first' if stage.first else 'last' if stage.last else 'middle'}",
+        name="stage_" + "_".join(str(q).replace("-", "m") for q in stage.region),
     )(*operands)
+    if outs:
+        out, *fresh = fresh
     return out, dict(zip(stage.given, fresh))
 
 
@@ -385,53 +400,49 @@
     weights = jnp.concatenate([high, high, low], axis=0).astype(jnp.bfloat16)
     scalar = jnp.stack([odd, 0 * odd]).astype(jnp.int32)
 
-    stages = [(0, STEPS)]
-    while stages[-1][1] < len(groups):
-        low_cut = stages[-1][1]
-        stages.append((low_cut, max(min(low_cut + TOGETHER, len(groups) - 1), low_cut + 1)))
     cuts = [sum(groups[:i]) for i in range(len(groups) + 1)]
+    regions = [(0, cut) for cut in cuts[STEPS + 1 : STEPS + 3]]
+    regions.append((-STEPS, regions[-1][1]))
+    while regions[-1][1] < half:
+        upto = cuts.index(regions[-1][1])
+        upto = max(min(upto + TOGETHER, len(groups) - 1), upto + 1)
+        regions.append((-STEPS, cuts[upto]))
+    stages = [Stage(new, old, half) for old, new in zip([(0, 0), *regions], regions)]
+    for number, stage in enumerate(stages):
+        stage.hand_on(stages[number + 1 :])
     carried, out = {}, None
     halos = []
 
     def run(number):
         nonlocal out
-        low_cut, high_cut = stages[number]
-        mine = groups[low_cut:high_cut]
-        stage = Stage(cuts[low_cut] if number else -STEPS, cuts[high_cut], half)
+        stage = stages[number]
+        at = slice(cuts.index(stage.known[1]), cuts.index(stage.region[1]))
         out, fresh = run_stage(
-            stage, mine, coupling, scalar, weights, adjoint_in, sensor,
-            chunks[low_cut:high_cut], halos, carried, out,
+            stage, groups[at], coupling, scalar, weights, adjoint_in, sensor, chunks[at], halos, carried, out
         )
         carried.update(fresh)
 
     chunks, exchanged = [], []
     ran = 0
 
-    def unpack():
-        nonlocal halos
-        halos = sum(exchanged, [])
-
     for i, packed in enumerate([first_chunk, *rest]):
-        if i >= STEPS + 3 and stages[ran][1] < i:
-            if ran == 0:
-                unpack()
+        k = {STEPS: 0, STEPS + 1: 1, STEPS + 3: 2}.get(i)
+        ends = exchanged[k] if k is not None and k < len(exchanged) else []
+        if i >= STEPS + 3 and not stages[ran].halos and cuts.index(stages[ran].region[1]) < i:
             run(ran)
+            key = stages[ran].given[-1]
             ran += 1
-            key = max(carried)
-            packed, carried[key] = lax.optimization_barrier((packed, carried[key]))
+            packed, carried[key], *ends = lax.optimization_barrier((packed, carried[key], *ends))
         elif i > 1:
-            k = {STEPS: 0, STEPS + 2: 1}.get(i)
-            ends = [] if k is None else exchanged[k]
             packed, weights, chunks[i - 2], *ends = lax.optimization_barrier((packed, weights, chunks[i - 2], *ends))
-            if ends:
-                exchanged[k] = ends
+        if ends:
+            exchanged[k] = ends
         chunks.append(lax.ppermute(packed, "seg", back))
         if 1 <= i <= STEPS:
             edges = [chunks[i - 1][0]] + ([sensor_edges[i - 1][:, None]] if i < STEPS else [])
             exchanged.append(swapped(edges))
+    halos = sum(exchanged, [])
     for number in range(ran, len(stages)):
-        if number == 0:
-            unpack()
         run(number)
     return out
 

time: 94 us -> 85.7 us (0.912)
  the two profiles are of different devices: /device:TPU:9 before, /device:TPU:0 now
where the time goes in v5:
time: 85.7 us; the launch traced here: 85.5 us
  Pallas kernels  45.3 us (53%)
  starting transfers between devices  25.4 us (30%)
  waiting for transfers between devices  12.6 us (15%)
  local copies, waits for them, and re-layouts  1.22 us (1%)
    pallas_call x5, Pallas kernels, run_stage(): pl.pallas_call(functools.partial(stage_kernel, stage, fields, planes, ali...  39.2 us
    ppermute x6, starting transfers between devices, swapped(): result.append(lax.ppermute(mine, 'gx', pairs + [(j, i) for i, j in pairs]))  13.9 us
    ppermute x8, starting transfers between devices, shards(): chunks.append(lax.ppermute(packed, 'seg', back))  11.5 us
    ppermute x6, waiting for transfers between devices, swapped(): result.append(lax.ppermute(mine, 'gx', pairs + [(j, i) for i, j in pairs]))  8.4 us
    ppermute x8, waiting for transfers between devices, shards(): chunks.append(lax.ppermute(packed, 'seg', back))  4.2 us
    pallas_call x1, Pallas kernels, pack_rest(): pl.pallas_call(functools.partial(pack_rest_kernel, planes, groups), out_s...  4.16 us
    pallas_call x1, Pallas kernels, pack_first(): pl.pallas_call(functools.partial(pack_first_kernel, planes), out_shape=ja...  1.92 us
  transfers between devices with their start and end apart: 14, of which 5 were waited for; matrix products, arithmetic and copies ran while one was open for 2% of the time, Pallas kernels for 39%

profile of v5, /device:TPU:0, one launch (start us, length us, event | category | flops | bytes accessed | tf_op | source)
XLA Modules:
  0.0 85.5 jit_solution(15593381304695633636)
XLA Ops:
  0.0 1.9 %pack_first.1.first = f32[1,2,5,32,512]{4,3,2,1,0:T(8,128)} custom-call(f32[1,5,16,32,512]{4,3,2,1,0:T(8,128)} %refs_11_.1), custom_call_target="tpu_custom_call" | custom-call | tf_op jit(solution)/shard_map/pack_first/pallas_call | solution.py:299
  1.9 3.4 %collective-permute-start = (f32[1,2,5,32,512]{4,3,2,1,0:T(8,128)}, f32[1,2,5,32,512]{4,3,2,1,0:T(8,128)S(1)}, u32[]{:S(2)}, u32[]{:S(2)}) collective-permute-start(f32[1,2,5,32,512]{4,3,2,1,0:T(8,128)} %pack_first.1.first), channel_id=1, source_target_pairs={{4,0},{8,4},{12,8},{16,12},{20,16},{24,20},{28,24},{0,28},{5,1},{9... | collective-permute-start | bytes 1966088 | tf_op jit(solution)/shard_map/ppermute | solution.py:440
  5.3 4.2 %pack_rest.1 = (f32[1,2,5,32,512]{4,3,2,1,0:T(8,128)}, f32[1,2,5,32,512]{4,3,2,1,0:T(8,128)}, f32[1,2,5,32,512]{4,3,2,1,0:T(8,128)}, f32[1,2,5,32,512]{4,3,2,1,0...) custom-call(f32[1,5,16,32,512]{4,3,2,1,0:T(8,128)} %refs_11_.1, ...), custom_call_target="tpu_custom_call" | custom-call | bytes 9699328 | tf_op jit(solution)/shard_map/pack_rest/pallas_call | solution.py:316
  9.5 0.7 collective-permute-start.1
  10.2 1.0 %fusion.1 = (f32[1,2,32,512]{3,2,1,0:T(8,128)S(1)}, f32[1,2,32,512]{3,2,1,0:T(8,128)S(1)}) fusion(f32[2,2,32,512]{3,2,1,0:T(8,128)} %get-tuple-element.59), kind=kLoop, calls=%fused_computation.19 | loop fusion | bytes 524288 | tf_op jit(solution)/shard_map/slice | solution.py:442
  11.6 2.1 %collective-permute-done.refs_4_ = f32[1,2,5,32,512]{4,3,2,1,0:T(8,128)S(1)} collective-permute-done((f32[1,2,5,32,512]{4,3,2,1,0:T(8,128)}, f32[1,2,5,32,512]{4,3,2,1,0:T(8,128)S(1)}, u32[]{:S(2)}, u32[]{:S(2)}) %collective-permute-start) | collective-permute-done | bytes 655392 | tf_op jit(solution)/shard_map/ppermute | solution.py:440
  13.9 1.6 %collective-permute-start.2 = (f32[6,32,512]{2,1,0:T(8,128)S(1)}, f32[6,32,512]{2,1,0:T(8,128)S(1)}, u32[]{:S(2)}, u32[]{:S(2)}) collective-permute-start(f32[6,32,512]{2,1,0:T(8,128)S(1)} %pad_maximum_fusion.1), channel_id=1, source_target_pairs={{0,1},{2,3},{1,0},{3,2},{4,5},{6,7},{5,4},{7,6},{8,9},{10,11},{9,8... | collective-permute-start | bytes 1179656 | tf_op jit(solution)/shard_map/ppermute | solution.py:395
  15.6 0.7 collective-permute-start.3
  16.3 2.5 %collective-permute-start.4 = (f32[1,2,5,32,512]{4,3,2,1,0:T(8,128)S(1)}, f32[1,2,5,32,512]{4,3,2,1,0:T(8,128)S(1)}, u32[]{:S(2)}, u32[]{:S(2)}) collective-permute-start(f32[1,2,5,32,512]{4,3,2,1,0:T(8,128)S(1)} %copy-done.8), channel_id=1, source_target_pairs={{4,0},{8,4},{12,8},{16,12},{20,16},{24,20},{28,24},{0,28},{5,1},{9... | collective-permute-start | bytes 1966088 | tf_op jit(solution)/shard_map/ppermute | solution.py:440
  18.7 2.0 %collective-permute-done.1.refs_5_ = f32[1,2,5,32,512]{4,3,2,1,0:T(8,128)S(1)} collective-permute-done((f32[1,2,5,32,512]{4,3,2,1,0:T(8,128)}, f32[1,2,5,32,512]{4,3,2,1,0:T(8,128)S(1)}, u32[]{:S(2)}, u32[]{:S(2)}) %collective-permute-start.1) | collective-permute-done | bytes 655392 | tf_op jit(solution)/shard_map/ppermute | solution.py:440
  20.9 2.1 %collective-permute-start.5 = (f32[6,32,512]{2,1,0:T(8,128)S(1)}, f32[6,32,512]{2,1,0:T(8,128)S(1)}, u32[]{:S(2)}, u32[]{:S(2)}) collective-permute-start(f32[6,32,512]{2,1,0:T(8,128)S(1)} %pad_maximum_fusion.3), channel_id=1, source_target_pairs={{0,1},{2,3},{1,0},{3,2},{4,5},{6,7},{5,4},{7,6},{8,9},{10,11},{9,8... | collective-permute-start | bytes 1179656 | tf_op jit(solution)/shard_map/ppermute | solution.py:395
  23.0 0.8 collective-permute-start.6
  23.8 2.0 %collective-permute-done.2.refs_4_ = f32[6,32,512]{2,1,0:T(8,128)S(1)} collective-permute-done((f32[6,32,512]{2,1,0:T(8,128)S(1)}, f32[6,32,512]{2,1,0:T(8,128)S(1)}, u32[]{:S(2)}, u32[]{:S(2)}) %collective-permute-start.2) | collective-permute-done | bytes 393248 | tf_op jit(solution)/shard_map/ppermute | solution.py:395
  25.8 1.8 %collective-permute-start.7 = (f32[1,2,5,32,512]{4,3,2,1,0:T(8,128)S(1)}, f32[1,2,5,32,512]{4,3,2,1,0:T(8,128)S(1)}, u32[]{:S(2)}, u32[]{:S(2)}) collective-permute-start(f32[1,2,5,32,512]{4,3,2,1,0:T(8,128)S(1)} %copy-done.7), channel_id=1, source_target_pairs={{4,0},{8,4},{12,8},{16,12},{20,16},{24,20},{28,24},{0,28},{5,1},{9... | collective-permute-start | bytes 1966088 | tf_op jit(solution)/shard_map/ppermute | solution.py:440
  27.6 5.6 %collective-permute-done.5.refs_6_ = f32[6,32,512]{2,1,0:T(8,128)S(1)} collective-permute-done((f32[6,32,512]{2,1,0:T(8,128)S(1)}, f32[6,32,512]{2,1,0:T(8,128)S(1)}, u32[]{:S(2)}, u32[]{:S(2)}) %collective-permute-start.5) | collective-permute-done | bytes 393248 | tf_op jit(solution)/shard_map/ppermute | solution.py:395
  33.2 1.2 %collective-permute-start.8 = (f32[1,2,5,32,512]{4,3,2,1,0:T(8,128)S(1)}, f32[1,2,5,32,512]{4,3,2,1,0:T(8,128)S(1)}, u32[]{:S(2)}, u32[]{:S(2)}) collective-permute-start(f32[1,2,5,32,512]{4,3,2,1,0:T(8,128)S(1)} %copy-done.6), channel_id=1, source_target_pairs={{4,0},{8,4},{12,8},{16,12},{20,16},{24,20},{28,24},{0,28},{5,1},{9... | collective-permute-start | bytes 1966088 | tf_op jit(solution)/shard_map/ppermute | solution.py:440
  35.2 7.9 %collective-permute-start.9 = (f32[5,32,512]{2,1,0:T(8,128)S(1)}, f32[5,32,512]{2,1,0:T(8,128)S(1)}, u32[]{:S(2)}, u32[]{:S(2)}) collective-permute-start(f32[5,32,512]{2,1,0:T(8,128)S(1)} %get-tuple-element.104), channel_id=1, source_target_pairs={{0,1},{2,3},{1,0},{3,2},{4,5},{6,7},{5,4},{7,6},{8,9},{10,11},{9,8... | collective-permute-start | bytes 983048 | tf_op jit(solution)/shard_map/ppermute | solution.py:395
  43.3 5.6 %stage_0_4.1 = (f32[4,408,128]{2,1,0:T(8,128)S(1)}, f32[4,408,128]{2,1,0:T(8,128)S(1)}, f32[4,408,128]{2,1,0:T(8,128)S(1)}, f32[4,408,128]{2,1,0:T(8,128)S(1)}, ...) custom-call(f32[5,5]{1,0:T(8,128)S(1)} %copy-done.1, s32[2]{0:T(128)S(1)} %pad_add_fusion.refs_1_, ...), custom_call_target="tpu_custom_call" | custom-call | tf_op jit(solution)/shard_map/stage_0_4/pallas_call | solution.py:355
  48.9 0.8 collective-permute-done.9.refs_8_
  49.9 3.9 %stage_0_5.1 = (f32[4,408,128]{2,1,0:T(8,128)S(1)}, f32[4,408,128]{2,1,0:T(8,128)S(1)}, f32[4,408,128]{2,1,0:T(8,128)S(1)}) custom-call(f32[5,5]{1,0:T(8,128)S(1)} %copy-done.1, s32[2]{0:T(128)S(1)} %pad_add_fusion.refs_1_, bf16[1536,512]{1,0:T(8,128)(2,1)S(1)} %pad_maximum_fusion.refs_2_, f32[1,16,32,512]{3,2,1,0:T(8,128)S(1)} %copy-done, ...), custom_call_target="tpu_custom_call" | custom-call | tf_op jit(solution)/shard_map/stage_0_5/pallas_call | solution.py:355
  53.9 1.7 %collective-permute-start.11 = (f32[1,2,5,32,512]{4,3,2,1,0:T(8,128)S(1)}, f32[1,2,5,32,512]{4,3,2,1,0:T(8,128)S(1)}, u32[]{:S(2)}, u32[]{:S(2)}) collective-permute-start(f32[1,2,5,32,512]{4,3,2,1,0:T(8,128)S(1)} %copy-done.3), channel_id=1, source_target_pairs={{4,0},{8,4},{12,8},{16,12},{20,16},{24,20},{28,24},{0,28},{5,1},{9... | collective-permute-start | bytes 1966088 | tf_op jit(solution)/shard_map/ppermute | solution.py:440
  55.5 10.7 %stage_m3_5.1 = (f32[1,5,16,32,512]{4,3,2,1,0:T(8,128)}, f32[4,408,128]{2,1,0:T(8,128)S(1)}) custom-call(f32[5,5]{1,0:T(8,128)S(1)} %copy-done.1, s32[2]{0:T(128)S(1)} %pad_add_fusion.refs_1_, bf16[1536,512]{1,0:T(8,128)(2,1)S(1)} %pad_maximum_fusion.refs_2_, f32[1,16,32,512]{3,2,1,0:T(8,128)S(1)} %copy-done, ...), custom_call_target="tpu_custom_call" | custom-call | tf_op jit(solution)/shard_map/stage_m3_5/pallas_call | solution.py:355
  66.3 9.1 %stage_m3_7.1 = (f32[1,5,16,32,512]{4,3,2,1,0:T(8,128)}, f32[4,408,128]{2,1,0:T(8,128)S(1)}, f32[4,408,128]{2,1,0:T(8,128)S(1)}, f32[4,408,128]{2,1,0:T(8,128)S(...) custom-call(f32[5,5]{1,0:T(8,128)S(1)} %copy-done.1, ...), custom_call_target="tpu_custom_call", output_to_operand_aliasing={{0}: (13, {})} | custom-call | tf_op jit(solution)/shard_map/stage_m3_7/pallas_call | solution.py:355
  75.4 9.9 %stage_m3_8.1 = f32[1,5,16,32,512]{4,3,2,1,0:T(8,128)} custom-call(f32[5,5]{1,0:T(8,128)S(1)} %copy-done.1, s32[2]{0:T(128)S(1)} %pad_add_fusion.refs_1_, bf16[1536,512]{1,0:T(8,128)(2,1)S(1)} %pad_maximum_fusion.refs_2_, f32[1,16,32,512]{3,2,1,0:T(8,128)S(1)} %copy-done, ...), custom_call_target="tpu_custom_call", output_to_operand_aliasing={{}: (12, {})} | custom-call | tf_op jit(solution)/shard_map/stage_m3_8/pallas_call | solution.py:355
  (47 shorter events, 1.6 us)
Async XLA Ops:
  1.9 9.3 %copy-start.2 = (f32[512,512]{1,0:T(8,128)S(1)}, f32[512,512]{1,0:T(8,128)}, u32[]{:S(2)}) copy-start(f32[512,512]{1,0:T(8,128)} %param.6) | copy-start | bytes 3145732
  1.9 11.8 %collective-permute-start = (f32[1,2,5,32,512]{4,3,2,1,0:T(8,128)}, f32[1,2,5,32,512]{4,3,2,1,0:T(8,128)S(1)}, u32[]{:S(2)}, u32[]{:S(2)}) collective-permute-start(f32[1,2,5,32,512]{4,3,2,1,0:T(8,128)} %pack_first.1.first), channel_id=1, source_target_pairs={{4,0},{8,4},{12,8},{16,12},{20,16},{24,20},{28,24},{0,28},{5,1},{9... | collective-permute-start | bytes 1966088 | tf_op jit(solution)/shard_map/ppermute | solution.py:440
  9.5 11.3 %collective-permute-start.1 = (f32[1,2,5,32,512]{4,3,2,1,0:T(8,128)}, f32[1,2,5,32,512]{4,3,2,1,0:T(8,128)S(1)}, u32[]{:S(2)}, u32[]{:S(2)}) collective-permute-start(f32[1,2,5,32,512]{4,3,2,1,0:T(8,128)} %get-tuple-element.58), channel_id=1, source_target_pairs={{4,0},{8,4},{12,8},{16,12},{20,16},{24,20},{28,24},{0,28},{5,1},{9... | collective-permute-start | bytes 1966088 | tf_op jit(solution)/shard_map/ppermute | solution.py:440
  11.4 4.8 %copy-start.8 = (f32[1,2,5,32,512]{4,3,2,1,0:T(8,128)S(1)}, f32[1,2,5,32,512]{4,3,2,1,0:T(8,128)}, u32[]{:S(2)}) copy-start(f32[1,2,5,32,512]{4,3,2,1,0:T(8,128)} %get-tuple-element.61) | copy-start | bytes 1966084
  11.6 14.3 %copy-start.7 = (f32[1,2,5,32,512]{4,3,2,1,0:T(8,128)S(1)}, f32[1,2,5,32,512]{4,3,2,1,0:T(8,128)}, u32[]{:S(2)}) copy-start(f32[1,2,5,32,512]{4,3,2,1,0:T(8,128)} %get-tuple-element.63) | copy-start | bytes 1966084
  11.6 21.6 %copy-start.6 = (f32[1,2,5,32,512]{4,3,2,1,0:T(8,128)S(1)}, f32[1,2,5,32,512]{4,3,2,1,0:T(8,128)}, u32[]{:S(2)}) copy-start(f32[1,2,5,32,512]{4,3,2,1,0:T(8,128)} %get-tuple-element.66) | copy-start | bytes 1966084
  13.8 29.4 %copy-start.5 = (f32[1,2,5,32,512]{4,3,2,1,0:T(8,128)S(1)}, f32[1,2,5,32,512]{4,3,2,1,0:T(8,128)}, u32[]{:S(2)}) copy-start(f32[1,2,5,32,512]{4,3,2,1,0:T(8,128)} %get-tuple-element.79) | copy-start | bytes 1966084
  13.8 29.4 %copy-start = (f32[1,16,32,512]{3,2,1,0:T(8,128)S(1)}, f32[1,16,32,512]{3,2,1,0:T(8,128)}, u32[]{:S(2)}) copy-start(f32[1,16,32,512]{3,2,1,0:T(8,128)} %refs_3_.9) | copy-start | bytes 3145732
  13.8 29.4 %copy-start.1 = (f32[5,5]{1,0:T(8,128)S(1)}, f32[5,5]{1,0:T(8,128)}, u32[]{:S(2)}) copy-start(f32[5,5]{1,0:T(8,128)} %refs_0_.9) | copy-start | bytes 304
  13.9 12.0 %collective-permute-start.2 = (f32[6,32,512]{2,1,0:T(8,128)S(1)}, f32[6,32,512]{2,1,0:T(8,128)S(1)}, u32[]{:S(2)}, u32[]{:S(2)}) collective-permute-start(f32[6,32,512]{2,1,0:T(8,128)S(1)} %pad_maximum_fusion.1), channel_id=1, source_target_pairs={{0,1},{2,3},{1,0},{3,2},{4,5},{6,7},{5,4},{7,6},{8,9},{10,11},{9,8... | collective-permute-start | bytes 1179656 | tf_op jit(solution)/shard_map/ppermute | solution.py:395
  15.6 10.3 %collective-permute-start.3 = (f32[6,32,512]{2,1,0:T(8,128)S(1)}, f32[6,32,512]{2,1,0:T(8,128)S(1)}, u32[]{:S(2)}, u32[]{:S(2)}) collective-permute-start(f32[6,32,512]{2,1,0:T(8,128)S(1)} %pad_maximum_fusion.2), channel_id=1, source_target_pairs={{1,2},{2,1},{5,6},{6,5},{9,10},{10,9},{13,14},{14,13},{17,18},{18,... | collective-permute-start | bytes 1179656 | tf_op jit(solution)/shard_map/ppermute | solution.py:395
  16.3 16.9 %collective-permute-start.4 = (f32[1,2,5,32,512]{4,3,2,1,0:T(8,128)S(1)}, f32[1,2,5,32,512]{4,3,2,1,0:T(8,128)S(1)}, u32[]{:S(2)}, u32[]{:S(2)}) collective-permute-start(f32[1,2,5,32,512]{4,3,2,1,0:T(8,128)S(1)} %copy-done.8), channel_id=1, source_target_pairs={{4,0},{8,4},{12,8},{16,12},{20,16},{24,20},{28,24},{0,28},{5,1},{9... | collective-permute-start | bytes 1966088 | tf_op jit(solution)/shard_map/ppermute | solution.py:440
  20.9 12.3 %collective-permute-start.5 = (f32[6,32,512]{2,1,0:T(8,128)S(1)}, f32[6,32,512]{2,1,0:T(8,128)S(1)}, u32[]{:S(2)}, u32[]{:S(2)}) collective-permute-start(f32[6,32,512]{2,1,0:T(8,128)S(1)} %pad_maximum_fusion.3), channel_id=1, source_target_pairs={{0,1},{2,3},{1,0},{3,2},{4,5},{6,7},{5,4},{7,6},{8,9},{10,11},{9,8... | collective-permute-start | bytes 1179656 | tf_op jit(solution)/shard_map/ppermute | solution.py:395
  23.0 32.6 %slice-start = ((s8[5242880]{0:T(1024)(128)(4,1)}), s8[4194304]{0:T(1024)(128)(4,1)S(1)}, s32[]{:S(2)}) async-start(s8[5242880]{0:T(1024)(128)(4,1)} %bitcast.21), calls=%async_computation | async-start | bytes 8388608
  23.0 10.2 %collective-permute-start.6 = (f32[6,32,512]{2,1,0:T(8,128)S(1)}, f32[6,32,512]{2,1,0:T(8,128)S(1)}, u32[]{:S(2)}, u32[]{:S(2)}) collective-permute-start(f32[6,32,512]{2,1,0:T(8,128)S(1)} %pad_maximum_fusion.4), channel_id=1, source_target_pairs={{1,2},{2,1},{5,6},{6,5},{9,10},{10,9},{13,14},{14,13},{17,18},{18,... | collective-permute-start | bytes 1179656 | tf_op jit(solution)/shard_map/ppermute | solution.py:395
  25.8 17.3 %collective-permute-start.7 = (f32[1,2,5,32,512]{4,3,2,1,0:T(8,128)S(1)}, f32[1,2,5,32,512]{4,3,2,1,0:T(8,128)S(1)}, u32[]{:S(2)}, u32[]{:S(2)}) collective-permute-start(f32[1,2,5,32,512]{4,3,2,1,0:T(8,128)S(1)} %copy-done.7), channel_id=1, source_target_pairs={{4,0},{8,4},{12,8},{16,12},{20,16},{24,20},{28,24},{0,28},{5,1},{9... | collective-permute-start | bytes 1966088 | tf_op jit(solution)/shard_map/ppermute | solution.py:440
  33.2 16.6 %copy-start.4 = (f32[1,2,5,32,512]{4,3,2,1,0:T(8,128)S(1)}, f32[1,2,5,32,512]{4,3,2,1,0:T(8,128)}, u32[]{:S(2)}) copy-start(f32[1,2,5,32,512]{4,3,2,1,0:T(8,128)} %get-tuple-element.80) | copy-start | bytes 1966084
  33.2 16.7 %collective-permute-start.8 = (f32[1,2,5,32,512]{4,3,2,1,0:T(8,128)S(1)}, f32[1,2,5,32,512]{4,3,2,1,0:T(8,128)S(1)}, u32[]{:S(2)}, u32[]{:S(2)}) collective-permute-start(f32[1,2,5,32,512]{4,3,2,1,0:T(8,128)S(1)} %copy-done.6), channel_id=1, source_target_pairs={{4,0},{8,4},{12,8},{16,12},{20,16},{24,20},{28,24},{0,28},{5,1},{9... | collective-permute-start | bytes 1966088 | tf_op jit(solution)/shard_map/ppermute | solution.py:440
  34.5 14.4 %collective-permute-start.10 = (f32[5,32,512]{2,1,0:T(8,128)S(1)}, f32[5,32,512]{2,1,0:T(8,128)S(1)}, u32[]{:S(2)}, u32[]{:S(2)}) collective-permute-start(f32[5,32,512]{2,1,0:T(8,128)S(1)} %get-tuple-element.103), channel_id=1, source_target_pairs={{1,2},{2,1},{5,6},{6,5},{9,10},{10,9},{13,14},{14,13},{17,18},{18,... | collective-permute-start | bytes 983048 | tf_op jit(solution)/shard_map/ppermute | solution.py:395
  35.2 14.6 %collective-permute-start.9 = (f32[5,32,512]{2,1,0:T(8,128)S(1)}, f32[5,32,512]{2,1,0:T(8,128)S(1)}, u32[]{:S(2)}, u32[]{:S(2)}) collective-permute-start(f32[5,32,512]{2,1,0:T(8,128)S(1)} %get-tuple-element.104), channel_id=1, source_target_pairs={{0,1},{2,3},{1,0},{3,2},{4,5},{6,7},{5,4},{7,6},{8,9},{10,11},{9,8... | collective-permute-start | bytes 983048 | tf_op jit(solution)/shard_map/ppermute | solution.py:395
  43.2 12.4 %slice-start.1 = ((s8[5242880]{0:T(1024)(128)(4,1)}), s8[1048576]{0:T(1024)(128)(4,1)S(1)}, s32[]{:S(2)}) async-start(s8[5242880]{0:T(1024)(128)(4,1)} %bitcast.21), calls=%async_computation.1 | async-start | bytes 2097152
  43.2 23.1 %collective-permute-start.12 = (f32[1,2,5,32,512]{4,3,2,1,0:T(8,128)S(1)}, f32[1,2,5,32,512]{4,3,2,1,0:T(8,128)S(1)}, u32[]{:S(2)}, u32[]{:S(2)}) collective-permute-start(f32[1,2,5,32,512]{4,3,2,1,0:T(8,128)S(1)} %copy-done.5), channel_id=1, source_target_pairs={{4,0},{8,4},{12,8},{16,12},{20,16},{24,20},{28,24},{0,28},{5,1},{9... | collective-permute-start | bytes 1966088 | tf_op jit(solution)/shard_map/ppermute | solution.py:440
  49.8 16.6 %collective-permute-start.13 = (f32[1,2,5,32,512]{4,3,2,1,0:T(8,128)S(1)}, f32[1,2,5,32,512]{4,3,2,1,0:T(8,128)S(1)}, u32[]{:S(2)}, u32[]{:S(2)}) collective-permute-start(f32[1,2,5,32,512]{4,3,2,1,0:T(8,128)S(1)} %copy-done.4), channel_id=1, source_target_pairs={{4,0},{8,4},{12,8},{16,12},{20,16},{24,20},{28,24},{0,28},{5,1},{9... | collective-permute-start | bytes 1966088 | tf_op jit(solution)/shard_map/ppermute | solution.py:440
  53.9 21.6 %collective-permute-start.11 = (f32[1,2,5,32,512]{4,3,2,1,0:T(8,128)S(1)}, f32[1,2,5,32,512]{4,3,2,1,0:T(8,128)S(1)}, u32[]{:S(2)}, u32[]{:S(2)}) collective-permute-start(f32[1,2,5,32,512]{4,3,2,1,0:T(8,128)S(1)} %copy-done.3), channel_id=1, source_target_pairs={{4,0},{8,4},{12,8},{16,12},{20,16},{24,20},{28,24},{0,28},{5,1},{9... | collective-permute-start | bytes 1966088 | tf_op jit(solution)/shard_map/ppermute | solution.py:440
  (1 other events, 3.9 us)

commit v6 on v5

--- a/solution.py
+++ b/solution.py
@@ -104,7 +104,7 @@
         del refs[:count]
         return got
 
-    (coupling, odd_ref, weights_in, sensor) = take(4)
+    (coupling, odd_ref, weights, sensor) = take(4)
     chunks = take(len(groups))
     halos = take(2 * STEPS) if stage.halos else []
     filtered = dict(zip(stage.taken, take(len(stage.taken))))
@@ -113,7 +113,7 @@
     take(1 if aliased else 0)
     (out,) = take(1) if outs else [None]
     fresh = dict(zip(stage.given, take(len(stage.given))))
-    (result, weights) = take(2)
+    (result,) = take(1)
     fresh.update(zip(stage.kept, take(len(stage.kept))))
     filtered.update(fresh)
     highs = take(2)
@@ -134,14 +134,6 @@
                 ref[b, pl.ds(pl.multiple_of(i * stride, PAD), PAD)] = blank
 
         pl.loop(0, sides + 1)(clear)
-
-    step = 4 * ROWS
-
-    def fetch(i):
-        at = pl.ds(pl.multiple_of(i * step, step), step)
-        weights[at] = weights_in[at]
-
-    pl.loop(0, weights.shape[0] // step)(fetch)
 
     lane = lax.broadcasted_iota(jnp.int32, (ROWS, LANES), 1)
     at_start = lane == 0
@@ -347,7 +339,6 @@
     written = [jax.ShapeDtypeStruct(own.shape, jnp.float32)] if outs else []
     scratch = [
         pltpu.VMEM((max(outs, 1), 2, fields, nth, nr), jnp.float32),
-        pltpu.VMEM(weights.shape, weights.dtype),
         *[pltpu.VMEM(slot, jnp.float32)] * len(stage.kept),
         *[pltpu.VMEM((sides * nth, nr), jnp.bfloat16)] * 4,
     ]
@@ -386,11 +377,13 @@
 
     odd = lax.rem(lax.axis_index("gx"), 2)
 
-    def swapped(edges):
+    def swapped(edges, after=None):
         result = []
         for parity in range(2):
             pairs = [(i, i + 1) for i in range(parity, slabs - 1, 2)]
             side = 1 - odd if parity == 0 else odd
+            if parity and after is not None:
+                chunks[after], *edges = lax.optimization_barrier((chunks[after], *edges))
             mine = jnp.concatenate([lax.dynamic_index_in_dim(part, side, 0, keepdims=False) for part in edges])
             result.append(lax.ppermute(mine, "gx", pairs + [(j, i) for i, j in pairs]))
         return result
@@ -440,7 +433,7 @@
         chunks.append(lax.ppermute(packed, "seg", back))
         if 1 <= i <= STEPS:
             edges = [chunks[i - 1][0]] + ([sensor_edges[i - 1][:, None]] if i < STEPS else [])
-            exchanged.append(swapped(edges))
+            exchanged.append(swapped(edges, i if i == STEPS else None))
     halos = sum(exchanged, [])
     for number in range(ran, len(stages)):
         run(number)

time: 85.7 us -> 87.9 us (1.026)
  starting transfers between devices: 25.4 us -> 28.4 us
  Pallas kernels: 45.3 us -> 44.4 us
    ppermute x8, starting transfers between devices: 11.5 us -> 13 us  [shards(): chunks.append(lax.ppermute(packed, 'seg', back))]
    ppermute x6, starting transfers between devices: 13.9 us -> 15.3 us  [swapped(): result.append(lax.ppermute(mine, 'gx', pairs + [(j, i) for i, j in pairs]))]
    pallas_call x5, Pallas kernels: 39.2 us -> 38.3 us  [run_stage(): pl.pallas_call(functools.partial(stage_kernel, stage, fields, planes, ali...]
  transfers between devices with their start and end apart: 14 -> 14, of which waited for: 5 -> 5; matrix products, arithmetic and copies ran while one was open for 2% -> 2% of each run, Pallas kernels for 39% -> 38%
where the time goes in v6:
time: 87.9 us; the launch traced here: 86.9 us
  Pallas kernels  44.4 us (51%)
  starting transfers between devices  28.4 us (32%)
  waiting for transfers between devices  12 us (14%)
  local copies, waits for them, and re-layouts  1.2 us (1%)
    pallas_call x5, Pallas kernels, run_stage(): pl.pallas_call(functools.partial(stage_kernel, stage, fields, planes, ali...  38.3 us
    ppermute x6, starting transfers between devices, swapped(): result.append(lax.ppermute(mine, 'gx', pairs + [(j, i) for i, j in pairs]))  15.3 us
    ppermute x8, starting transfers between devices, shards(): chunks.append(lax.ppermute(packed, 'seg', back))  13 us
    ppermute x6, waiting for transfers between devices, swapped(): result.append(lax.ppermute(mine, 'gx', pairs + [(j, i) for i, j in pairs]))  7.87 us
    pallas_call x1, Pallas kernels, pack_rest(): pl.pallas_call(functools.partial(pack_rest_kernel, planes, groups), out_s...  4.17 us
    ppermute x8, waiting for transfers between devices, shards(): chunks.append(lax.ppermute(packed, 'seg', back))  4.08 us
    pallas_call x1, Pallas kernels, pack_first(): pl.pallas_call(functools.partial(pack_first_kernel, planes), out_shape=ja...  1.92 us
  transfers between devices with their start and end apart: 14, of which 5 were waited for; matrix products, arithmetic and copies ran while one was open for 2% of the time, Pallas kernels for 38%

profile of v6, /device:TPU:0, one launch (start us, length us, event | category | flops | bytes accessed | tf_op | source)
XLA Modules:
  0.0 86.9 jit_solution(11402471881500262213)
XLA Ops:
  0.0 1.9 %pack_first.1.first = f32[1,2,5,32,512]{4,3,2,1,0:T(8,128)} custom-call(f32[1,5,16,32,512]{4,3,2,1,0:T(8,128)} %refs_11_.1), custom_call_target="tpu_custom_call" | custom-call | tf_op jit(solution)/shard_map/pack_first/pallas_call | solution.py:291
  1.9 3.4 %collective-permute-start = (f32[1,2,5,32,512]{4,3,2,1,0:T(8,128)}, f32[1,2,5,32,512]{4,3,2,1,0:T(8,128)S(1)}, u32[]{:S(2)}, u32[]{:S(2)}) collective-permute-start(f32[1,2,5,32,512]{4,3,2,1,0:T(8,128)} %pack_first.1.first), channel_id=1, source_target_pairs={{4,0},{8,4},{12,8},{16,12},{20,16},{24,20},{28,24},{0,28},{5,1},{9... | collective-permute-start | bytes 1966088 | tf_op jit(solution)/shard_map/ppermute | solution.py:433
  5.3 4.2 %pack_rest.1 = (f32[1,2,5,32,512]{4,3,2,1,0:T(8,128)}, f32[1,2,5,32,512]{4,3,2,1,0:T(8,128)}, f32[1,2,5,32,512]{4,3,2,1,0:T(8,128)}, f32[1,2,5,32,512]{4,3,2,1,0...) custom-call(f32[1,5,16,32,512]{4,3,2,1,0:T(8,128)} %refs_11_.1, ...), custom_call_target="tpu_custom_call" | custom-call | bytes 9699328 | tf_op jit(solution)/shard_map/pack_rest/pallas_call | solution.py:308
  10.2 1.0 %fusion.1 = (f32[1,2,32,512]{3,2,1,0:T(8,128)S(1)}, f32[1,2,32,512]{3,2,1,0:T(8,128)S(1)}) fusion(f32[2,2,32,512]{3,2,1,0:T(8,128)} %get-tuple-element.61), kind=kLoop, calls=%fused_computation.19 | loop fusion | bytes 524288 | tf_op jit(solution)/shard_map/slice | solution.py:435
  11.4 2.3 %collective-permute-done.refs_4_ = f32[1,2,5,32,512]{4,3,2,1,0:T(8,128)S(1)} collective-permute-done((f32[1,2,5,32,512]{4,3,2,1,0:T(8,128)}, f32[1,2,5,32,512]{4,3,2,1,0:T(8,128)S(1)}, u32[]{:S(2)}, u32[]{:S(2)}) %collective-permute-start) | collective-permute-done | bytes 655392 | tf_op jit(solution)/shard_map/ppermute | solution.py:433
  13.8 1.6 %collective-permute-start.2 = (f32[6,32,512]{2,1,0:T(8,128)S(1)}, f32[6,32,512]{2,1,0:T(8,128)S(1)}, u32[]{:S(2)}, u32[]{:S(2)}) collective-permute-start(f32[6,32,512]{2,1,0:T(8,128)S(1)} %pad_maximum_fusion.1), channel_id=1, source_target_pairs={{0,1},{2,3},{1,0},{3,2},{4,5},{6,7},{5,4},{7,6},{8,9},{10,11},{9,8... | collective-permute-start | bytes 1179656 | tf_op jit(solution)/shard_map/ppermute | solution.py:388
  15.5 0.8 collective-permute-start.3
  16.5 2.5 %collective-permute-start.4 = (f32[1,2,5,32,512]{4,3,2,1,0:T(8,128)S(1)}, f32[1,2,5,32,512]{4,3,2,1,0:T(8,128)S(1)}, u32[]{:S(2)}, u32[]{:S(2)}) collective-permute-start(f32[1,2,5,32,512]{4,3,2,1,0:T(8,128)S(1)} %copy-done.8), channel_id=1, source_target_pairs={{4,0},{8,4},{12,8},{16,12},{20,16},{24,20},{28,24},{0,28},{5,1},{9... | collective-permute-start | bytes 1966088 | tf_op jit(solution)/shard_map/ppermute | solution.py:433
  19.0 1.8 %collective-permute-done.1.refs_5_ = f32[1,2,5,32,512]{4,3,2,1,0:T(8,128)S(1)} collective-permute-done((f32[1,2,5,32,512]{4,3,2,1,0:T(8,128)}, f32[1,2,5,32,512]{4,3,2,1,0:T(8,128)S(1)}, u32[]{:S(2)}, u32[]{:S(2)}) %collective-permute-start.1) | collective-permute-done | bytes 655392 | tf_op jit(solution)/shard_map/ppermute | solution.py:433
  20.9 2.4 %collective-permute-start.5 = (f32[6,32,512]{2,1,0:T(8,128)S(1)}, f32[6,32,512]{2,1,0:T(8,128)S(1)}, u32[]{:S(2)}, u32[]{:S(2)}) collective-permute-start(f32[6,32,512]{2,1,0:T(8,128)S(1)} %pad_maximum_fusion.3), channel_id=1, source_target_pairs={{0,1},{2,3},{1,0},{3,2},{4,5},{6,7},{5,4},{7,6},{8,9},{10,11},{9,8... | collective-permute-start | bytes 1179656 | tf_op jit(solution)/shard_map/ppermute | solution.py:388
  23.3 2.5 %collective-permute-done.2.refs_4_ = f32[6,32,512]{2,1,0:T(8,128)S(1)} collective-permute-done((f32[6,32,512]{2,1,0:T(8,128)S(1)}, f32[6,32,512]{2,1,0:T(8,128)S(1)}, u32[]{:S(2)}, u32[]{:S(2)}) %collective-permute-start.2) | collective-permute-done | bytes 393248 | tf_op jit(solution)/shard_map/ppermute | solution.py:388
  25.8 1.8 %collective-permute-start.7 = (f32[1,2,5,32,512]{4,3,2,1,0:T(8,128)S(1)}, f32[1,2,5,32,512]{4,3,2,1,0:T(8,128)S(1)}, u32[]{:S(2)}, u32[]{:S(2)}) collective-permute-start(f32[1,2,5,32,512]{4,3,2,1,0:T(8,128)S(1)} %copy-done.7), channel_id=1, source_target_pairs={{4,0},{8,4},{12,8},{16,12},{20,16},{24,20},{28,24},{0,28},{5,1},{9... | collective-permute-start | bytes 1966088 | tf_op jit(solution)/shard_map/ppermute | solution.py:433
  27.6 0.8 collective-permute-start.6
  28.4 4.7 %collective-permute-done.5.refs_6_ = f32[6,32,512]{2,1,0:T(8,128)S(1)} collective-permute-done((f32[6,32,512]{2,1,0:T(8,128)S(1)}, f32[6,32,512]{2,1,0:T(8,128)S(1)}, u32[]{:S(2)}, u32[]{:S(2)}) %collective-permute-start.5) | collective-permute-done | bytes 393248 | tf_op jit(solution)/shard_map/ppermute | solution.py:388
  33.2 1.2 %collective-permute-start.8 = (f32[1,2,5,32,512]{4,3,2,1,0:T(8,128)S(1)}, f32[1,2,5,32,512]{4,3,2,1,0:T(8,128)S(1)}, u32[]{:S(2)}, u32[]{:S(2)}) collective-permute-start(f32[1,2,5,32,512]{4,3,2,1,0:T(8,128)S(1)} %copy-done.6), channel_id=1, source_target_pairs={{4,0},{8,4},{12,8},{16,12},{20,16},{24,20},{28,24},{0,28},{5,1},{9... | collective-permute-start | bytes 1966088 | tf_op jit(solution)/shard_map/ppermute | solution.py:433
  34.4 9.0 %collective-permute-start.9 = (f32[5,32,512]{2,1,0:T(8,128)S(1)}, f32[5,32,512]{2,1,0:T(8,128)S(1)}, u32[]{:S(2)}, u32[]{:S(2)}) collective-permute-start(f32[5,32,512]{2,1,0:T(8,128)S(1)} %dynamic-slice_bitcast_fusion.1), channel_id=1, source_target_pairs={{0,1},{2,3},{1,0},{3,2},{4,5},{6,7},{5,4},{7,6},{8,9},{10,11},{9,8... | collective-permute-start | bytes 983048 | tf_op jit(solution)/shard_map/ppermute | solution.py:388
  44.2 1.5 %collective-permute-start.12 = (f32[1,2,5,32,512]{4,3,2,1,0:T(8,128)S(1)}, f32[1,2,5,32,512]{4,3,2,1,0:T(8,128)S(1)}, u32[]{:S(2)}, u32[]{:S(2)}) collective-permute-start(f32[1,2,5,32,512]{4,3,2,1,0:T(8,128)S(1)} %copy-done.5), channel_id=1, source_target_pairs={{4,0},{8,4},{12,8},{16,12},{20,16},{24,20},{28,24},{0,28},{5,1},{9... | collective-permute-start | bytes 1966088 | tf_op jit(solution)/shard_map/ppermute | solution.py:433
  45.7 5.4 %stage_0_4.1 = (f32[4,408,128]{2,1,0:T(8,128)S(1)}, f32[4,408,128]{2,1,0:T(8,128)S(1)}, f32[4,408,128]{2,1,0:T(8,128)S(1)}, f32[4,408,128]{2,1,0:T(8,128)S(1)}, ...) custom-call(f32[5,5]{1,0:T(8,128)S(1)} %copy-done.1, s32[2]{0:T(128)S(1)} %pad_add_fusion.refs_1_, ...), custom_call_target="tpu_custom_call" | custom-call | tf_op jit(solution)/shard_map/stage_0_4/pallas_call | solution.py:346
  51.8 1.0 %collective-permute-start.13 = (f32[1,2,5,32,512]{4,3,2,1,0:T(8,128)S(1)}, f32[1,2,5,32,512]{4,3,2,1,0:T(8,128)S(1)}, u32[]{:S(2)}, u32[]{:S(2)}) collective-permute-start(f32[1,2,5,32,512]{4,3,2,1,0:T(8,128)S(1)} %copy-done.4), channel_id=1, source_target_pairs={{4,0},{8,4},{12,8},{16,12},{20,16},{24,20},{28,24},{0,28},{5,1},{9... | collective-permute-start | bytes 1966088 | tf_op jit(solution)/shard_map/ppermute | solution.py:433
  52.8 3.7 %stage_0_5.1 = (f32[4,408,128]{2,1,0:T(8,128)S(1)}, f32[4,408,128]{2,1,0:T(8,128)S(1)}, f32[4,408,128]{2,1,0:T(8,128)S(1)}) custom-call(f32[5,5]{1,0:T(8,128)S(1)} %copy-done.1, s32[2]{0:T(128)S(1)} %pad_add_fusion.refs_1_, bf16[1536,512]{1,0:T(8,128)(2,1)S(1)} %pad_maximum_fusion.refs_2_, f32[1,16,32,512]{3,2,1,0:T(8,128)S(1)} %copy-done, ...), custom_call_target="tpu_custom_call" | custom-call | tf_op jit(solution)/shard_map/stage_0_5/pallas_call | solution.py:346
  56.5 1.0 %collective-permute-start.11 = (f32[1,2,5,32,512]{4,3,2,1,0:T(8,128)S(1)}, f32[1,2,5,32,512]{4,3,2,1,0:T(8,128)S(1)}, u32[]{:S(2)}, u32[]{:S(2)}) collective-permute-start(f32[1,2,5,32,512]{4,3,2,1,0:T(8,128)S(1)} %copy-done.3), channel_id=1, source_target_pairs={{4,0},{8,4},{12,8},{16,12},{20,16},{24,20},{28,24},{0,28},{5,1},{9... | collective-permute-start | bytes 1966088 | tf_op jit(solution)/shard_map/ppermute | solution.py:433
  57.5 10.5 %stage_m3_5.1 = (f32[1,5,16,32,512]{4,3,2,1,0:T(8,128)}, f32[4,408,128]{2,1,0:T(8,128)S(1)}) custom-call(f32[5,5]{1,0:T(8,128)S(1)} %copy-done.1, s32[2]{0:T(128)S(1)} %pad_add_fusion.refs_1_, bf16[1536,512]{1,0:T(8,128)(2,1)S(1)} %pad_maximum_fusion.refs_2_, f32[1,16,32,512]{3,2,1,0:T(8,128)S(1)} %copy-done, ...), custom_call_target="tpu_custom_call" | custom-call | tf_op jit(solution)/shard_map/stage_m3_5/pallas_call | solution.py:346
  68.1 8.9 %stage_m3_7.1 = (f32[1,5,16,32,512]{4,3,2,1,0:T(8,128)}, f32[4,408,128]{2,1,0:T(8,128)S(1)}, f32[4,408,128]{2,1,0:T(8,128)S(1)}, f32[4,408,128]{2,1,0:T(8,128)S(...) custom-call(f32[5,5]{1,0:T(8,128)S(1)} %copy-done.1, ...), custom_call_target="tpu_custom_call", output_to_operand_aliasing={{0}: (13, {})} | custom-call | tf_op jit(solution)/shard_map/stage_m3_7/pallas_call | solution.py:346
  76.9 9.7 %stage_m3_8.1 = f32[1,5,16,32,512]{4,3,2,1,0:T(8,128)} custom-call(f32[5,5]{1,0:T(8,128)S(1)} %copy-done.1, s32[2]{0:T(128)S(1)} %pad_add_fusion.refs_1_, bf16[1536,512]{1,0:T(8,128)(2,1)S(1)} %pad_maximum_fusion.refs_2_, f32[1,16,32,512]{3,2,1,0:T(8,128)S(1)} %copy-done, ...), custom_call_target="tpu_custom_call", output_to_operand_aliasing={{}: (12, {})} | custom-call | tf_op jit(solution)/shard_map/stage_m3_8/pallas_call | solution.py:346
  (48 shorter events, 2.7 us)
Async XLA Ops:
  1.9 9.3 %copy-start.2 = (f32[512,512]{1,0:T(8,128)S(1)}, f32[512,512]{1,0:T(8,128)}, u32[]{:S(2)}) copy-start(f32[512,512]{1,0:T(8,128)} %param.6) | copy-start | bytes 3145732
  1.9 11.8 %collective-permute-start = (f32[1,2,5,32,512]{4,3,2,1,0:T(8,128)}, f32[1,2,5,32,512]{4,3,2,1,0:T(8,128)S(1)}, u32[]{:S(2)}, u32[]{:S(2)}) collective-permute-start(f32[1,2,5,32,512]{4,3,2,1,0:T(8,128)} %pack_first.1.first), channel_id=1, source_target_pairs={{4,0},{8,4},{12,8},{16,12},{20,16},{24,20},{28,24},{0,28},{5,1},{9... | collective-permute-start | bytes 1966088 | tf_op jit(solution)/shard_map/ppermute | solution.py:433
  9.5 11.3 %collective-permute-start.1 = (f32[1,2,5,32,512]{4,3,2,1,0:T(8,128)}, f32[1,2,5,32,512]{4,3,2,1,0:T(8,128)S(1)}, u32[]{:S(2)}, u32[]{:S(2)}) collective-permute-start(f32[1,2,5,32,512]{4,3,2,1,0:T(8,128)} %get-tuple-element.60), channel_id=1, source_target_pairs={{4,0},{8,4},{12,8},{16,12},{20,16},{24,20},{28,24},{0,28},{5,1},{9... | collective-permute-start | bytes 1966088 | tf_op jit(solution)/shard_map/ppermute | solution.py:433
  11.4 5.1 %copy-start.8 = (f32[1,2,5,32,512]{4,3,2,1,0:T(8,128)S(1)}, f32[1,2,5,32,512]{4,3,2,1,0:T(8,128)}, u32[]{:S(2)}) copy-start(f32[1,2,5,32,512]{4,3,2,1,0:T(8,128)} %get-tuple-element.63) | copy-start | bytes 1966084
  13.8 12.0 %copy-start.7 = (f32[1,2,5,32,512]{4,3,2,1,0:T(8,128)S(1)}, f32[1,2,5,32,512]{4,3,2,1,0:T(8,128)}, u32[]{:S(2)}) copy-start(f32[1,2,5,32,512]{4,3,2,1,0:T(8,128)} %get-tuple-element.65) | copy-start | bytes 1966084
  13.8 11.9 %collective-permute-start.2 = (f32[6,32,512]{2,1,0:T(8,128)S(1)}, f32[6,32,512]{2,1,0:T(8,128)S(1)}, u32[]{:S(2)}, u32[]{:S(2)}) collective-permute-start(f32[6,32,512]{2,1,0:T(8,128)S(1)} %pad_maximum_fusion.1), channel_id=1, source_target_pairs={{0,1},{2,3},{1,0},{3,2},{4,5},{6,7},{5,4},{7,6},{8,9},{10,11},{9,8... | collective-permute-start | bytes 1179656 | tf_op jit(solution)/shard_map/ppermute | solution.py:388
  15.5 17.7 %copy-start.6 = (f32[1,2,5,32,512]{4,3,2,1,0:T(8,128)S(1)}, f32[1,2,5,32,512]{4,3,2,1,0:T(8,128)}, u32[]{:S(2)}) copy-start(f32[1,2,5,32,512]{4,3,2,1,0:T(8,128)} %get-tuple-element.69) | copy-start | bytes 1966084
  15.5 10.2 %collective-permute-start.3 = (f32[6,32,512]{2,1,0:T(8,128)S(1)}, f32[6,32,512]{2,1,0:T(8,128)S(1)}, u32[]{:S(2)}, u32[]{:S(2)}) collective-permute-start(f32[6,32,512]{2,1,0:T(8,128)S(1)} %pad_maximum_fusion.2), channel_id=1, source_target_pairs={{1,2},{2,1},{5,6},{6,5},{9,10},{10,9},{13,14},{14,13},{17,18},{18,... | collective-permute-start | bytes 1179656 | tf_op jit(solution)/shard_map/ppermute | solution.py:388
  16.3 27.8 %copy-start.5 = (f32[1,2,5,32,512]{4,3,2,1,0:T(8,128)S(1)}, f32[1,2,5,32,512]{4,3,2,1,0:T(8,128)}, u32[]{:S(2)}) copy-start(f32[1,2,5,32,512]{4,3,2,1,0:T(8,128)} %get-tuple-element.83) | copy-start | bytes 1966084
  16.4 29.3 %copy-start = (f32[1,16,32,512]{3,2,1,0:T(8,128)S(1)}, f32[1,16,32,512]{3,2,1,0:T(8,128)}, u32[]{:S(2)}) copy-start(f32[1,16,32,512]{3,2,1,0:T(8,128)} %refs_3_.9) | copy-start | bytes 3145732
  16.4 29.3 %copy-start.1 = (f32[5,5]{1,0:T(8,128)S(1)}, f32[5,5]{1,0:T(8,128)}, u32[]{:S(2)}) copy-start(f32[5,5]{1,0:T(8,128)} %refs_0_.9) | copy-start | bytes 304
  16.5 16.6 %collective-permute-start.4 = (f32[1,2,5,32,512]{4,3,2,1,0:T(8,128)S(1)}, f32[1,2,5,32,512]{4,3,2,1,0:T(8,128)S(1)}, u32[]{:S(2)}, u32[]{:S(2)}) collective-permute-start(f32[1,2,5,32,512]{4,3,2,1,0:T(8,128)S(1)} %copy-done.8), channel_id=1, source_target_pairs={{4,0},{8,4},{12,8},{16,12},{20,16},{24,20},{28,24},{0,28},{5,1},{9... | collective-permute-start | bytes 1966088 | tf_op jit(solution)/shard_map/ppermute | solution.py:433
  20.9 12.3 %collective-permute-start.5 = (f32[6,32,512]{2,1,0:T(8,128)S(1)}, f32[6,32,512]{2,1,0:T(8,128)S(1)}, u32[]{:S(2)}, u32[]{:S(2)}) collective-permute-start(f32[6,32,512]{2,1,0:T(8,128)S(1)} %pad_maximum_fusion.3), channel_id=1, source_target_pairs={{0,1},{2,3},{1,0},{3,2},{4,5},{6,7},{5,4},{7,6},{8,9},{10,11},{9,8... | collective-permute-start | bytes 1179656 | tf_op jit(solution)/shard_map/ppermute | solution.py:388
  25.8 17.6 %collective-permute-start.7 = (f32[1,2,5,32,512]{4,3,2,1,0:T(8,128)S(1)}, f32[1,2,5,32,512]{4,3,2,1,0:T(8,128)S(1)}, u32[]{:S(2)}, u32[]{:S(2)}) collective-permute-start(f32[1,2,5,32,512]{4,3,2,1,0:T(8,128)S(1)} %copy-done.7), channel_id=1, source_target_pairs={{4,0},{8,4},{12,8},{16,12},{20,16},{24,20},{28,24},{0,28},{5,1},{9... | collective-permute-start | bytes 1966088 | tf_op jit(solution)/shard_map/ppermute | solution.py:433
  27.5 30.0 %slice-start = ((s8[5242880]{0:T(1024)(128)(4,1)}), s8[4194304]{0:T(1024)(128)(4,1)S(1)}, s32[]{:S(2)}) async-start(s8[5242880]{0:T(1024)(128)(4,1)} %bitcast.22), calls=%async_computation | async-start | bytes 8388608
  27.6 5.6 %collective-permute-start.6 = (f32[6,32,512]{2,1,0:T(8,128)S(1)}, f32[6,32,512]{2,1,0:T(8,128)S(1)}, u32[]{:S(2)}, u32[]{:S(2)}) collective-permute-start(f32[6,32,512]{2,1,0:T(8,128)S(1)} %pad_maximum_fusion.4), channel_id=1, source_target_pairs={{1,2},{2,1},{5,6},{6,5},{9,10},{10,9},{13,14},{14,13},{17,18},{18,... | collective-permute-start | bytes 1179656 | tf_op jit(solution)/shard_map/ppermute | solution.py:388
  33.1 18.6 %copy-start.4 = (f32[1,2,5,32,512]{4,3,2,1,0:T(8,128)S(1)}, f32[1,2,5,32,512]{4,3,2,1,0:T(8,128)}, u32[]{:S(2)}) copy-start(f32[1,2,5,32,512]{4,3,2,1,0:T(8,128)} %get-tuple-element.84) | copy-start | bytes 1966084
  33.2 19.6 %collective-permute-start.8 = (f32[1,2,5,32,512]{4,3,2,1,0:T(8,128)S(1)}, f32[1,2,5,32,512]{4,3,2,1,0:T(8,128)S(1)}, u32[]{:S(2)}, u32[]{:S(2)}) collective-permute-start(f32[1,2,5,32,512]{4,3,2,1,0:T(8,128)S(1)} %copy-done.6), channel_id=1, source_target_pairs={{4,0},{8,4},{12,8},{16,12},{20,16},{24,20},{28,24},{0,28},{5,1},{9... | collective-permute-start | bytes 1966088 | tf_op jit(solution)/shard_map/ppermute | solution.py:433
  34.4 17.3 %collective-permute-start.9 = (f32[5,32,512]{2,1,0:T(8,128)S(1)}, f32[5,32,512]{2,1,0:T(8,128)S(1)}, u32[]{:S(2)}, u32[]{:S(2)}) collective-permute-start(f32[5,32,512]{2,1,0:T(8,128)S(1)} %dynamic-slice_bitcast_fusion.1), channel_id=1, source_target_pairs={{0,1},{2,3},{1,0},{3,2},{4,5},{6,7},{5,4},{7,6},{8,9},{10,11},{9,8... | collective-permute-start | bytes 983048 | tf_op jit(solution)/shard_map/ppermute | solution.py:388
  43.4 8.3 %collective-permute-start.10 = (f32[5,32,512]{2,1,0:T(8,128)S(1)}, f32[5,32,512]{2,1,0:T(8,128)S(1)}, u32[]{:S(2)}, u32[]{:S(2)}) collective-permute-start(f32[5,32,512]{2,1,0:T(8,128)S(1)} %dynamic-slice_bitcast_fusion), channel_id=1, source_target_pairs={{1,2},{2,1},{5,6},{6,5},{9,10},{10,9},{13,14},{14,13},{17,18},{18,... | collective-permute-start | bytes 983048 | tf_op jit(solution)/shard_map/ppermute | solution.py:388
  44.2 13.3 %slice-start.1 = ((s8[5242880]{0:T(1024)(128)(4,1)}), s8[1048576]{0:T(1024)(128)(4,1)S(1)}, s32[]{:S(2)}) async-start(s8[5242880]{0:T(1024)(128)(4,1)} %bitcast.22), calls=%async_computation.1 | async-start | bytes 2097152
  44.2 23.9 %collective-permute-start.12 = (f32[1,2,5,32,512]{4,3,2,1,0:T(8,128)S(1)}, f32[1,2,5,32,512]{4,3,2,1,0:T(8,128)S(1)}, u32[]{:S(2)}, u32[]{:S(2)}) collective-permute-start(f32[1,2,5,32,512]{4,3,2,1,0:T(8,128)S(1)} %copy-done.5), channel_id=1, source_target_pairs={{4,0},{8,4},{12,8},{16,12},{20,16},{24,20},{28,24},{0,28},{5,1},{9... | collective-permute-start | bytes 1966088 | tf_op jit(solution)/shard_map/ppermute | solution.py:433
  51.8 16.3 %collective-permute-start.13 = (f32[1,2,5,32,512]{4,3,2,1,0:T(8,128)S(1)}, f32[1,2,5,32,512]{4,3,2,1,0:T(8,128)S(1)}, u32[]{:S(2)}, u32[]{:S(2)}) collective-permute-start(f32[1,2,5,32,512]{4,3,2,1,0:T(8,128)S(1)} %copy-done.4), channel_id=1, source_target_pairs={{4,0},{8,4},{12,8},{16,12},{20,16},{24,20},{28,24},{0,28},{5,1},{9... | collective-permute-start | bytes 1966088 | tf_op jit(solution)/shard_map/ppermute | solution.py:433
  56.5 20.4 %collective-permute-start.11 = (f32[1,2,5,32,512]{4,3,2,1,0:T(8,128)S(1)}, f32[1,2,5,32,512]{4,3,2,1,0:T(8,128)S(1)}, u32[]{:S(2)}, u32[]{:S(2)}) collective-permute-start(f32[1,2,5,32,512]{4,3,2,1,0:T(8,128)S(1)} %copy-done.3), channel_id=1, source_target_pairs={{4,0},{8,4},{12,8},{16,12},{20,16},{24,20},{28,24},{0,28},{5,1},{9... | collective-permute-start | bytes 1966088 | tf_op jit(solution)/shard_map/ppermute | solution.py:433
  (1 other events, 3.7 us)

commit v7 on v6

--- a/solution.py
+++ b/solution.py
@@ -377,13 +377,11 @@
 
     odd = lax.rem(lax.axis_index("gx"), 2)
 
-    def swapped(edges, after=None):
+    def swapped(edges, parities=(0, 1)):
         result = []
-        for parity in range(2):
+        for parity in parities:
             pairs = [(i, i + 1) for i in range(parity, slabs - 1, 2)]
             side = 1 - odd if parity == 0 else odd
-            if parity and after is not None:
-                chunks[after], *edges = lax.optimization_barrier((chunks[after], *edges))
             mine = jnp.concatenate([lax.dynamic_index_in_dim(part, side, 0, keepdims=False) for part in edges])
             result.append(lax.ppermute(mine, "gx", pairs + [(j, i) for i, j in pairs]))
         return result
@@ -425,6 +423,9 @@
             run(ran)
             key = stages[ran].given[-1]
             ran += 1
+            if k is not None:
+                edge, carried[key] = lax.optimization_barrier((chunks[STEPS - 1][0], carried[key]))
+                ends = swapped([edge], (0,)) + ends
             packed, carried[key], *ends = lax.optimization_barrier((packed, carried[key], *ends))
         elif i > 1:
             packed, weights, chunks[i - 2], *ends = lax.optimization_barrier((packed, weights, chunks[i - 2], *ends))
@@ -433,7 +434,7 @@
         chunks.append(lax.ppermute(packed, "seg", back))
         if 1 <= i <= STEPS:
             edges = [chunks[i - 1][0]] + ([sensor_edges[i - 1][:, None]] if i < STEPS else [])
-            exchanged.append(swapped(edges, i if i == STEPS else None))
+            exchanged.append(swapped(edges, (0, 1) if i < STEPS else (1,)))
     halos = sum(exchanged, [])
     for number in range(ran, len(stages)):
         run(number)

time: 87.9 us -> 95.9 us (1.091)
  waiting for transfers between devices: 12 us -> 18.7 us
  starting transfers between devices: 28.4 us -> 30.5 us
    ppermute x6, waiting for transfers between devices: 7.87 us -> 14.3 us  [swapped(): result.append(lax.ppermute(mine, 'gx', pairs + [(j, i) for i, j in pairs]))]
    ppermute x6, starting transfers between devices: 15.3 us -> 17.9 us  [swapped(): result.append(lax.ppermute(mine, 'gx', pairs + [(j, i) for i, j in pairs]))]
  transfers between devices with their start and end apart: 14 -> 14, of which waited for: 5 -> 6; matrix products, arithmetic and copies ran while one was open for 2% -> 2% of each run, Pallas kernels for 38% -> 34%
where the time goes in v7:
time: 95.9 us; the launch traced here: 95.7 us
  Pallas kernels  44.4 us (46%)
  starting transfers between devices  30.5 us (32%)
  waiting for transfers between devices  18.7 us (19%)
  local copies, waits for them, and re-layouts  1.22 us (1%)
    pallas_call x5, Pallas kernels, run_stage(): pl.pallas_call(functools.partial(stage_kernel, stage, fields, planes, ali...  38.3 us
    ppermute x6, starting transfers between devices, swapped(): result.append(lax.ppermute(mine, 'gx', pairs + [(j, i) for i, j in pairs]))  17.9 us
    ppermute x6, waiting for transfers between devices, swapped(): result.append(lax.ppermute(mine, 'gx', pairs + [(j, i) for i, j in pairs]))  14.3 us
    ppermute x8, starting transfers between devices, shards(): chunks.append(lax.ppermute(packed, 'seg', back))  12.6 us
    ppermute x8, waiting for transfers between devices, shards(): chunks.append(lax.ppermute(packed, 'seg', back))  4.41 us
    pallas_call x1, Pallas kernels, pack_rest(): pl.pallas_call(functools.partial(pack_rest_kernel, planes, groups), out_s...  4.17 us
    pallas_call x1, Pallas kernels, pack_first(): pl.pallas_call(functools.partial(pack_first_kernel, planes), out_shape=ja...  1.92 us
  transfers between devices with their start and end apart: 14, of which 6 were waited for; matrix products, arithmetic and copies ran while one was open for 2% of the time, Pallas kernels for 34%

profile of v7, /device:TPU:0, one launch (start us, length us, event | category | flops | bytes accessed | tf_op | source)
XLA Modules:
  0.0 95.7 jit_solution(4176355351903736659)
XLA Ops:
  0.0 1.9 %pack_first.1.first = f32[1,2,5,32,512]{4,3,2,1,0:T(8,128)} custom-call(f32[1,5,16,32,512]{4,3,2,1,0:T(8,128)} %refs_11_.1), custom_call_target="tpu_custom_call" | custom-call | tf_op jit(solution)/shard_map/pack_first/pallas_call | solution.py:291
  1.9 3.4 %collective-permute-start = (f32[1,2,5,32,512]{4,3,2,1,0:T(8,128)}, f32[1,2,5,32,512]{4,3,2,1,0:T(8,128)S(1)}, u32[]{:S(2)}, u32[]{:S(2)}) collective-permute-start(f32[1,2,5,32,512]{4,3,2,1,0:T(8,128)} %pack_first.1.first), channel_id=1, source_target_pairs={{4,0},{8,4},{12,8},{16,12},{20,16},{24,20},{28,24},{0,28},{5,1},{9... | collective-permute-start | bytes 1966088 | tf_op jit(solution)/shard_map/ppermute | solution.py:434
  5.3 4.2 %pack_rest.1 = (f32[1,2,5,32,512]{4,3,2,1,0:T(8,128)}, f32[1,2,5,32,512]{4,3,2,1,0:T(8,128)}, f32[1,2,5,32,512]{4,3,2,1,0:T(8,128)}, f32[1,2,5,32,512]{4,3,2,1,0...) custom-call(f32[1,5,16,32,512]{4,3,2,1,0:T(8,128)} %refs_11_.1, ...), custom_call_target="tpu_custom_call" | custom-call | bytes 9699328 | tf_op jit(solution)/shard_map/pack_rest/pallas_call | solution.py:308
  10.2 1.0 %fusion.1 = (f32[1,2,32,512]{3,2,1,0:T(8,128)S(1)}, f32[1,2,32,512]{3,2,1,0:T(8,128)S(1)}) fusion(f32[2,2,32,512]{3,2,1,0:T(8,128)} %get-tuple-element.61), kind=kLoop, calls=%fused_computation.19 | loop fusion | bytes 524288 | tf_op jit(solution)/shard_map/slice | solution.py:436
  11.4 2.3 %collective-permute-done.refs_4_ = f32[1,2,5,32,512]{4,3,2,1,0:T(8,128)S(1)} collective-permute-done((f32[1,2,5,32,512]{4,3,2,1,0:T(8,128)}, f32[1,2,5,32,512]{4,3,2,1,0:T(8,128)S(1)}, u32[]{:S(2)}, u32[]{:S(2)}) %collective-permute-start) | collective-permute-done | bytes 655392 | tf_op jit(solution)/shard_map/ppermute | solution.py:434
  13.8 1.6 %collective-permute-start.2 = (f32[6,32,512]{2,1,0:T(8,128)S(1)}, f32[6,32,512]{2,1,0:T(8,128)S(1)}, u32[]{:S(2)}, u32[]{:S(2)}) collective-permute-start(f32[6,32,512]{2,1,0:T(8,128)S(1)} %pad_maximum_fusion.1), channel_id=1, source_target_pairs={{0,1},{2,3},{1,0},{3,2},{4,5},{6,7},{5,4},{7,6},{8,9},{10,11},{9,8... | collective-permute-start | bytes 1179656 | tf_op jit(solution)/shard_map/ppermute | solution.py:386
  15.5 0.8 collective-permute-start.3
  16.5 2.5 %collective-permute-start.4 = (f32[1,2,5,32,512]{4,3,2,1,0:T(8,128)S(1)}, f32[1,2,5,32,512]{4,3,2,1,0:T(8,128)S(1)}, u32[]{:S(2)}, u32[]{:S(2)}) collective-permute-start(f32[1,2,5,32,512]{4,3,2,1,0:T(8,128)S(1)} %copy-done.8), channel_id=1, source_target_pairs={{4,0},{8,4},{12,8},{16,12},{20,16},{24,20},{28,24},{0,28},{5,1},{9... | collective-permute-start | bytes 1966088 | tf_op jit(solution)/shard_map/ppermute | solution.py:434
  19.0 1.8 %collective-permute-done.1.refs_5_ = f32[1,2,5,32,512]{4,3,2,1,0:T(8,128)S(1)} collective-permute-done((f32[1,2,5,32,512]{4,3,2,1,0:T(8,128)}, f32[1,2,5,32,512]{4,3,2,1,0:T(8,128)S(1)}, u32[]{:S(2)}, u32[]{:S(2)}) %collective-permute-start.1) | collective-permute-done | bytes 655392 | tf_op jit(solution)/shard_map/ppermute | solution.py:434
  20.9 2.4 %collective-permute-start.5 = (f32[6,32,512]{2,1,0:T(8,128)S(1)}, f32[6,32,512]{2,1,0:T(8,128)S(1)}, u32[]{:S(2)}, u32[]{:S(2)}) collective-permute-start(f32[6,32,512]{2,1,0:T(8,128)S(1)} %pad_maximum_fusion.3), channel_id=1, source_target_pairs={{0,1},{2,3},{1,0},{3,2},{4,5},{6,7},{5,4},{7,6},{8,9},{10,11},{9,8... | collective-permute-start | bytes 1179656 | tf_op jit(solution)/shard_map/ppermute | solution.py:386
  23.3 2.5 %collective-permute-done.2.refs_4_ = f32[6,32,512]{2,1,0:T(8,128)S(1)} collective-permute-done((f32[6,32,512]{2,1,0:T(8,128)S(1)}, f32[6,32,512]{2,1,0:T(8,128)S(1)}, u32[]{:S(2)}, u32[]{:S(2)}) %collective-permute-start.2) | collective-permute-done | bytes 393248 | tf_op jit(solution)/shard_map/ppermute | solution.py:386
  25.8 1.8 %collective-permute-start.7 = (f32[1,2,5,32,512]{4,3,2,1,0:T(8,128)S(1)}, f32[1,2,5,32,512]{4,3,2,1,0:T(8,128)S(1)}, u32[]{:S(2)}, u32[]{:S(2)}) collective-permute-start(f32[1,2,5,32,512]{4,3,2,1,0:T(8,128)S(1)} %copy-done.7), channel_id=1, source_target_pairs={{4,0},{8,4},{12,8},{16,12},{20,16},{24,20},{28,24},{0,28},{5,1},{9... | collective-permute-start | bytes 1966088 | tf_op jit(solution)/shard_map/ppermute | solution.py:434
  28.3 4.9 %collective-permute-done.5.refs_6_ = f32[6,32,512]{2,1,0:T(8,128)S(1)} collective-permute-done((f32[6,32,512]{2,1,0:T(8,128)S(1)}, f32[6,32,512]{2,1,0:T(8,128)S(1)}, u32[]{:S(2)}, u32[]{:S(2)}) %collective-permute-start.5) | collective-permute-done | bytes 393248 | tf_op jit(solution)/shard_map/ppermute | solution.py:386
  33.1 1.2 %collective-permute-start.8 = (f32[1,2,5,32,512]{4,3,2,1,0:T(8,128)S(1)}, f32[1,2,5,32,512]{4,3,2,1,0:T(8,128)S(1)}, u32[]{:S(2)}, u32[]{:S(2)}) collective-permute-start(f32[1,2,5,32,512]{4,3,2,1,0:T(8,128)S(1)} %copy-done.6), channel_id=1, source_target_pairs={{4,0},{8,4},{12,8},{16,12},{20,16},{24,20},{28,24},{0,28},{5,1},{9... | collective-permute-start | bytes 1966088 | tf_op jit(solution)/shard_map/ppermute | solution.py:434
  35.6 5.4 %stage_0_4.1 = (f32[4,408,128]{2,1,0:T(8,128)S(1)}, f32[4,408,128]{2,1,0:T(8,128)S(1)}, f32[4,408,128]{2,1,0:T(8,128)S(1)}, f32[4,408,128]{2,1,0:T(8,128)S(1)}, ...) custom-call(f32[5,5]{1,0:T(8,128)S(1)} %copy-done.1, s32[2]{0:T(128)S(1)} %pad_add_fusion.refs_1_, ...), custom_call_target="tpu_custom_call" | custom-call | tf_op jit(solution)/shard_map/stage_0_4/pallas_call | solution.py:346
  41.1 11.5 %collective-permute-start.9 = (f32[5,32,512]{2,1,0:T(8,128)S(1)}, f32[5,32,512]{2,1,0:T(8,128)S(1)}, u32[]{:S(2)}, u32[]{:S(2)}) collective-permute-start(f32[5,32,512]{2,1,0:T(8,128)S(1)} %dynamic-slice_bitcast_fusion.1), channel_id=1, source_target_pairs={{0,1},{2,3},{1,0},{3,2},{4,5},{6,7},{5,4},{7,6},{8,9},{10,11},{9,8... | collective-permute-start | bytes 983048 | tf_op jit(solution)/shard_map/ppermute | solution.py:386
  52.7 1.0 %collective-permute-start.12 = (f32[1,2,5,32,512]{4,3,2,1,0:T(8,128)S(1)}, f32[1,2,5,32,512]{4,3,2,1,0:T(8,128)S(1)}, u32[]{:S(2)}, u32[]{:S(2)}) collective-permute-start(f32[1,2,5,32,512]{4,3,2,1,0:T(8,128)S(1)} %copy-done.5), channel_id=1, source_target_pairs={{4,0},{8,4},{12,8},{16,12},{20,16},{24,20},{28,24},{0,28},{5,1},{9... | collective-permute-start | bytes 1966088 | tf_op jit(solution)/shard_map/ppermute | solution.py:434
  53.7 6.9 %collective-permute-done.9.refs_8_ = f32[5,32,512]{2,1,0:T(8,128)S(1)} collective-permute-done((f32[5,32,512]{2,1,0:T(8,128)S(1)}, f32[5,32,512]{2,1,0:T(8,128)S(1)}, u32[]{:S(2)}, u32[]{:S(2)}) %collective-permute-start.9) | collective-permute-done | bytes 327712 | tf_op jit(solution)/shard_map/ppermute | solution.py:386
  60.6 1.0 %collective-permute-start.13 = (f32[1,2,5,32,512]{4,3,2,1,0:T(8,128)S(1)}, f32[1,2,5,32,512]{4,3,2,1,0:T(8,128)S(1)}, u32[]{:S(2)}, u32[]{:S(2)}) collective-permute-start(f32[1,2,5,32,512]{4,3,2,1,0:T(8,128)S(1)} %copy-done.4), channel_id=1, source_target_pairs={{4,0},{8,4},{12,8},{16,12},{20,16},{24,20},{28,24},{0,28},{5,1},{9... | collective-permute-start | bytes 1966088 | tf_op jit(solution)/shard_map/ppermute | solution.py:434
  61.5 3.7 %stage_0_5.1 = (f32[4,408,128]{2,1,0:T(8,128)S(1)}, f32[4,408,128]{2,1,0:T(8,128)S(1)}, f32[4,408,128]{2,1,0:T(8,128)S(1)}) custom-call(f32[5,5]{1,0:T(8,128)S(1)} %copy-done.1, s32[2]{0:T(128)S(1)} %pad_add_fusion.refs_1_, bf16[1536,512]{1,0:T(8,128)(2,1)S(1)} %pad_maximum_fusion.refs_2_, f32[1,16,32,512]{3,2,1,0:T(8,128)S(1)} %copy-done, ...), custom_call_target="tpu_custom_call" | custom-call | tf_op jit(solution)/shard_map/stage_0_5/pallas_call | solution.py:346
  65.3 1.0 %collective-permute-start.11 = (f32[1,2,5,32,512]{4,3,2,1,0:T(8,128)S(1)}, f32[1,2,5,32,512]{4,3,2,1,0:T(8,128)S(1)}, u32[]{:S(2)}, u32[]{:S(2)}) collective-permute-start(f32[1,2,5,32,512]{4,3,2,1,0:T(8,128)S(1)} %copy-done.3), channel_id=1, source_target_pairs={{4,0},{8,4},{12,8},{16,12},{20,16},{24,20},{28,24},{0,28},{5,1},{9... | collective-permute-start | bytes 1966088 | tf_op jit(solution)/shard_map/ppermute | solution.py:434
  66.3 10.5 %stage_m3_5.1 = (f32[1,5,16,32,512]{4,3,2,1,0:T(8,128)}, f32[4,408,128]{2,1,0:T(8,128)S(1)}) custom-call(f32[5,5]{1,0:T(8,128)S(1)} %copy-done.1, s32[2]{0:T(128)S(1)} %pad_add_fusion.refs_1_, bf16[1536,512]{1,0:T(8,128)(2,1)S(1)} %pad_maximum_fusion.refs_2_, f32[1,16,32,512]{3,2,1,0:T(8,128)S(1)} %copy-done, ...), custom_call_target="tpu_custom_call" | custom-call | tf_op jit(solution)/shard_map/stage_m3_5/pallas_call | solution.py:346
  76.9 8.9 %stage_m3_7.1 = (f32[1,5,16,32,512]{4,3,2,1,0:T(8,128)}, f32[4,408,128]{2,1,0:T(8,128)S(1)}, f32[4,408,128]{2,1,0:T(8,128)S(1)}, f32[4,408,128]{2,1,0:T(8,128)S(...) custom-call(f32[5,5]{1,0:T(8,128)S(1)} %copy-done.1, ...), custom_call_target="tpu_custom_call", output_to_operand_aliasing={{0}: (13, {})} | custom-call | tf_op jit(solution)/shard_map/stage_m3_7/pallas_call | solution.py:346
  85.7 9.7 %stage_m3_8.1 = f32[1,5,16,32,512]{4,3,2,1,0:T(8,128)} custom-call(f32[5,5]{1,0:T(8,128)S(1)} %copy-done.1, s32[2]{0:T(128)S(1)} %pad_add_fusion.refs_1_, bf16[1536,512]{1,0:T(8,128)(2,1)S(1)} %pad_maximum_fusion.refs_2_, f32[1,16,32,512]{3,2,1,0:T(8,128)S(1)} %copy-done, ...), custom_call_target="tpu_custom_call", output_to_operand_aliasing={{}: (12, {})} | custom-call | tf_op jit(solution)/shard_map/stage_m3_8/pallas_call | solution.py:346
  (48 shorter events, 3.3 us)
Async XLA Ops:
  1.9 9.3 %copy-start.2 = (f32[512,512]{1,0:T(8,128)S(1)}, f32[512,512]{1,0:T(8,128)}, u32[]{:S(2)}) copy-start(f32[512,512]{1,0:T(8,128)} %param.6) | copy-start | bytes 3145732
  1.9 11.8 %collective-permute-start = (f32[1,2,5,32,512]{4,3,2,1,0:T(8,128)}, f32[1,2,5,32,512]{4,3,2,1,0:T(8,128)S(1)}, u32[]{:S(2)}, u32[]{:S(2)}) collective-permute-start(f32[1,2,5,32,512]{4,3,2,1,0:T(8,128)} %pack_first.1.first), channel_id=1, source_target_pairs={{4,0},{8,4},{12,8},{16,12},{20,16},{24,20},{28,24},{0,28},{5,1},{9... | collective-permute-start | bytes 1966088 | tf_op jit(solution)/shard_map/ppermute | solution.py:434
  9.5 11.3 %collective-permute-start.1 = (f32[1,2,5,32,512]{4,3,2,1,0:T(8,128)}, f32[1,2,5,32,512]{4,3,2,1,0:T(8,128)S(1)}, u32[]{:S(2)}, u32[]{:S(2)}) collective-permute-start(f32[1,2,5,32,512]{4,3,2,1,0:T(8,128)} %get-tuple-element.60), channel_id=1, source_target_pairs={{4,0},{8,4},{12,8},{16,12},{20,16},{24,20},{28,24},{0,28},{5,1},{9... | collective-permute-start | bytes 1966088 | tf_op jit(solution)/shard_map/ppermute | solution.py:434
  11.4 5.1 %copy-start.8 = (f32[1,2,5,32,512]{4,3,2,1,0:T(8,128)S(1)}, f32[1,2,5,32,512]{4,3,2,1,0:T(8,128)}, u32[]{:S(2)}) copy-start(f32[1,2,5,32,512]{4,3,2,1,0:T(8,128)} %get-tuple-element.63) | copy-start | bytes 1966084
  13.8 12.0 %copy-start.7 = (f32[1,2,5,32,512]{4,3,2,1,0:T(8,128)S(1)}, f32[1,2,5,32,512]{4,3,2,1,0:T(8,128)}, u32[]{:S(2)}) copy-start(f32[1,2,5,32,512]{4,3,2,1,0:T(8,128)} %get-tuple-element.65) | copy-start | bytes 1966084
  13.8 11.9 %collective-permute-start.2 = (f32[6,32,512]{2,1,0:T(8,128)S(1)}, f32[6,32,512]{2,1,0:T(8,128)S(1)}, u32[]{:S(2)}, u32[]{:S(2)}) collective-permute-start(f32[6,32,512]{2,1,0:T(8,128)S(1)} %pad_maximum_fusion.1), channel_id=1, source_target_pairs={{0,1},{2,3},{1,0},{3,2},{4,5},{6,7},{5,4},{7,6},{8,9},{10,11},{9,8... | collective-permute-start | bytes 1179656 | tf_op jit(solution)/shard_map/ppermute | solution.py:386
  15.5 17.7 %copy-start.6 = (f32[1,2,5,32,512]{4,3,2,1,0:T(8,128)S(1)}, f32[1,2,5,32,512]{4,3,2,1,0:T(8,128)}, u32[]{:S(2)}) copy-start(f32[1,2,5,32,512]{4,3,2,1,0:T(8,128)} %get-tuple-element.68) | copy-start | bytes 1966084
  15.5 10.2 %collective-permute-start.3 = (f32[6,32,512]{2,1,0:T(8,128)S(1)}, f32[6,32,512]{2,1,0:T(8,128)S(1)}, u32[]{:S(2)}, u32[]{:S(2)}) collective-permute-start(f32[6,32,512]{2,1,0:T(8,128)S(1)} %pad_maximum_fusion.2), channel_id=1, source_target_pairs={{1,2},{2,1},{5,6},{6,5},{9,10},{10,9},{13,14},{14,13},{17,18},{18,... | collective-permute-start | bytes 1179656 | tf_op jit(solution)/shard_map/ppermute | solution.py:386
  16.3 19.3 %copy-start = (f32[1,16,32,512]{3,2,1,0:T(8,128)S(1)}, f32[1,16,32,512]{3,2,1,0:T(8,128)}, u32[]{:S(2)}) copy-start(f32[1,16,32,512]{3,2,1,0:T(8,128)} %refs_3_.9) | copy-start | bytes 3145732
  16.4 19.3 %copy-start.1 = (f32[5,5]{1,0:T(8,128)S(1)}, f32[5,5]{1,0:T(8,128)}, u32[]{:S(2)}) copy-start(f32[5,5]{1,0:T(8,128)} %refs_0_.9) | copy-start | bytes 304
  16.5 16.6 %collective-permute-start.4 = (f32[1,2,5,32,512]{4,3,2,1,0:T(8,128)S(1)}, f32[1,2,5,32,512]{4,3,2,1,0:T(8,128)S(1)}, u32[]{:S(2)}, u32[]{:S(2)}) collective-permute-start(f32[1,2,5,32,512]{4,3,2,1,0:T(8,128)S(1)} %copy-done.8), channel_id=1, source_target_pairs={{4,0},{8,4},{12,8},{16,12},{20,16},{24,20},{28,24},{0,28},{5,1},{9... | collective-permute-start | bytes 1966088 | tf_op jit(solution)/shard_map/ppermute | solution.py:434
  20.8 45.5 %slice-start = ((s8[5242880]{0:T(1024)(128)(4,1)}), s8[4194304]{0:T(1024)(128)(4,1)S(1)}, s32[]{:S(2)}) async-start(s8[5242880]{0:T(1024)(128)(4,1)} %bitcast.22), calls=%async_computation | async-start | bytes 8388608
  20.9 12.3 %collective-permute-start.5 = (f32[6,32,512]{2,1,0:T(8,128)S(1)}, f32[6,32,512]{2,1,0:T(8,128)S(1)}, u32[]{:S(2)}, u32[]{:S(2)}) collective-permute-start(f32[6,32,512]{2,1,0:T(8,128)S(1)} %pad_maximum_fusion.3), channel_id=1, source_target_pairs={{0,1},{2,3},{1,0},{3,2},{4,5},{6,7},{5,4},{7,6},{8,9},{10,11},{9,8... | collective-permute-start | bytes 1179656 | tf_op jit(solution)/shard_map/ppermute | solution.py:386
  25.8 9.9 %collective-permute-start.7 = (f32[1,2,5,32,512]{4,3,2,1,0:T(8,128)S(1)}, f32[1,2,5,32,512]{4,3,2,1,0:T(8,128)S(1)}, u32[]{:S(2)}, u32[]{:S(2)}) collective-permute-start(f32[1,2,5,32,512]{4,3,2,1,0:T(8,128)S(1)} %copy-done.7), channel_id=1, source_target_pairs={{4,0},{8,4},{12,8},{16,12},{20,16},{24,20},{28,24},{0,28},{5,1},{9... | collective-permute-start | bytes 1966088 | tf_op jit(solution)/shard_map/ppermute | solution.py:434
  27.6 5.6 %collective-permute-start.6 = (f32[6,32,512]{2,1,0:T(8,128)S(1)}, f32[6,32,512]{2,1,0:T(8,128)S(1)}, u32[]{:S(2)}, u32[]{:S(2)}) collective-permute-start(f32[6,32,512]{2,1,0:T(8,128)S(1)} %pad_maximum_fusion.4), channel_id=1, source_target_pairs={{1,2},{2,1},{5,6},{6,5},{9,10},{10,9},{13,14},{14,13},{17,18},{18,... | collective-permute-start | bytes 1179656 | tf_op jit(solution)/shard_map/ppermute | solution.py:386
  33.1 28.4 %collective-permute-start.8 = (f32[1,2,5,32,512]{4,3,2,1,0:T(8,128)S(1)}, f32[1,2,5,32,512]{4,3,2,1,0:T(8,128)S(1)}, u32[]{:S(2)}, u32[]{:S(2)}) collective-permute-start(f32[1,2,5,32,512]{4,3,2,1,0:T(8,128)S(1)} %copy-done.6), channel_id=1, source_target_pairs={{4,0},{8,4},{12,8},{16,12},{20,16},{24,20},{28,24},{0,28},{5,1},{9... | collective-permute-start | bytes 1966088 | tf_op jit(solution)/shard_map/ppermute | solution.py:434
  34.5 18.2 %copy-start.5 = (f32[1,2,5,32,512]{4,3,2,1,0:T(8,128)S(1)}, f32[1,2,5,32,512]{4,3,2,1,0:T(8,128)}, u32[]{:S(2)}) copy-start(f32[1,2,5,32,512]{4,3,2,1,0:T(8,128)} %get-tuple-element.83) | copy-start | bytes 1966084
  34.5 26.1 %copy-start.4 = (f32[1,2,5,32,512]{4,3,2,1,0:T(8,128)S(1)}, f32[1,2,5,32,512]{4,3,2,1,0:T(8,128)}, u32[]{:S(2)}) copy-start(f32[1,2,5,32,512]{4,3,2,1,0:T(8,128)} %get-tuple-element.84) | copy-start | bytes 1966084
  34.5 19.2 %collective-permute-start.10 = (f32[5,32,512]{2,1,0:T(8,128)S(1)}, f32[5,32,512]{2,1,0:T(8,128)S(1)}, u32[]{:S(2)}, u32[]{:S(2)}) collective-permute-start(f32[5,32,512]{2,1,0:T(8,128)S(1)} %dynamic-slice_bitcast_fusion), channel_id=1, source_target_pairs={{1,2},{2,1},{5,6},{6,5},{9,10},{10,9},{13,14},{14,13},{17,18},{18,... | collective-permute-start | bytes 983048 | tf_op jit(solution)/shard_map/ppermute | solution.py:386
  35.6 30.7 %slice-start.1 = ((s8[5242880]{0:T(1024)(128)(4,1)}), s8[1048576]{0:T(1024)(128)(4,1)S(1)}, s32[]{:S(2)}) async-start(s8[5242880]{0:T(1024)(128)(4,1)} %bitcast.22), calls=%async_computation.1 | async-start | bytes 2097152
  41.1 19.4 %collective-permute-start.9 = (f32[5,32,512]{2,1,0:T(8,128)S(1)}, f32[5,32,512]{2,1,0:T(8,128)S(1)}, u32[]{:S(2)}, u32[]{:S(2)}) collective-permute-start(f32[5,32,512]{2,1,0:T(8,128)S(1)} %dynamic-slice_bitcast_fusion.1), channel_id=1, source_target_pairs={{0,1},{2,3},{1,0},{3,2},{4,5},{6,7},{5,4},{7,6},{8,9},{10,11},{9,8... | collective-permute-start | bytes 983048 | tf_op jit(solution)/shard_map/ppermute | solution.py:386
  52.7 24.2 %collective-permute-start.12 = (f32[1,2,5,32,512]{4,3,2,1,0:T(8,128)S(1)}, f32[1,2,5,32,512]{4,3,2,1,0:T(8,128)S(1)}, u32[]{:S(2)}, u32[]{:S(2)}) collective-permute-start(f32[1,2,5,32,512]{4,3,2,1,0:T(8,128)S(1)} %copy-done.5), channel_id=1, source_target_pairs={{4,0},{8,4},{12,8},{16,12},{20,16},{24,20},{28,24},{0,28},{5,1},{9... | collective-permute-start | bytes 1966088 | tf_op jit(solution)/shard_map/ppermute | solution.py:434
  60.6 16.3 %collective-permute-start.13 = (f32[1,2,5,32,512]{4,3,2,1,0:T(8,128)S(1)}, f32[1,2,5,32,512]{4,3,2,1,0:T(8,128)S(1)}, u32[]{:S(2)}, u32[]{:S(2)}) collective-permute-start(f32[1,2,5,32,512]{4,3,2,1,0:T(8,128)S(1)} %copy-done.4), channel_id=1, source_target_pairs={{4,0},{8,4},{12,8},{16,12},{20,16},{24,20},{28,24},{0,28},{5,1},{9... | collective-permute-start | bytes 1966088 | tf_op jit(solution)/shard_map/ppermute | solution.py:434
  65.3 20.5 %collective-permute-start.11 = (f32[1,2,5,32,512]{4,3,2,1,0:T(8,128)S(1)}, f32[1,2,5,32,512]{4,3,2,1,0:T(8,128)S(1)}, u32[]{:S(2)}, u32[]{:S(2)}) collective-permute-start(f32[1,2,5,32,512]{4,3,2,1,0:T(8,128)S(1)} %copy-done.3), channel_id=1, source_target_pairs={{4,0},{8,4},{12,8},{16,12},{20,16},{24,20},{28,24},{0,28},{5,1},{9... | collective-permute-start | bytes 1966088 | tf_op jit(solution)/shard_map/ppermute | solution.py:434
  (1 other events, 3.7 us)
